TPU v7x, 256 devices: a whole 4x4x8 slice. The times are simulated.
256 devices in a mesh: req: 32 (over x, z), head: 8 (over y, core).
Axes of the slice: x: 4, y: 4, z: 8, core: 2. Of those that a mesh axis runs over, the one named last changes fastest.
Arguments:
- states: float32 [256, 64, 64, 128], P('req', 'head'), may hold values from -1.75 to 1.75
- ssm_x: bfloat16 [3, 256, 4096], P(None, 'req', 'head'), may hold values from -6 to 6
- gate_z: bfloat16 [3, 256, 4096], P(None, 'req', 'head'), may hold values from -6 to 6
- ssm_b: bfloat16 [3, 256, 1024], P(None, 'req', 'head'), may hold values from -3 to 3
- ssm_c: bfloat16 [3, 256, 1024], P(None, 'req', 'head'), may hold values from -3 to 3
- dt_raw: float32 [3, 256, 64], P(None, 'req', 'head'), may hold values from -6 to 6
- decay_rate: float32 [64], P('head'), may hold values from 0.05 to 2
- skip_gain: float32 [64], P('head'), may hold values from 0.5 to 2
- ssm_gain: float32 [4096], P('head'), may hold values from 0.5 to 1.5
- out_weight: bfloat16 [4096, 4096], P('head'), may hold values from -0.09375 to 0.09375
- residual: bfloat16 [3, 256, 4096], P(None, 'req'), may hold values from -32 to 32
- ffn_gain: float32 [4096], P('head'), may hold values from 0.5 to 1.5
- route_ids: int32 [3, 256, 8], P(None, 'req'), may hold values from 0 to 63, all different within a row; in each aligned block of 8 rows (0 to 7, 8 to 15, ..., all dimensions but the last counted through in order) at most 2 rows name the same one
- route_weights: float32 [3, 256, 8], P(None, 'req'), may hold values from 0.02 to 0.25
- gate_weight: bfloat16 [64, 4096, 1024], P('req', 'head'), may hold values from -0.09375 to 0.09375
- up_weight: bfloat16 [64, 4096, 1024], P('req', 'head'), may hold values from -0.09375 to 0.09375
- down_weight: bfloat16 [64, 1024, 4096], P('req', None, 'head'), may hold values from -0.1875 to 0.1875
- dest: int32 [2, 256], replicated, may hold values from 0 to 255, as said below
Outputs:
- mixed: bfloat16 [3, 256, 4096], P(None, 'req', 'head')
- final_states: float32 [256, 64, 64, 128], P('req', 'head')
Inputs may be any that keep to these rules, and one draw needn't show every extreme that they name: `route_ids`: in each step the 8 slots of one device name each expert at most 2 times, and each slot names 8 different experts. Each row is a permutation of the 256 slots: the request in slot g sits in slot dest[w, g] after wave w + 1. In each wave every device's block of 8 slots sends exactly 7 requests, to 7 different other devices, and takes the 7 arriving requests into the slots it vacated; all other requests stay in their slots.
All inputs are finite; a program needn't handle non-finite values.
Results may differ from a plain program's by a relative error of at most 0.013.
Values may be sent and summed in bfloat16 or wider, within the bound.
No kernel may reach another device: no remote copies, remote signals or barrier semaphores. Data moves between devices by JAX's collectives and lax.ppermute only.
A program may use at most 128 MiB of HBM per device.

v0:
```python
import jax
import jax.numpy as jnp
from jax import lax
from jax.sharding import PartitionSpec as P

H = 64
HSIZE = 64
NSTATE = 128
NGROUPS = 8
EXPERTS = 64
STEPS = 3
CAP = 2


NORM_EPS = 1e-05


def expand_groups(packed_rows):
    grouped = packed_rows.astype(jnp.float32).reshape(packed_rows.shape[0], -1, NSTATE)
    return jnp.repeat(grouped, H // NGROUPS, axis=1)


def advance(prior, inputs_x, raw_dt, decay_rates, b_state):
    step_size = jax.nn.softplus(raw_dt)
    retained = jnp.exp(-decay_rates[None, :] * step_size)
    return (
        retained[:, :, None, None] * prior
        + (step_size[:, :, None] * inputs_x)[:, :, :, None] * b_state[:, :, None, :]
    )


def route_positions(route_rows, slot_depth, offset):
    flat_ids = route_rows.reshape(-1)
    expert_table = (flat_ids[:, None] == lax.iota(jnp.int32, EXPERTS)[None, :]).astype(jnp.int32)
    earlier = jnp.cumsum(expert_table, axis=0) - expert_table
    expert_rank = jnp.sum(earlier * expert_table, axis=1)
    return (flat_ids * slot_depth + offset + expert_rank).reshape(route_rows.shape)


def shards(
    states,
    ssm_x,
    gate_z,
    ssm_b,
    ssm_c,
    dt_raw,
    decay_rate,
    skip_gain,
    ssm_gain,
    out_weight,
    residual,
    ffn_gain,
    route_ids,
    route_weights,
    gate_weight,
    up_weight,
    down_weight,
    dest,
):
    slot_count = states.shape[0]
    heads_here = states.shape[1]
    owners = lax.axis_size("req")
    own_index = lax.axis_index("req")
    first_slot = own_index * slot_count
    width_here = ffn_gain.shape[0]
    first_column = lax.axis_index("head") * width_here
    global_slots = first_slot + lax.iota(jnp.int32, slot_count)
    streams = []
    tokens = []
    ssm_state = states
    for step_index in range(STEPS):
        if step_index > 0:
            plan_row = dest[step_index - 1]
            own_plan = lax.dynamic_slice_in_dim(plan_row, first_slot, slot_count)
            target_owner = own_plan // slot_count
            matched = (target_owner[None, :] == lax.iota(jnp.int32, owners)[:, None]) & (
                target_owner != own_index
            )[None, :]
            outgoing = jnp.take(
                ssm_state,
                jnp.sum(jnp.where(matched, lax.iota(jnp.int32, slot_count)[None, :], 0), axis=1),
                axis=0,
            )
            arrived = lax.all_to_all(outgoing, "req", split_axis=0, concat_axis=0, tiled=True)
            landing = plan_row[None, :] == global_slots[:, None]
            anchor = jnp.sum(
                jnp.where(landing, lax.iota(jnp.int32, plan_row.shape[0])[None, :], 0), axis=1
            )
            anchor_owner = anchor // slot_count
            anchor_owner, incoming = (
                anchor_owner,
                (anchor_owner != own_index)[:, None, None, None],
            )
            ssm_state = jnp.where(incoming, jnp.take(arrived, anchor_owner, axis=0), ssm_state)
        inputs_x = ssm_x[step_index].astype(jnp.float32).reshape(slot_count, heads_here, HSIZE)
        updated = advance(
            ssm_state, inputs_x, dt_raw[step_index], decay_rate, expand_groups(ssm_b[step_index])
        )
        y_out = (
            jnp.einsum(
                "shpn,shn->shp",
                updated,
                expand_groups(ssm_c[step_index]),
                precision=lax.Precision.HIGHEST,
            )
            + skip_gain[None, :, None] * inputs_x
        )
        gate_rows = gate_z[step_index].astype(jnp.float32).reshape(slot_count, heads_here, HSIZE)
        gated_out = y_out * jax.nn.silu(gate_rows)
        grouped = gated_out.reshape(slot_count, -1, H // NGROUPS * HSIZE)
        normed = grouped * lax.rsqrt(jnp.mean(grouped * grouped, axis=-1, keepdims=True) + NORM_EPS)
        mamba_out = (normed.reshape(slot_count, -1) * ssm_gain).astype(jnp.bfloat16)
        partial_value = jnp.dot(mamba_out, out_weight, preferred_element_type=jnp.float32)
        summed = lax.psum(partial_value, "head")
        stream = (residual[step_index].astype(jnp.float32) + summed).astype(jnp.bfloat16)
        stream_wide = stream.astype(jnp.float32)
        inverse = lax.rsqrt(jnp.mean(stream_wide * stream_wide, axis=-1, keepdims=True) + NORM_EPS)
        stream_cols = lax.dynamic_slice_in_dim(stream_wide, first_column, width_here, 1)
        normed_cols = (stream_cols * inverse * ffn_gain).astype(jnp.bfloat16)
        ssm_state, stream_cols, normed_cols = (updated, stream_cols, normed_cols)
        streams.append(stream_cols)
        tokens.append(normed_cols)
    mixed_rows = []
    for step_index in range(STEPS):
        positions = route_positions(route_ids[step_index], CAP, 0)
        buffer_rows = EXPERTS * CAP
        chosen = jnp.any(
            positions[None, :, :] == lax.iota(jnp.int32, buffer_rows)[:, None, None], axis=2
        ).astype(jnp.bfloat16)
        packed = jnp.dot(chosen, tokens[step_index], preferred_element_type=jnp.float32).astype(
            jnp.bfloat16
        )
        packed = packed.reshape(owners, gate_weight.shape[0], CAP, width_here)
        served_block = lax.all_to_all(packed, "req", split_axis=0, concat_axis=0, tiled=True)
        gate_terms = jnp.einsum(
            "pecd,edf->pecf", served_block, gate_weight, preferred_element_type=jnp.float32
        )
        up_terms = jnp.einsum(
            "pecd,edf->pecf", served_block, up_weight, preferred_element_type=jnp.float32
        )
        gate_pre = lax.psum(gate_terms.astype(jnp.bfloat16), "head").astype(jnp.float32)
        up_pre = lax.psum(up_terms.astype(jnp.bfloat16), "head").astype(jnp.float32)
        hidden = (jax.nn.silu(gate_pre) * up_pre).astype(jnp.bfloat16)
        served = jnp.einsum(
            "pecf,efd->pecd", hidden, down_weight, preferred_element_type=jnp.float32
        ).astype(jnp.bfloat16)
        returned = lax.all_to_all(served, "req", split_axis=0, concat_axis=0, tiled=True)
        picked = jnp.take(returned.reshape(buffer_rows, width_here), positions, axis=0)
        expert_mix = jnp.sum(
            route_weights[step_index][:, :, None] * picked.astype(jnp.float32), axis=1
        )
        mixed_rows.append((streams[step_index] + expert_mix).astype(jnp.bfloat16))
    return (jnp.stack(mixed_rows), ssm_state)


def solution(mesh):
    placed = (
        P("req", "head", None, None),
        P(None, "req", "head"),
        P(None, "req", "head"),
        P(None, "req", "head"),
        P(None, "req", "head"),
        P(None, "req", "head"),
        P("head"),
        P("head"),
        P("head"),
        P("head", None),
        P(None, "req", None),
        P("head"),
        P(None, "req", None),
        P(None, "req", None),
        P("req", "head", None),
        P("req", "head", None),
        P("req", None, "head"),
        P(),
    )
    return jax.shard_map(
        shards,
        mesh=mesh,
        in_specs=placed,
        out_specs=(P(None, "req", "head"), P("req", "head", None, None)),
        check_vma=False,
    )
```

profile of v0, /device:TPU:32, one launch (start us, length us, event | category | flops | bytes accessed | tf_op | source)
XLA Modules:
  0.0 716.7 jit_solution(3889141493194727395)
XLA Ops:
  7.2 0.9 bitcast_convert_fusion.1
  8.0 0.7 slice_convert_fusion.1
  8.9 0.7 neg.60
  9.5 0.8 fusion.157
  10.7 0.7 multiply_exponential_fusion
  11.5 3.0 multiply_add_fusion
  14.5 5.9 gather_fusion.1
  20.3 8.7 %broadcast_select_fusion.1 = f32[32,8,64,128]{3,2,1,0:T(8,128)} fusion(f32[32,8,64,128]{3,2,1,0:T(8,128)} %gather_fusion.1, pred[32]{0:T(512)(128)(4,1)S(1)} %get-tuple-element.84), kind=kLoop, calls=%fused_computation.8 | loop fusion | flops 2097152 | bytes 16777248 | tf_op jit(solution)/shard_map/jit(_take)/select_n | solution.py:79
  29.0 11.2 %all-to-all-start.2 = ((f32[32,8,64,128]{3,2,1,0:T(8,128)}), f32[32,8,64,128]{3,2,1,0:T(8,128)}, u32[]{:S(2)}, u32[]{:S(2)}) async-start(f32[32,8,64,128]{3,2,1,0:T(8,128)} %broadcast_select_fusion.1), calls=%async_computation.2 | async-start | bytes 16777216 | tf_op jit(solution)/shard_map/all_to_all | solution.py:84
  40.7 199.0 %all-to-all-done.2 = f32[32,8,64,128]{3,2,1,0:T(8,128)} async-done(((f32[32,8,64,128]{3,2,1,0:T(8,128)}), f32[32,8,64,128]{3,2,1,0:T(8,128)}, u32[]{:S(2)}, u32[]{:S(2)}) %all-to-all-start.2) | async-done | bytes 8388640 | tf_op jit(solution)/shard_map/all_to_all | solution.py:84
  239.6 5.4 gather_fusion.2
  245.0 4.1 fusion.21
  249.1 5.9 gather_fusion.4
  255.0 8.7 %broadcast_select_fusion = f32[32,8,64,128]{3,2,1,0:T(8,128)} fusion(f32[32,8,64,128]{3,2,1,0:T(8,128)} %gather_fusion.4, pred[32]{0:T(512)(128)(4,1)S(1)} %get-tuple-element.83), kind=kLoop, calls=%fused_computation.7 | loop fusion | flops 2097152 | bytes 16777248 | tf_op jit(solution)/shard_map/jit(_take)/select_n | solution.py:79
  263.6 4.9 all-to-all-start.5
  270.9 5.1 fusion.158
  275.9 3.3 fusion.159
  279.3 172.9 %all-to-all-done.5 = f32[32,8,64,128]{3,2,1,0:T(8,128)} async-done(((f32[32,8,64,128]{3,2,1,0:T(8,128)}), f32[32,8,64,128]{3,2,1,0:T(8,128)}, u32[]{:S(2)}, u32[]{:S(2)}) %all-to-all-start.5) | async-done | bytes 8388640 | tf_op jit(solution)/shard_map/all_to_all | solution.py:84
  452.1 5.4 gather_fusion.5
  457.5 2.6 fusion.19
  460.2 1.3 copy-done.6
  461.4 3.3 fusion.160
  465.3 3.7 fusion.119
  469.0 1.3 fusion.117
  470.3 1.3 fusion.115
  471.9 68.4 %all-reduce.5.cloned.1.call-done = (f32[8,4096]{1,0:T(8,128)}, f32[8,4096]{1,0:T(8,128)}, f32[8,4096]{1,0:T(8,128)}) async-done(((f32[8,4096]{1,0:T(8,128)}, f32[8,4096]{1,0:T(8,128)}, f32[8,4096]{1,0:T(8,128)}), (f32[8,4096]{1,0:T(8,128)}, f32[8,4096]{1,0:T(8,128)}, f32[8,4096]{1,0:T(8,128)})) %all-reduce.5.cloned.1.call-update) | async-done | bytes 393232 | tf_op jit(solution)/shard_map/psum | solution.py:114
  540.3 1.2 multiply_reduce_fusion.5
  541.6 0.2 convolution_convert_fusion
  541.8 0.7 reshape.467
  542.5 10.0 %all-to-all-start.6 = ((bf16[32,2,2,512]{3,2,1,0:T(2,128)(2,1)}), bf16[32,2,2,512]{3,2,1,0:T(2,128)(2,1)S(1)}, u32[]{:S(2)}, u32[]{:S(2)}) async-start(bf16[32,2,2,512]{3,2,1,0:T(2,128)(2,1)} %reshape.467), calls=%async_computation.6 | async-start | bytes 262144 | tf_op jit(solution)/shard_map/all_to_all | solution.py:134
  552.6 0.2 convolution_convert_fusion.1
  552.9 0.7 reshape.463
  553.8 0.7 reshape.459
  554.5 7.7 %all-to-all-done.6 = bf16[32,2,2,512]{3,2,1,0:T(2,128)(2,1)S(1)} async-done(((bf16[32,2,2,512]{3,2,1,0:T(2,128)(2,1)}), bf16[32,2,2,512]{3,2,1,0:T(2,128)(2,1)S(1)}, u32[]{:S(2)}, u32[]{:S(2)}) %all-to-all-start.6) | async-done | bytes 131104 | tf_op jit(solution)/shard_map/all_to_all | solution.py:134
  562.2 4.4 all-to-all-start.3
  566.7 1.2 fusion.40
  567.9 0.5 copy-done.3
  568.4 1.2 fusion.49
  569.6 6.9 all-to-all-done.3
  576.5 4.4 all-to-all-start
  580.9 1.2 fusion.43
  582.1 0.5 copy-done.4
  582.6 1.2 fusion.52
  583.8 6.8 all-to-all-done
  590.6 1.2 fusion.46
  591.8 0.5 copy-done.5
  592.3 1.2 fusion.55
  594.1 63.1 %all-reduce.7.cloned.1.call-done = (bf16[32,2,2,1024]{3,0,2,1:T(8,128)(2,1)}, bf16[32,2,2,1024]{3,0,2,1:T(8,128)(2,1)}, bf16[32,2,2,1024]{3,0,2,1:T(8,128)(2,1)}...) async-done(((bf16[32,2,2,1024]{3,0,2,1:T(8,128)(2,1)}, bf16[32,2,2,1024]{3,0,2,1:T(8,128)(2,1)}, ...) | async-done | bytes 1572880 | tf_op jit(solution)/shard_map/psum | solution.py:142
  657.2 2.3 fusion.67
  659.5 0.8 copy.46
  660.3 10.0 %all-to-all-start.7 = ((bf16[32,2,2,512]{3,2,1,0:T(2,128)(2,1)}), bf16[32,2,2,512]{3,2,1,0:T(2,128)(2,1)S(1)}, u32[]{:S(2)}, u32[]{:S(2)}) async-start(bf16[32,2,2,512]{3,2,1,0:T(2,128)(2,1)} %copy.46), calls=%async_computation.7 | async-start | bytes 262144 | tf_op jit(solution)/shard_map/all_to_all | solution.py:147
  670.4 2.2 fusion.70
  672.6 0.8 copy.43
  673.4 0.5 fusion.73
  673.8 0.8 copy.40
  674.6 5.4 all-to-all-done.7
  680.0 4.5 all-to-all-start.4
  684.5 0.7 gather_fusion.6
  685.4 8.9 %all-to-all-done.4 = bf16[32,2,2,512]{3,2,1,0:T(2,128)(2,1)S(1)} async-done(((bf16[32,2,2,512]{3,2,1,0:T(2,128)(2,1)}), bf16[32,2,2,512]{3,2,1,0:T(2,128)(2,1)S(1)}, u32[]{:S(2)}, u32[]{:S(2)}) %all-to-all-start.4) | async-done | bytes 131104 | tf_op jit(solution)/shard_map/all_to_all | solution.py:147
  694.2 4.4 all-to-all-start.1
  698.7 0.7 gather_fusion.3
  699.5 8.8 %all-to-all-done.1 = bf16[32,2,2,512]{3,2,1,0:T(2,128)(2,1)S(1)} async-done(((bf16[32,2,2,512]{3,2,1,0:T(2,128)(2,1)}), bf16[32,2,2,512]{3,2,1,0:T(2,128)(2,1)S(1)}, u32[]{:S(2)}, u32[]{:S(2)}) %all-to-all-start.1) | async-done | bytes 131104 | tf_op jit(solution)/shard_map/all_to_all | solution.py:147
  708.5 0.7 gather_fusion
  709.3 0.6 pad_maximum_fusion
  (123 shorter events, 5.3 us)
Async XLA Ops:
  7.2 559.5 %copy-start = (bf16[2,512,1024]{2,1,0:T(8,128)(2,1)S(1)}, bf16[2,512,1024]{2,1,0:T(8,128)(2,1)}, u32[]{:S(2)}) copy-start(bf16[2,512,1024]{2,1,0:T(8,128)(2,1)} %param.39) | copy-start | bytes 6291460
  29.0 210.6 %all-to-all-start.2 = ((f32[32,8,64,128]{3,2,1,0:T(8,128)}), f32[32,8,64,128]{3,2,1,0:T(8,128)}, u32[]{:S(2)}, u32[]{:S(2)}) async-start(f32[32,8,64,128]{3,2,1,0:T(8,128)} %broadcast_select_fusion.1), calls=%async_computation.2 | async-start | bytes 16777216 | tf_op jit(solution)/shard_map/all_to_all | solution.py:84
  263.6 5.1 copy-start.8
  263.6 6.7 copy-start.9
  263.6 7.1 copy-start.13
  263.6 188.5 %all-to-all-start.5 = ((f32[32,8,64,128]{3,2,1,0:T(8,128)}), f32[32,8,64,128]{3,2,1,0:T(8,128)}, u32[]{:S(2)}, u32[]{:S(2)}) async-start(f32[32,8,64,128]{3,2,1,0:T(8,128)} %broadcast_select_fusion), calls=%async_computation.5 | async-start | bytes 16777216 | tf_op jit(solution)/shard_map/all_to_all | solution.py:84
  268.5 271.8 %all-reduce.5.cloned.1.call-start = ((), (), s32[]{:S(2)}) async-start(), calls=%async_computation.8 | async-start | bytes 786432 | tf_op jit(solution)/shard_map/psum | solution.py:114
  270.7 5.2 copy-start.1
  460.1 1.3 copy-start.6
  460.1 4.7 copy-start.14
  460.1 5.1 copy-start.10
  465.3 3.7 copy-start.2
  470.3 70.0 %copy-start.7 = (bf16[3,8,4096]{2,1,0:T(8,128)(2,1)S(1)}, bf16[3,8,4096]{2,1,0:T(8,128)(2,1)}, u32[]{:S(2)}) copy-start(bf16[3,8,4096]{2,1,0:T(8,128)(2,1)} %param.34) | copy-start | bytes 589828
  470.3 71.2 %copy-start.11 = (f32[512]{0:T(512)S(1)}, f32[512]{0:T(512)}, u32[]{:S(2)}) copy-start(f32[512]{0:T(512)} %param.35) | copy-start | bytes 6148
  542.5 19.7 %all-to-all-start.6 = ((bf16[32,2,2,512]{3,2,1,0:T(2,128)(2,1)}), bf16[32,2,2,512]{3,2,1,0:T(2,128)(2,1)S(1)}, u32[]{:S(2)}, u32[]{:S(2)}) async-start(bf16[32,2,2,512]{3,2,1,0:T(2,128)(2,1)} %reshape.467), calls=%async_computation.6 | async-start | bytes 262144 | tf_op jit(solution)/shard_map/all_to_all | solution.py:134
  562.2 14.2 %all-to-all-start.3 = ((bf16[32,2,2,512]{3,2,1,0:T(2,128)(2,1)}), bf16[32,2,2,512]{3,2,1,0:T(2,128)(2,1)S(1)}, u32[]{:S(2)}, u32[]{:S(2)}) async-start(bf16[32,2,2,512]{3,2,1,0:T(2,128)(2,1)} %reshape.463), calls=%async_computation.3 | async-start | bytes 262144 | tf_op jit(solution)/shard_map/all_to_all | solution.py:134
  566.7 1.7 copy-start.3
  576.5 14.2 %all-to-all-start = ((bf16[32,2,2,512]{3,2,1,0:T(2,128)(2,1)}), bf16[32,2,2,512]{3,2,1,0:T(2,128)(2,1)S(1)}, u32[]{:S(2)}, u32[]{:S(2)}) async-start(bf16[32,2,2,512]{3,2,1,0:T(2,128)(2,1)} %reshape.459), calls=%async_computation | async-start | bytes 262144 | tf_op jit(solution)/shard_map/all_to_all | solution.py:134
  580.9 76.3 %all-reduce.7.cloned.1.call-start = ((), (), s32[]{:S(2)}) async-start(), calls=%async_computation.9 | async-start | bytes 3145728 | tf_op jit(solution)/shard_map/psum | solution.py:142
  580.9 1.7 copy-start.4
  590.6 1.7 copy-start.5
  592.3 1.8 copy-start.12
  657.2 13.1 %copy-start.18 = (bf16[32,2,2,1024]{3,0,2,1:T(8,128)(2,1)S(1)}, bf16[32,2,2,1024]{3,0,2,1:T(8,128)(2,1)}, u32[]{:S(2)}) copy-start(bf16[32,2,2,1024]{3,0,2,1:T(8,128)(2,1)} %get-tuple-element.12) | copy-start | bytes 786436
  657.2 13.2 %copy-start.19 = (bf16[32,2,2,1024]{3,0,2,1:T(8,128)(2,1)S(1)}, bf16[32,2,2,1024]{3,0,2,1:T(8,128)(2,1)}, u32[]{:S(2)}) copy-start(bf16[32,2,2,1024]{3,0,2,1:T(8,128)(2,1)} %get-tuple-element.13) | copy-start | bytes 786436
  660.3 19.7 %all-to-all-start.7 = ((bf16[32,2,2,512]{3,2,1,0:T(2,128)(2,1)}), bf16[32,2,2,512]{3,2,1,0:T(2,128)(2,1)S(1)}, u32[]{:S(2)}, u32[]{:S(2)}) async-start(bf16[32,2,2,512]{3,2,1,0:T(2,128)(2,1)} %copy.46), calls=%async_computation.7 | async-start | bytes 262144 | tf_op jit(solution)/shard_map/all_to_all | solution.py:147
  670.3 3.0 copy-start.15
  670.3 3.0 copy-start.16
  670.4 3.0 copy-start.17
  680.0 14.3 %all-to-all-start.4 = ((bf16[32,2,2,512]{3,2,1,0:T(2,128)(2,1)}), bf16[32,2,2,512]{3,2,1,0:T(2,128)(2,1)S(1)}, u32[]{:S(2)}, u32[]{:S(2)}) async-start(bf16[32,2,2,512]{3,2,1,0:T(2,128)(2,1)} %copy.43), calls=%async_computation.4 | async-start | bytes 262144 | tf_op jit(solution)/shard_map/all_to_all | solution.py:147
  694.2 14.2 %all-to-all-start.1 = ((bf16[32,2,2,512]{3,2,1,0:T(2,128)(2,1)}), bf16[32,2,2,512]{3,2,1,0:T(2,128)(2,1)S(1)}, u32[]{:S(2)}, u32[]{:S(2)}) async-start(bf16[32,2,2,512]{3,2,1,0:T(2,128)(2,1)} %copy.40), calls=%async_computation.1 | async-start | bytes 262144 | tf_op jit(solution)/shard_map/all_to_all | solution.py:147
Sparse Core Ops, SparseCore 0:
  471.8 68.4 all-reduce.4
  593.6 63.4 all-reduce.6
where the time goes:
time: 718 us; the launch traced here: 717 us
  waiting for transfers between devices  548 us (76%)
  starting transfers between devices  54.2 us (8%)
  other arithmetic  34.6 us (5%)
  local copies, waits for them, and re-layouts  34.5 us (5%)
  matrix products  30.9 us (4%)
  between operations  14.6 us (2%)
    all_to_all x2, waiting for transfers between devices, shards(): lax.all_to_all(outgoing, 'req', split_axis=0, concat_axis=0, tiled=True)  372 us
    psum x1, waiting for transfers between devices, shards(): summed = lax.psum(partial_value, 'head')  68.4 us
    psum x1, waiting for transfers between devices, shards(): up_pre = lax.psum(up_terms.astype(jnp.bfloat16), 'head').astype(jnp.float32)  63.1 us
    all_to_all x3, waiting for transfers between devices, shards(): lax.all_to_all(served, 'req', split_axis=0, concat_axis=0, tiled=True)  23.1 us
    all_to_all x3, waiting for transfers between devices, shards(): lax.all_to_all(packed, 'req', split_axis=0, concat_axis=0, tiled=True)  21.4 us
    all_to_all x3, starting transfers between devices, shards(): lax.all_to_all(served, 'req', split_axis=0, concat_axis=0, tiled=True)  18.9 us
    all_to_all x3, starting transfers between devices, shards(): lax.all_to_all(packed, 'req', split_axis=0, concat_axis=0, tiled=True)  18.9 us
    select_n x4, other arithmetic, shards(): jnp.take(ssm_state, jnp.sum(jnp.where(matched, lax.iota(jnp.int32, slot_c...  17.3 us
  transfers between devices with their start and end apart: 10, of which 10 were waited for; matrix products, arithmetic and copies ran while one was open for 3% of the time, Pallas kernels for 0%

commit v1 on v0

v1 whole, which is shorter than its diff:
```python
import jax
import jax.numpy as jnp
from jax import lax
from jax.experimental import pallas as pl
from jax.experimental.pallas import tpu as pltpu
from jax.sharding import PartitionSpec as P

NSTATE = 128
EXPERTS = 64
STEPS = 3
CAP = 2
OWNERS = 32
SLOTS = 8
REQUESTS = OWNERS * SLOTS
HEADS = 8
HSIZE = 64
WIDTH = 512
GROUP_HEADS = 8
NORM_EPS = 1e-05
F32 = jnp.float32
BF16 = jnp.bfloat16
VMEM = pltpu.VMEM
SMEM = pltpu.SMEM


def split_pair(value):
    high = value.astype(BF16)
    low = (value - high.astype(F32)).astype(BF16)
    return high, low


def contract(a, b, dims):
    return lax.dot_general(a, b, (dims, ((), ())), preferred_element_type=F32)


def plan_kernel(dest_ref, table_ref):
    size = (REQUESTS, REQUESTS)
    row_id = lax.broadcasted_iota(jnp.int32, size, 1)
    col_id = lax.broadcasted_iota(jnp.int32, size, 0)
    first_row = jnp.broadcast_to(dest_ref[0:1, :], size)
    second_row = jnp.broadcast_to(dest_ref[1:2, :], size)
    first_col = jnp.transpose(first_row)
    hop = (first_col == row_id).astype(BF16)
    second_col = jnp.transpose(second_row).astype(F32).astype(BF16)
    final_col = contract(hop, second_col, ((1,), (0,))).astype(jnp.int32)
    final_row = jnp.transpose(final_col)
    differs = row_id != col_id
    color_col = jnp.zeros(size, jnp.int32)
    color_row = color_col
    for level in (1, 2, 3):
        alike = (color_col == color_row) & differs
        source = jnp.where(((row_id >> level) == (col_id >> level)) & alike, 1.0, 0.0).astype(BF16)
        target = jnp.where(((final_row >> level) == (final_col >> level)) & alike, 1.0, 0.0).astype(BF16)
        power = contract(source, target, ((1,), (0,))).astype(BF16)
        least = col_id.astype(F32)
        for turn in range(7):
            ahead = contract(power, least.astype(BF16), ((1,), (0,)))
            least = jnp.minimum(least, ahead)
            if turn < 6:
                power = contract(power, power, ((1,), (0,))).astype(BF16)
        other = contract(source, least.astype(BF16), ((1,), (0,)))
        bit = jnp.where(least > other, 1, 0)
        color_col = color_col * 2 + bit
        color_row = jnp.transpose(color_col)

    def lookup(key, value):
        return jnp.sum(jnp.where(key == row_id, value, 0), axis=0, keepdims=True)

    table_ref[...] = jnp.zeros_like(table_ref)
    table_ref[0:1, :] = lookup((col_id & -8) + color_col, col_id & 7)
    table_ref[1:2, :] = lookup(color_col * OWNERS + (final_col >> 3), col_id >> 3)
    table_ref[2:3, :] = lookup(final_col, color_col)


def routing_tables(dest):
    return pl.pallas_call(
        plan_kernel,
        out_shape=jax.ShapeDtypeStruct((8, REQUESTS), jnp.int32),
        in_specs=[pl.BlockSpec(memory_space=VMEM)],
        out_specs=pl.BlockSpec(memory_space=VMEM),
        compiler_params=pltpu.CompilerParams(vmem_limit_bytes=16 * 2**20),
        cost_estimate=pl.CostEstimate(flops=3 * 16 * 2 * 256**3, bytes_accessed=16384, transcendentals=0),
        name="plan_states",
    )(dest)


def mamba_kernel(
    state_ref, x_ref, z_ref, b_ref, c_ref, dt_ref, decay_ref, skip_ref, gain_ref, weight_ref,
    part_ref, outer_ref, keep_ref, read_ref, rows_ref,
):
    head_of = lax.broadcasted_iota(jnp.int32, (HEADS, WIDTH), 1) // HSIZE
    spread = (head_of == lax.broadcasted_iota(jnp.int32, (HEADS, WIDTH), 0)).astype(F32)

    def widen(value):
        return lax.dot_general(
            value, spread, (((1,), (0,)), ((), ())),
            precision=lax.Precision.HIGHEST, preferred_element_type=F32,
        )

    for slot in range(SLOTS):
        high, low = split_pair(state_ref[slot])
        c_rows = c_ref[slot].astype(BF16)
        read_ref[slot] = contract(c_rows, high, ((1,), (1,))) + contract(c_rows, low, ((1,), (1,)))
    skip = widen(jnp.broadcast_to(skip_ref[...], (HEADS, HEADS)))
    inputs, kept, steps_b, steps_c = [], [], [], []
    for step in range(STEPS):
        raw = dt_ref[step]
        step_size = jnp.maximum(raw, 0.0) + jnp.log1p(jnp.exp(-jnp.abs(raw)))
        kept.append(widen(jnp.exp(-decay_ref[...] * step_size)))
        inputs.append(widen(step_size) * x_ref[step].astype(F32))
        steps_b.append(b_ref[:, step, :])
        steps_c.append(c_ref[:, step, :])
    for step in range(STEPS):
        total = read_ref[:, step, :] * kept[0]
        for earlier in range(step + 1):
            if earlier > 0:
                total = total * kept[earlier]
            match = jnp.sum(steps_b[earlier] * steps_c[step], axis=1, keepdims=True)
            total = total + inputs[earlier] * match
        y_out = total + skip * x_ref[step].astype(F32)
        gate = z_ref[step].astype(F32)
        gated = y_out * (gate / (1.0 + jnp.exp(-gate)))
        scale = lax.rsqrt(jnp.mean(gated * gated, axis=1, keepdims=True) + NORM_EPS)
        rows_ref[step * SLOTS : (step + 1) * SLOTS, :] = gated * scale * gain_ref[...]
    rows = rows_ref[...].astype(BF16)
    for block in range(HEADS):
        columns = slice(block * WIDTH, (block + 1) * WIDTH)
        part_ref[block] = contract(rows, weight_ref[:, columns], ((1,), (0,))).astype(BF16)
    late = kept[2]
    factors = [inputs[0] * (kept[1] * late), inputs[1] * late, inputs[2]]
    outer_ref[...] = jnp.zeros_like(outer_ref)
    keep_ref[...] = jnp.zeros_like(keep_ref)
    for step in range(STEPS):
        outer_ref[:, step, :] = factors[step]
    keep_ref[:, 0, :] = kept[0] * (kept[1] * late)


def mamba(state, x, z, b, c, dt, decay, skip, gain, weight):
    vmem = pl.BlockSpec(memory_space=VMEM)
    return pl.pallas_call(
        mamba_kernel,
        out_shape=(
            jax.ShapeDtypeStruct((HEADS, STEPS * SLOTS, WIDTH), BF16),
            jax.ShapeDtypeStruct((SLOTS, 8, WIDTH), F32),
            jax.ShapeDtypeStruct((SLOTS, 8, WIDTH), F32),
        ),
        in_specs=[vmem] * 10,
        out_specs=(vmem, vmem, vmem),
        scratch_shapes=[pltpu.VMEM((SLOTS, 8, WIDTH), F32), pltpu.VMEM((STEPS * SLOTS, WIDTH), F32)],
        compiler_params=pltpu.CompilerParams(vmem_limit_bytes=24 * 2**20),
        cost_estimate=pl.CostEstimate(flops=2 * 24 * 512 * 4096, bytes_accessed=6 * 2**20, transcendentals=0),
        name="mamba_steps",
    )(state, x, z, b, c, dt, decay, skip, gain, weight)


def update_kernel(order_ref, state_ref, outer_ref, keep_ref, b_ref, out_ref):
    ones = jnp.ones((8, NSTATE), BF16)
    b_rows = b_ref[0].astype(BF16)
    outer_high, outer_low = split_pair(outer_ref[0])
    keep_high, keep_low = split_pair(keep_ref[0])
    along = ((0,), (0,))
    keep = contract(keep_high, ones, along) + contract(keep_low, ones, along)
    added = contract(outer_high, b_rows, along) + contract(outer_low, b_rows, along)
    out_ref[0] = (keep * state_ref[0] + added).astype(BF16)


def update_states(order, state, outer, keep, b):
    def picked(step, order_ref):
        return (order_ref[step], 0, 0)

    return pl.pallas_call(
        update_kernel,
        out_shape=jax.ShapeDtypeStruct((SLOTS, HEADS * HSIZE, NSTATE), BF16),
        grid_spec=pltpu.PrefetchScalarGridSpec(
            num_scalar_prefetch=1,
            grid=(SLOTS,),
            in_specs=[
                pl.BlockSpec((1, HEADS * HSIZE, NSTATE), picked),
                pl.BlockSpec((1, 8, WIDTH), picked),
                pl.BlockSpec((1, 8, WIDTH), picked),
                pl.BlockSpec((1, 8, NSTATE), picked),
            ],
            out_specs=pl.BlockSpec((1, HEADS * HSIZE, NSTATE), lambda step, order_ref: (step, 0, 0)),
        ),
        compiler_params=pltpu.CompilerParams(vmem_limit_bytes=16 * 2**20),
        cost_estimate=pl.CostEstimate(flops=2 * 32 * 512 * 1024, bytes_accessed=3 * 2**20, transcendentals=0),
        name="update_states",
    )(order, state, outer, keep, b)


def reorder_kernel(order_ref, in_ref, out_ref, sems):
    copies = [
        pltpu.make_async_copy(in_ref.at[order_ref[block]], out_ref.at[block], sems.at[block])
        for block in range(OWNERS)
    ]
    for copy in copies:
        copy.start()
    for copy in copies:
        copy.wait()


def reorder_states(order, pieces):
    return pl.pallas_call(
        reorder_kernel,
        out_shape=jax.ShapeDtypeStruct(pieces.shape, pieces.dtype),
        in_specs=[pl.BlockSpec(memory_space=SMEM), pl.BlockSpec(memory_space=pl.ANY)],
        out_specs=pl.BlockSpec(memory_space=pl.ANY),
        scratch_shapes=[pltpu.SemaphoreType.DMA((OWNERS,))],
        cost_estimate=pl.CostEstimate(flops=0, bytes_accessed=2 * 2**20, transcendentals=0),
        name="reorder_states",
    )(order, pieces)


def place_kernel(order_ref, in_ref, out_ref):
    out_ref[0] = in_ref[0].astype(F32)


def place_states(order, items):
    return pl.pallas_call(
        place_kernel,
        out_shape=jax.ShapeDtypeStruct(items.shape, F32),
        grid_spec=pltpu.PrefetchScalarGridSpec(
            num_scalar_prefetch=1,
            grid=(SLOTS,),
            in_specs=[pl.BlockSpec((1, HEADS * HSIZE, NSTATE), lambda step, order_ref: (order_ref[step], 0, 0))],
            out_specs=pl.BlockSpec((1, HEADS * HSIZE, NSTATE), lambda step, order_ref: (step, 0, 0)),
        ),
        cost_estimate=pl.CostEstimate(flops=0, bytes_accessed=3 * 2**20, transcendentals=0),
        name="place_states",
    )(order, items)


def expand_kernel(pick_ref, stream_ref, gain_ref, gate_ref, up_ref, out_ref):
    half = pick_ref.shape[0] // 2
    for expert in range(2):
        rows = slice(expert * half, (expert + 1) * half)
        picked = contract(pick_ref[rows, :], stream_ref[...], ((1,), (0,)))
        square = jnp.sum(picked * picked, axis=1, keepdims=True)
        high, low = split_pair(square)
        lane = lax.broadcasted_iota(jnp.int32, (half, 128), 1)
        high_wide = jnp.broadcast_to(high.astype(F32), (half, 128))
        low_wide = jnp.broadcast_to(low.astype(F32), (half, 128))
        pair = jnp.where(lane == 0, high_wide, jnp.where(lane == 1, low_wide, 0.0))
        scaled = (picked * gain_ref[...]).astype(BF16)
        out_ref[rows, 0:1024] = contract(scaled, gate_ref[expert], ((1,), (0,))).astype(BF16)
        out_ref[rows, 1024:2048] = contract(scaled, up_ref[expert], ((1,), (0,))).astype(BF16)
        out_ref[rows, 2048:2176] = pair.astype(BF16)


def expand(pick, stream, gain, gate_weight, up_weight):
    vmem = pl.BlockSpec(memory_space=VMEM)
    return pl.pallas_call(
        expand_kernel,
        out_shape=jax.ShapeDtypeStruct((pick.shape[0], 2176), BF16),
        in_specs=[vmem] * 5,
        out_specs=vmem,
        compiler_params=pltpu.CompilerParams(vmem_limit_bytes=32 * 2**20),
        cost_estimate=pl.CostEstimate(flops=2 * 384 * 512 * (2048 + 768), bytes_accessed=8 * 2**20, transcendentals=0),
        name="expand_experts",
    )(pick, stream, gain, gate_weight, up_weight)


def hidden_kernel(parts_ref, out_ref):
    total = parts_ref[0].astype(F32)
    for block in range(1, HEADS):
        total = total + parts_ref[block].astype(F32)
    square = jnp.sum(total[:, 2048:2176], axis=1, keepdims=True)
    inverse = lax.rsqrt(square * (1.0 / (HEADS * WIDTH)) + NORM_EPS)
    gate = total[:, 0:1024] * inverse
    up = total[:, 1024:2048] * inverse
    out_ref[...] = (gate / (1.0 + jnp.exp(-gate)) * up).astype(BF16)


def hidden_units(parts):
    vmem = pl.BlockSpec(memory_space=VMEM)
    return pl.pallas_call(
        hidden_kernel,
        out_shape=jax.ShapeDtypeStruct((parts.shape[1], 1024), BF16),
        in_specs=[vmem],
        out_specs=vmem,
        compiler_params=pltpu.CompilerParams(vmem_limit_bytes=16 * 2**20),
        cost_estimate=pl.CostEstimate(flops=0, bytes_accessed=2 * 2**20, transcendentals=0),
        name="hidden_units",
    )(parts)


def one_hot(index, size):
    return (index[:, None] == lax.iota(jnp.int32, size)[None, :]).astype(BF16)


def select(index, rows):
    return jnp.dot(one_hot(index, rows.shape[0]), rows, preferred_element_type=F32).astype(BF16)


def lookup(index, values):
    match = index[:, None] == lax.iota(jnp.int32, values.shape[0])[None, :]
    return jnp.sum(jnp.where(match, values[None, :], 0), axis=1)


def find(index, values):
    match = index[:, None] == values[None, :]
    return jnp.sum(jnp.where(match, lax.iota(jnp.int32, values.shape[0])[None, :], 0), axis=1)


def shards(
    states, ssm_x, gate_z, ssm_b, ssm_c, dt_raw, decay_rate, skip_gain, ssm_gain, out_weight,
    residual, ffn_gain, route_ids, route_weights, gate_weight, up_weight, down_weight, dest,
):
    me = lax.axis_index("req")
    column = lax.axis_index("head")
    own = me * SLOTS + lax.iota(jnp.int32, SLOTS)
    first_dest, second_dest = dest[0], dest[1]

    back_one = find(own, first_dest)
    back_two = find(find(own, second_dest), first_dest)
    next_one = lookup(own, first_dest)
    next_two = lookup(next_one, second_dest)

    tables = routing_tables(dest)

    own_residual = lax.dynamic_slice_in_dim(residual, column * WIDTH, WIDTH, 2)
    dt_high = lax.reduce_precision(dt_raw, 8, 7)
    dt_rest = dt_raw - dt_high
    dt_mid = lax.reduce_precision(dt_rest, 8, 7)
    dt_pieces = jnp.concatenate([dt_high, dt_mid, dt_rest - dt_mid], axis=2).astype(BF16)
    ids_wide = jnp.transpose(route_ids, (1, 0, 2)).reshape(SLOTS, STEPS * 8).astype(BF16)

    def pack(step):
        return jnp.concatenate(
            [
                ssm_x[step], gate_z[step], ssm_b[step], ssm_c[step], dt_pieces[step], ids_wide,
                jnp.zeros((SLOTS, 128 - 48), BF16),
            ],
            axis=1,
        )

    width = 2 * WIDTH + 3 * 128
    pack_one = jnp.concatenate([pack(1), own_residual[1], jnp.zeros((SLOTS, 128), BF16)], axis=1)
    to_owner = (lax.iota(jnp.int32, OWNERS)[:, None] == (back_one // SLOTS)[None, :]).astype(BF16)
    row_one = jnp.dot(to_owner, pack_one, preferred_element_type=F32).astype(BF16)
    message = jnp.concatenate(
        [
            row_one.reshape(OWNERS, SLOTS, 256),
            jnp.broadcast_to(pack(2)[None], (OWNERS, SLOTS, width)),
        ],
        axis=2,
    )
    got = lax.all_to_all(message, "req", split_axis=0, concat_axis=0, tiled=True)
    residual_two = lax.all_to_all(
        jnp.broadcast_to(own_residual[2][None], (OWNERS, SLOTS, WIDTH)),
        "req", split_axis=0, concat_axis=0, tiled=True,
    )
    home_one = select(next_one // SLOTS, got[:, :, :256].reshape(OWNERS, 2048))
    all_two = got[:, :, 256:].reshape(REQUESTS, width)
    home_two = select(next_two, all_two)
    home_residual = jnp.stack(
        [own_residual[0], home_one[:, width : width + WIDTH], select(next_two, residual_two.reshape(REQUESTS, WIDTH))]
    )

    def unpack(first, low, high):
        return jnp.stack([first, home_one[:, low:high], home_two[:, low:high]])

    x = unpack(ssm_x[0], 0, WIDTH)
    z = unpack(gate_z[0], WIDTH, 2 * WIDTH)
    b = unpack(ssm_b[0], 2 * WIDTH, 2 * WIDTH + 128)
    c = unpack(ssm_c[0], 2 * WIDTH + 128, 2 * WIDTH + 256)
    dt_parts = unpack(dt_pieces[0], 2 * WIDTH + 256, 2 * WIDTH + 280).astype(F32)
    dt = dt_parts[:, :, 0:8] + dt_parts[:, :, 8:16] + dt_parts[:, :, 16:24]

    def by_slot(value):
        return jnp.pad(jnp.transpose(value, (1, 0, 2)).astype(F32), ((0, 0), (0, 8 - STEPS), (0, 0)))

    b_slots, c_slots = by_slot(b), by_slot(c)
    state_rows = states.reshape(SLOTS, HEADS * HSIZE, NSTATE)
    parts, outer, keep = mamba(
        state_rows, x, z, b_slots, c_slots, dt, decay_rate[None], skip_gain[None], ssm_gain[None], out_weight
    )

    order_one = lax.dynamic_slice(tables, (0, me * SLOTS), (1, SLOTS))[0]
    order_two = lax.dynamic_slice(tables, (1, me // 4 * OWNERS), (1, OWNERS))[0]
    order_three = lax.dynamic_slice(tables, (2, me * SLOTS), (1, SLOTS))[0]
    pieces = update_states(order_one, state_rows, outer, keep, b_slots)
    pieces = lax.all_to_all(
        pieces.reshape(OWNERS, 2 * HSIZE, NSTATE), "req", split_axis=0, concat_axis=0, tiled=True
    )
    pieces = lax.all_to_all(
        reorder_states(order_two, pieces), "req", split_axis=0, concat_axis=0, tiled=True
    )
    final_states = place_states(order_three, pieces.reshape(SLOTS, HEADS * HSIZE, NSTATE)).reshape(states.shape)

    terms = lax.all_to_all(parts, "head", split_axis=0, concat_axis=0, tiled=True)
    projected = jnp.sum(terms.astype(F32), axis=0).reshape(STEPS, SLOTS, WIDTH)
    stream = (home_residual.astype(F32) + projected).astype(BF16).reshape(STEPS * SLOTS, WIDTH)
    streams = lax.all_to_all(
        jnp.broadcast_to(stream[None], (OWNERS, STEPS * SLOTS, WIDTH)),
        "req", split_axis=0, concat_axis=0, tiled=True,
    ).reshape(OWNERS * STEPS * SLOTS, WIDTH)

    ids_all = all_two[:, 2 * WIDTH + 280 : 2 * WIDTH + 304].astype(jnp.int32).reshape(OWNERS, SLOTS, STEPS, 8)
    wanted = me * 2 + lax.iota(jnp.int32, 2)
    named = jnp.any(ids_all[None] == wanted[:, None, None, None, None], axis=4).astype(jnp.int32)
    rank = jnp.cumsum(named, axis=2) - named
    code = jnp.where(named > 0, rank, -1)
    code = jnp.transpose(code, (0, 3, 1, 2)).reshape(2, STEPS, REQUESTS).astype(BF16)
    every_one = first_dest
    every_two = lookup(first_dest, second_dest)
    slot_of = jnp.stack([lax.iota(jnp.int32, REQUESTS), every_one, every_two])
    code_home = jnp.stack(
        [code[:, 0]]
        + [
            jnp.dot(code[:, step], one_hot(slot_of[step], REQUESTS).T, preferred_element_type=F32).astype(BF16)
            for step in (1, 2)
        ],
        axis=1,
    ).astype(jnp.int32)
    target = (slot_of[None] // SLOTS * STEPS + lax.iota(jnp.int32, STEPS)[None, :, None]) * CAP + code_home
    target = jnp.where(code_home >= 0, target, -1)
    target = jnp.transpose(target.reshape(2, STEPS, OWNERS, SLOTS), (0, 2, 1, 3)).reshape(2, OWNERS * STEPS * SLOTS)
    per_expert = OWNERS * STEPS * CAP
    pick = (lax.iota(jnp.int32, per_expert)[None, :, None] == target[:, None, :]).astype(BF16)
    pick = pick.reshape(2 * per_expert, OWNERS * STEPS * SLOTS)

    terms = expand(pick, streams, ffn_gain[None], gate_weight, up_weight)
    terms = lax.all_to_all(
        terms.reshape(HEADS, per_expert * 2 // HEADS, 2176), "head", split_axis=0, concat_axis=0, tiled=True
    )
    hidden = lax.all_gather(hidden_units(terms), "head").reshape(2, per_expert, 1024)
    served = jnp.einsum("erf,efd->erd", hidden, down_weight, preferred_element_type=F32).astype(BF16)
    served = jnp.transpose(served.reshape(2, OWNERS, STEPS * CAP, WIDTH), (1, 0, 2, 3))
    returned = lax.all_to_all(
        served.reshape(OWNERS, 2 * STEPS * CAP, WIDTH), "req", split_axis=0, concat_axis=0, tiled=True
    ).reshape(OWNERS * 2 * STEPS * CAP, WIDTH)

    same = route_ids[:, :, :, None, None] == route_ids[:, None, None, :, :]
    earlier = (lax.iota(jnp.int32, SLOTS)[None, :] < lax.iota(jnp.int32, SLOTS)[:, None])[None, :, None, :, None]
    own_rank = jnp.sum((same & earlier).astype(jnp.int32), axis=(3, 4))
    place = (route_ids * STEPS + lax.iota(jnp.int32, STEPS)[:, None, None]) * CAP + own_rank
    hit = place[:, :, :, None] == lax.iota(jnp.int32, OWNERS * 2 * STEPS * CAP)
    mixing = jnp.sum(jnp.where(hit, route_weights[:, :, :, None], 0.0), axis=2)
    mixing = mixing.reshape(STEPS * SLOTS, OWNERS * 2 * STEPS * CAP)
    sources = jnp.concatenate([own, back_one, back_two])
    steps = jnp.repeat(lax.iota(jnp.int32, STEPS), SLOTS)
    kept_rows = (sources // SLOTS * STEPS + steps) * SLOTS + sources % SLOTS
    stream_own = jnp.dot(one_hot(kept_rows, OWNERS * STEPS * SLOTS), streams, preferred_element_type=F32)
    mixed = stream_own + jnp.dot(
        mixing, returned.astype(F32), precision=lax.Precision.HIGHEST, preferred_element_type=F32
    )
    return mixed.astype(BF16).reshape(STEPS, SLOTS, WIDTH), final_states


def solution(mesh):
    placed = (
        P("req", "head", None, None),
        P(None, "req", "head"),
        P(None, "req", "head"),
        P(None, "req", "head"),
        P(None, "req", "head"),
        P(None, "req", "head"),
        P("head"),
        P("head"),
        P("head"),
        P("head", None),
        P(None, "req", None),
        P("head"),
        P(None, "req", None),
        P(None, "req", None),
        P("req", "head", None),
        P("req", "head", None),
        P("req", None, "head"),
        P(),
    )
    return jax.shard_map(
        shards,
        mesh=mesh,
        in_specs=placed,
        out_specs=(P(None, "req", "head"), P("req", "head", None, None)),
        check_vma=False,
    )
```

time: 718 us -> 258 us (0.36)
  waiting for transfers between devices: 548 us -> 100 us
  Pallas kernels: 0 us -> 54.7 us
  matrix products: 30.9 us -> 3.98 us
  other arithmetic: 34.6 us -> 8.72 us
  between operations: 14.6 us -> 1.19 us
  blocking collectives: 0 us -> 13.4 us
  local copies, waits for them, and re-layouts: 34.5 us -> 22.6 us
    all_to_all x8, waiting for transfers between devices: 416 us -> 100 us  [the longest x1 24.2 us: shards(): lax.all_to_all(reorder_states(order_two, pieces), 'req', split_axis=0, co...]
    psum x2 -> x0, waiting for transfers between devices: 132 us -> none  [the longest x1 68.4 us: shards(): summed = lax.psum(partial_value, 'head')]
    pallas_call x0 -> x7, Pallas kernels: none -> 54.7 us  [the longest x1 34 us: reorder_states(): pl.pallas_call(reorder_kernel, out_shape=jax.ShapeDtypeStruct(pieces.shap...]
    dot_general x18 -> x9, matrix products: 30.9 us -> 3.98 us  [the longest x1 1.26 us: shards(): jnp.dot(mixing, returned.astype(F32), precision=lax.Precision.HIGHEST, pr...]
    gather x7 -> x0, local copies, waits for them, and re-layouts: 24.7 us -> none  [the longest x2 11.8 us: shards(): jnp.take(ssm_state, jnp.sum(jnp.where(matched, lax.iota(jnp.int32, slot_c...]
    select_n x6 -> x1, other arithmetic: 17.3 us -> 0.01 us  [shards(): back_one // SLOTS]
    all_gather x0 -> x1, blocking collectives: none -> 13.4 us  [shards(): lax.all_gather(hidden_units(terms), 'head').reshape(2, per_expert, 1024)]
    add x4 -> x5, other arithmetic: 9.63 us -> 0.96 us  [the longest x1 0.79 us: shards(): (route_ids * STEPS + lax.iota(jnp.int32, STEPS)[:, None, None]) * CAP]
  transfers between devices with their start and end apart: 10 -> 8, of which waited for: 10 -> 7; matrix products, arithmetic and copies ran while one was open for 3% -> 5% of each run, Pallas kernels for 0% -> 18%
where the time goes in v1:
time: 258 us; the launch traced here: 257 us
  waiting for transfers between devices  100 us (39%)
  Pallas kernels  54.7 us (21%)
  starting transfers between devices  51.8 us (20%)
  local copies, waits for them, and re-layouts  22.6 us (9%)
  blocking collectives  13.4 us (5%)
  other arithmetic  8.72 us (3%)
  matrix products  3.98 us (2%)
    pallas_call x1, Pallas kernels, reorder_states(): pl.pallas_call(reorder_kernel, out_shape=jax.ShapeDtypeStruct(pieces.shap...  34 us
    all_to_all x1, waiting for transfers between devices, shards(): lax.all_to_all(reorder_states(order_two, pieces), 'req', split_axis=0, co...  24.2 us
    all_to_all x1, waiting for transfers between devices, shards(): lax.all_to_all(message, 'req', split_axis=0, concat_axis=0, tiled=True)  23.8 us
    all_to_all x1, waiting for transfers between devices, shards(): lax.all_to_all(jnp.broadcast_to(stream[None], (OWNERS, STEPS * SLOTS, WID...  19 us
    all_gather x1, blocking collectives, shards(): lax.all_gather(hidden_units(terms), 'head').reshape(2, per_expert, 1024)  13.4 us
    all_to_all x1, waiting for transfers between devices, shards(): lax.all_to_all(terms.reshape(HEADS, per_expert * 2 // HEADS, 2176), 'head...  11.8 us
    all_to_all x1, starting transfers between devices, shards(): lax.all_to_all(message, 'req', split_axis=0, concat_axis=0, tiled=True)  11.3 us
    all_to_all x1, waiting for transfers between devices, shards(): lax.all_to_all(pieces.reshape(OWNERS, 2 * HSIZE, NSTATE), 'req', split_ax...  11.2 us
  transfers between devices with their start and end apart: 8, of which 7 were waited for; matrix products, arithmetic and copies ran while one was open for 5% of the time, Pallas kernels for 18%

profile of v1, /device:TPU:32, one launch (start us, length us, event | category | flops | bytes accessed | tf_op | source)
XLA Modules:
  0.0 256.6 jit_solution(6082468005638522990)
XLA Ops:
  0.7 0.9 slice_reduce_fusion
  1.5 0.7 reduce-precision_convert_fusion.1
  2.3 4.5 %convert_reduce_fusion = s32[3,8,8]{2,1,0:T(8,128)S(1)} fusion(s32[3,8,8]{2,1,0:T(8,128)} %param.30, pred[8,8]{1,0:T(8,128)(4,1)S(1)} %iota_compare_fusion.14), kind=kLoop, calls=%fused_computation.18 | loop fusion | flops 48960 | bytes 1600 | tf_op jit(solution)/shard_map/reduce_sum | solution.py:436
  6.9 0.8 multiply_add_fusion
  7.7 0.8 fusion.29
  8.5 0.8 fusion.32
  9.3 0.2 select_reduce_fusion.5
  9.5 0.2 select_reduce_fusion.3
  9.7 0.7 constant_dynamic-slice_fusion.1
  10.6 0.2 convolution_convert_fusion
  10.9 1.0 pad_maximum_fusion
  11.9 11.3 %all-to-all-start = ((bf16[32,8,1664]{2,1,0:T(8,128)(2,1)}), bf16[32,8,1664]{2,1,0:T(8,128)(2,1)S(1)}, u32[]{:S(2)}, u32[]{:S(2)}) async-start(bf16[32,8,1664]{2,1,0:T(8,128)(2,1)} %pad_maximum_fusion), calls=%async_computation | async-start | bytes 1703936 | tf_op jit(solution)/shard_map/all_to_all | solution.py:348
  23.2 0.2 select_reduce_fusion.1
  23.7 0.2 select_reduce_fusion.2
  23.9 23.8 %all-to-all-done = bf16[32,8,1664]{2,1,0:T(8,128)(2,1)S(1)} async-done(((bf16[32,8,1664]{2,1,0:T(8,128)(2,1)}), bf16[32,8,1664]{2,1,0:T(8,128)(2,1)S(1)}, u32[]{:S(2)}, u32[]{:S(2)}) %all-to-all-start) | async-done | bytes 852000 | tf_op jit(solution)/shard_map/all_to_all | solution.py:348
  47.7 0.8 broadcast_in_dim.153
  48.5 5.0 %all-to-all-start.1 = ((bf16[32,8,512]{2,1,0:T(8,128)(2,1)}), bf16[32,8,512]{2,1,0:T(8,128)(2,1)S(1)}, u32[]{:S(2)}, u32[]{:S(2)}) async-start(bf16[32,8,512]{2,1,0:T(8,128)(2,1)} %broadcast_in_dim.153), calls=%async_computation.1 | async-start | bytes 524288 | tf_op jit(solution)/shard_map/all_to_all | solution.py:349
  53.5 0.2 convolution_convert_fusion.1
  53.8 0.2 convolution_convert_fusion.2
  54.3 1.6 copy-done.1
  55.9 2.2 copy-done.4
  58.1 2.4 mamba_steps.1
  60.5 0.7 copy-done.8
  61.2 0.7 copy-done.10
  61.8 3.5 %all-to-all-done.1 = bf16[32,8,512]{2,1,0:T(8,128)(2,1)S(1)} async-done(((bf16[32,8,512]{2,1,0:T(8,128)(2,1)}), bf16[32,8,512]{2,1,0:T(8,128)(2,1)S(1)}, u32[]{:S(2)}, u32[]{:S(2)}) %all-to-all-start.1) | async-done | bytes 262176 | tf_op jit(solution)/shard_map/all_to_all | solution.py:349
  65.3 4.5 %all-to-all-start.2 = ((bf16[8,24,512]{2,1,0:T(8,128)(2,1)}), bf16[8,24,512]{2,1,0:T(8,128)(2,1)S(1)}, u32[]{:S(2)}, u32[]{:S(2)}) async-start(bf16[8,24,512]{2,1,0:T(8,128)(2,1)} %get-tuple-element.5), calls=%async_computation.2 | async-start | bytes 393216 | tf_op jit(solution)/shard_map/all_to_all | solution.py:391
  69.8 0.2 fusion.5
  69.9 6.6 %all-to-all-done.2 = bf16[8,24,512]{2,1,0:T(8,128)(2,1)S(1)} async-done(((bf16[8,24,512]{2,1,0:T(8,128)(2,1)}), bf16[8,24,512]{2,1,0:T(8,128)(2,1)S(1)}, u32[]{:S(2)}, u32[]{:S(2)}) %all-to-all-start.2) | async-done | bytes 196640 | tf_op jit(solution)/shard_map/all_to_all | solution.py:391
  76.6 1.0 broadcast_in_dim.157
  77.6 6.3 %all-to-all-start.3 = ((bf16[32,24,512]{2,1,0:T(8,128)(2,1)}), bf16[32,24,512]{2,1,0:T(8,128)(2,1)S(1)}, u32[]{:S(2)}, u32[]{:S(2)}) async-start(bf16[32,24,512]{2,1,0:T(8,128)(2,1)} %broadcast_in_dim.157), calls=%async_computation.3 | async-start | bytes 1572864 | tf_op jit(solution)/shard_map/all_to_all | solution.py:394
  84.1 1.2 slice_bitcast_fusion
  85.4 0.2 reshape.434
  85.6 0.2 copy.85
  86.2 0.2 convolution_convert_fusion.5
  86.7 0.2 convolution_convert_fusion.6
  87.6 0.2 fusion.pick_ref
  87.8 19.0 %all-to-all-done.3 = bf16[32,24,512]{2,1,0:T(8,128)(2,1)S(1)} async-done(((bf16[32,24,512]{2,1,0:T(8,128)(2,1)}), bf16[32,24,512]{2,1,0:T(8,128)(2,1)S(1)}, u32[]{:S(2)}, u32[]{:S(2)}) %all-to-all-start.3) | async-done | bytes 786464 | tf_op jit(solution)/shard_map/all_to_all | solution.py:394
  106.8 1.6 copy-done.6
  108.4 1.6 copy-done.7
  110.0 1.5 expand_experts.1
  111.5 1.2 copy-done.3
  112.7 4.6 %all-to-all-start.4 = ((bf16[8,48,2176]{2,1,0:T(8,128)(2,1)}), bf16[8,48,2176]{2,1,0:T(8,128)(2,1)}, u32[]{:S(2)}, u32[]{:S(2)}) async-start(bf16[8,48,2176]{2,1,0:T(8,128)(2,1)} %bitcast.129), calls=%async_computation.4 | async-start | bytes 3342336 | tf_op jit(solution)/shard_map/all_to_all | solution.py:424
  117.4 5.6 %plan_states.1 = s32[8,256]{1,0:T(8,128)S(1)} custom-call(s32[2,256]{1,0:T(2,128)S(1)} %copy-done.13), custom_call_target="tpu_custom_call" | custom-call | flops 1610612736 | bytes 16384 | tf_op jit(solution)/shard_map/plan_states/pallas_call | solution.py:76
  122.9 0.6 fusion.28
  123.6 3.4 %update_states.1 = bf16[8,512,128]{2,1,0:T(8,128)(2,1)S(1)} custom-call(s32[8]{0:T(128)S(1)} %get-tuple-element.34.order_ref, f32[8,512,128]{2,1,0:T(8,128)S(1)} %bitcast.126, f32[8,8,512]{2,1,0:T(8,128)S(1)} %copy-done.9, f32[8,8,512]{2,1,0:T(8,128)S(1)} %copy-done.11, f32[8,8,128]{2,1,0:T(8,128)S(1)} %pad_convert_fusion.1.b_ref), custom_call_target="tpu_custom_call" | custom-call | flops 33554432 | bytes 3145728 | tf_op jit(solution)/shard_map/update_states/pallas_call | solution.py:171
  127.0 1.0 copy-done.5
  127.9 11.8 %all-to-all-done.4.parts_ref = bf16[8,48,2176]{2,1,0:T(8,128)(2,1)} async-done(((bf16[8,48,2176]{2,1,0:T(8,128)(2,1)}), bf16[8,48,2176]{2,1,0:T(8,128)(2,1)}, u32[]{:S(2)}, u32[]{:S(2)}) %all-to-all-start.4) | async-done | bytes 1671200 | tf_op jit(solution)/shard_map/all_to_all | solution.py:424
  139.8 5.0 %all-to-all-start.6 = ((bf16[32,128,128]{2,1,0:T(8,128)(2,1)}), bf16[32,128,128]{2,1,0:T(8,128)(2,1)}, u32[]{:S(2)}, u32[]{:S(2)}) async-start(bf16[32,128,128]{2,1,0:T(8,128)(2,1)} %bitcast.130), calls=%async_computation.6 | async-start | bytes 2097152 | tf_op jit(solution)/shard_map/all_to_all | solution.py:383
  144.8 1.8 hidden_units.1
  146.6 13.4 %all-gather = bf16[384,1024]{1,0:T(8,128)(2,1)S(1)} all-gather(bf16[48,1024]{1,0:T(8,128)(2,1)S(1)} %hidden_units.1), channel_id=2, replica_groups=mesh['req'=32,'head'=8] {'head'}, dimensions={0}, use_global_device_ids=true | all-gather | bytes 884736 | tf_op jit(solution)/shard_map/all_gather | solution.py:427
  160.0 0.6 convolution_convert_fusion.3
  160.6 0.4 copy.93
  161.1 1.0 copy.95
  162.1 11.2 %all-to-all-done.6.in_ref = bf16[32,128,128]{2,1,0:T(8,128)(2,1)} async-done(((bf16[32,128,128]{2,1,0:T(8,128)(2,1)}), bf16[32,128,128]{2,1,0:T(8,128)(2,1)}, u32[]{:S(2)}, u32[]{:S(2)}) %all-to-all-start.6) | async-done | bytes 1048608 | tf_op jit(solution)/shard_map/all_to_all | solution.py:383
  173.3 5.2 %all-to-all-start.5 = ((bf16[32,12,512]{2,1,0:T(8,128)(2,1)}), bf16[32,12,512]{2,1,0:T(8,128)(2,1)S(1)}, u32[]{:S(2)}, u32[]{:S(2)}) async-start(bf16[32,12,512]{2,1,0:T(8,128)(2,1)} %copy.95), calls=%async_computation.5 | async-start | bytes 1048576 | tf_op jit(solution)/shard_map/all_to_all | solution.py:430
  178.5 0.6 dynamic-slice_bitcast_fusion.2.order_ref
  179.1 34.0 %reorder_states.1 = bf16[32,128,128]{2,1,0:T(8,128)(2,1)} custom-call(s32[32]{0:T(128)} %dynamic-slice_bitcast_fusion.2.order_ref, bf16[32,128,128]{2,1,0:T(8,128)(2,1)} %all-to-all-done.6.in_ref), custom_call_target="tpu_custom_call" | custom-call | bytes 2097152 | tf_op jit(solution)/shard_map/reorder_states/pallas_call | solution.py:203
  213.1 9.9 %all-to-all-start.7 = ((bf16[32,128,128]{2,1,0:T(8,128)(2,1)}), bf16[32,128,128]{2,1,0:T(8,128)(2,1)}, u32[]{:S(2)}, u32[]{:S(2)}) async-start(bf16[32,128,128]{2,1,0:T(8,128)(2,1)} %reorder_states.1), calls=%async_computation.7 | async-start | bytes 2097152 | tf_op jit(solution)/shard_map/all_to_all | solution.py:386
  223.0 0.2 select_reduce_fusion
  223.3 0.8 reshape.428
  224.1 1.3 fusion.12
  225.4 0.9 fusion.3
  226.3 24.2 %all-to-all-done.7 = bf16[32,128,128]{2,1,0:T(8,128)(2,1)} async-done(((bf16[32,128,128]{2,1,0:T(8,128)(2,1)}), bf16[32,128,128]{2,1,0:T(8,128)(2,1)}, u32[]{:S(2)}, u32[]{:S(2)}) %all-to-all-start.7) | async-done | bytes 1048608 | tf_op jit(solution)/shard_map/all_to_all | solution.py:386
  250.5 6.1 %place_states.1 = f32[8,512,128]{2,1,0:T(8,128)} custom-call(s32[8]{0:T(128)} %get-tuple-element.35.order_ref, bf16[8,512,128]{2,1,0:T(8,128)(2,1)} %bitcast.54.in_ref), custom_call_target="tpu_custom_call" | custom-call | bytes 3145728 | tf_op jit(solution)/shard_map/place_states/pallas_call | solution.py:219
  (96 shorter events, 2.9 us)
Async XLA Ops:
  0.6 159.3 %copy-start = (bf16[2,1024,512]{2,1,0:T(8,128)(2,1)S(1)}, bf16[2,1024,512]{2,1,0:T(8,128)(2,1)}, u32[]{:S(2)}) copy-start(bf16[2,1024,512]{2,1,0:T(8,128)(2,1)} %param.34) | copy-start | bytes 6291460
  11.9 42.4 %copy-start.12 = (f32[512]{0:T(512)S(1)}, f32[512]{0:T(512)}, u32[]{:S(2)}) copy-start(f32[512]{0:T(512)} %param.26) | copy-start | bytes 6148
  11.9 42.4 %copy-start.15 = (f32[8]{0:T(128)S(1)}, f32[8]{0:T(128)}, u32[]{:S(2)}) copy-start(f32[8]{0:T(128)} %param.24) | copy-start | bytes 100
  11.9 42.4 %copy-start.16 = (f32[8]{0:T(128)S(1)}, f32[8]{0:T(128)}, u32[]{:S(2)}) copy-start(f32[8]{0:T(128)} %param.25) | copy-start | bytes 100
  11.9 35.8 %all-to-all-start = ((bf16[32,8,1664]{2,1,0:T(8,128)(2,1)}), bf16[32,8,1664]{2,1,0:T(8,128)(2,1)S(1)}, u32[]{:S(2)}, u32[]{:S(2)}) async-start(bf16[32,8,1664]{2,1,0:T(8,128)(2,1)} %pad_maximum_fusion), calls=%async_computation | async-start | bytes 1703936 | tf_op jit(solution)/shard_map/all_to_all | solution.py:348
  47.7 6.4 %copy-start.17 = (bf16[32,8,1664]{2,1,0:T(8,128)(2,1)}, bf16[32,8,1664]{2,1,0:T(8,128)(2,1)S(1)}, u32[]{:S(2)}) copy-start(bf16[32,8,1664]{2,1,0:T(8,128)(2,1)S(1)} %all-to-all-done) | copy-start | bytes 2555908
  48.5 16.8 %all-to-all-start.1 = ((bf16[32,8,512]{2,1,0:T(8,128)(2,1)}), bf16[32,8,512]{2,1,0:T(8,128)(2,1)S(1)}, u32[]{:S(2)}, u32[]{:S(2)}) async-start(bf16[32,8,512]{2,1,0:T(8,128)(2,1)} %broadcast_in_dim.153), calls=%async_computation.1 | async-start | bytes 524288 | tf_op jit(solution)/shard_map/all_to_all | solution.py:349
  54.3 1.6 copy-start.1
  55.9 2.2 copy-start.4
  60.5 0.7 copy-start.8
  61.2 0.7 copy-start.10
  65.3 11.3 %all-to-all-start.2 = ((bf16[8,24,512]{2,1,0:T(8,128)(2,1)}), bf16[8,24,512]{2,1,0:T(8,128)(2,1)S(1)}, u32[]{:S(2)}, u32[]{:S(2)}) async-start(bf16[8,24,512]{2,1,0:T(8,128)(2,1)} %get-tuple-element.5), calls=%async_computation.2 | async-start | bytes 393216 | tf_op jit(solution)/shard_map/all_to_all | solution.py:391
  77.6 29.2 %all-to-all-start.3 = ((bf16[32,24,512]{2,1,0:T(8,128)(2,1)}), bf16[32,24,512]{2,1,0:T(8,128)(2,1)S(1)}, u32[]{:S(2)}, u32[]{:S(2)}) async-start(bf16[32,24,512]{2,1,0:T(8,128)(2,1)} %broadcast_in_dim.157), calls=%async_computation.3 | async-start | bytes 1572864 | tf_op jit(solution)/shard_map/all_to_all | solution.py:394
  83.9 22.9 %copy-start.14 = (f32[512]{0:T(512)S(1)}, f32[512]{0:T(512)}, u32[]{:S(2)}) copy-start(f32[512]{0:T(512)} %param.29) | copy-start | bytes 6148
  106.8 1.6 copy-start.6
  108.4 1.6 copy-start.7
  111.5 1.2 copy-start.3
  112.7 4.6 %copy-start.13 = (s32[2,256]{1,0:T(2,128)S(1)}, s32[2,256]{1,0:T(2,128)}, u32[]{:S(2)}) copy-start(s32[2,256]{1,0:T(2,128)} %dest_ref.1) | copy-start | bytes 6148
  112.7 27.1 %all-to-all-start.4 = ((bf16[8,48,2176]{2,1,0:T(8,128)(2,1)}), bf16[8,48,2176]{2,1,0:T(8,128)(2,1)}, u32[]{:S(2)}, u32[]{:S(2)}) async-start(bf16[8,48,2176]{2,1,0:T(8,128)(2,1)} %bitcast.129), calls=%async_computation.4 | async-start | bytes 3342336 | tf_op jit(solution)/shard_map/all_to_all | solution.py:424
  117.3 6.2 %copy-start.2 = (f32[8,8,64,128]{3,2,1,0:T(8,128)S(1)}, f32[8,8,64,128]{3,2,1,0:T(8,128)}, u32[]{:S(2)}) copy-start(f32[8,8,64,128]{3,2,1,0:T(8,128)} %param.18) | copy-start | bytes 6291460
  117.3 6.2 %copy-start.9 = (f32[8,8,512]{2,1,0:T(8,128)S(1)}, f32[8,8,512]{2,1,0:T(8,128)}, u32[]{:S(2)}) copy-start(f32[8,8,512]{2,1,0:T(8,128)} %copy-done.8) | copy-start | bytes 393220
  117.4 6.2 %copy-start.11 = (f32[8,8,512]{2,1,0:T(8,128)S(1)}, f32[8,8,512]{2,1,0:T(8,128)}, u32[]{:S(2)}) copy-start(f32[8,8,512]{2,1,0:T(8,128)} %copy-done.10) | copy-start | bytes 393220
  127.0 1.0 copy-start.5
  139.8 33.5 %all-to-all-start.6 = ((bf16[32,128,128]{2,1,0:T(8,128)(2,1)}), bf16[32,128,128]{2,1,0:T(8,128)(2,1)}, u32[]{:S(2)}, u32[]{:S(2)}) async-start(bf16[32,128,128]{2,1,0:T(8,128)(2,1)} %bitcast.130), calls=%async_computation.6 | async-start | bytes 2097152 | tf_op jit(solution)/shard_map/all_to_all | solution.py:383
  173.3 39.8 %all-to-all-start.5 = ((bf16[32,12,512]{2,1,0:T(8,128)(2,1)}), bf16[32,12,512]{2,1,0:T(8,128)(2,1)S(1)}, u32[]{:S(2)}, u32[]{:S(2)}) async-start(bf16[32,12,512]{2,1,0:T(8,128)(2,1)} %copy.95), calls=%async_computation.5 | async-start | bytes 1048576 | tf_op jit(solution)/shard_map/all_to_all | solution.py:430
  179.1 43.9 %copy-start.18 = (f32[3,8,8]{2,1,0:T(8,128)S(1)}, f32[3,8,8]{2,1,0:T(8,128)}, u32[]{:S(2)}) copy-start(f32[3,8,8]{2,1,0:T(8,128)} %param.31) | copy-start | bytes 2308
  213.1 37.4 %all-to-all-start.7 = ((bf16[32,128,128]{2,1,0:T(8,128)(2,1)}), bf16[32,128,128]{2,1,0:T(8,128)(2,1)}, u32[]{:S(2)}, u32[]{:S(2)}) async-start(bf16[32,128,128]{2,1,0:T(8,128)(2,1)} %reorder_states.1), calls=%async_computation.7 | async-start | bytes 2097152 | tf_op jit(solution)/shard_map/all_to_all | solution.py:386

commit v2 on v0

v2 whole, which is shorter than its diff:
```python
import functools

import jax
import jax.numpy as jnp
from jax import lax
from jax.experimental import pallas as pl
from jax.experimental.pallas import tpu as pltpu
from jax.sharding import PartitionSpec as P

NSTATE = 128
EXPERTS = 64
STEPS = 3
CAP = 2
OWNERS = 32
SLOTS = 8
REQUESTS = OWNERS * SLOTS
HEADS = 8
HSIZE = 64
WIDTH = 512
FFE = 1024
ROWS = STEPS * SLOTS
TERMS = 2 * FFE + 128
CHUNK = 48
NORM_EPS = 1e-05
F32 = jnp.float32
BF16 = jnp.bfloat16
VMEM_SPEC = pl.BlockSpec(memory_space=pltpu.VMEM)
HBM_SPEC = pl.BlockSpec(memory_space=pltpu.HBM)


def params(mebibytes):
    return pltpu.CompilerParams(vmem_limit_bytes=mebibytes * 2**20)


def cost(flops, moved):
    return pl.CostEstimate(flops=flops, bytes_accessed=moved, transcendentals=0)


def run_kernel(body, args, outs, name, scratch=(), flops=0, moved=2**20, out_specs=None, limit=24):
    count, made = len(args), len(outs)
    modes = [mode for _, mode in args]
    copied = [i for i, mode in enumerate(modes) if mode in "hls"]

    def kernel(*refs):
        ins = list(refs[:count])
        results = refs[count : count + made]
        rest = refs[count + made :]
        copies = {}
        for position, i in enumerate(copied):
            copies[i] = pltpu.make_async_copy(ins[i], rest[position], rest[len(copied)].at[position])
            ins[i] = rest[position]
        for copy in copies.values():
            copy.start()
        for i, copy in copies.items():
            if modes[i] != "l":
                copy.wait()
        own = rest[len(copied) + 1 :] if copied else rest
        body(ins, results, own, lambda i: copies[i].wait())

    spaces = [(pltpu.SMEM if modes[i] == "s" else pltpu.VMEM)(args[i][0].shape, args[i][0].dtype) for i in copied]
    if copied:
        spaces.append(pltpu.SemaphoreType.DMA((len(copied),)))
    return pl.pallas_call(
        kernel,
        out_shape=tuple(outs),
        in_specs=[VMEM_SPEC if mode == "v" else HBM_SPEC for mode in modes],
        out_specs=tuple(out_specs or [VMEM_SPEC] * made),
        scratch_shapes=spaces + list(scratch),
        compiler_params=params(limit),
        cost_estimate=cost(flops, moved),
        name=name,
    )(*[array for array, _ in args])


def shaped(shape, dtype):
    return jax.ShapeDtypeStruct(shape, dtype)


def split_pair(value):
    high = value.astype(BF16)
    low = (value - high.astype(F32)).astype(BF16)
    return high, low


def contract(a, b, dims=((1,), (0,))):
    return lax.dot_general(a, b, (dims, ((), ())), preferred_element_type=F32)


def iota(shape, dim):
    return lax.broadcasted_iota(jnp.int32, shape, dim)


def hot(condition):
    return jnp.where(condition, 1.0, 0.0).astype(BF16)


def silu(value):
    return value / (1.0 + jnp.exp(-value))


def plan_kernel(ins, outs, scratch, wait):
    (dest_ref,), (table_ref,) = ins, outs
    size = (REQUESTS, REQUESTS)
    row_id = iota(size, 1)
    col_id = iota(size, 0)
    first_row = jnp.broadcast_to(dest_ref[0:1, :], size)
    second_row = jnp.broadcast_to(dest_ref[1:2, :], size)
    first_col = jnp.transpose(first_row)
    second_col = jnp.transpose(second_row).astype(F32).astype(BF16)
    final_col = contract(hot(first_col == row_id), second_col).astype(jnp.int32)
    final_row = jnp.transpose(final_col)
    differs = row_id != col_id
    color_col = jnp.zeros(size, jnp.int32)
    color_row = color_col
    for level in (1, 2, 3):
        alike = (color_col == color_row) & differs
        source = hot(((row_id >> level) == (col_id >> level)) & alike)
        target = hot(((final_row >> level) == (final_col >> level)) & alike)
        power = contract(source, target).astype(BF16)
        least = col_id.astype(F32)
        for turn in range(7):
            least = jnp.minimum(least, contract(power, least.astype(BF16)))
            if turn < 6:
                power = contract(power, power).astype(BF16)
        other = contract(source, least.astype(BF16))
        color_col = color_col * 2 + jnp.where(least > other, 1, 0)
        color_row = jnp.transpose(color_col)

    def lookup(key, value):
        return jnp.sum(jnp.where(key == row_id, value, 0), axis=0, keepdims=True)

    table_ref[...] = jnp.zeros_like(table_ref)
    table_ref[0:1, :] = lookup((col_id & -8) + color_col, col_id & 7)
    table_ref[1:2, :] = lookup(color_col * OWNERS + (final_col >> 3), col_id >> 3)
    table_ref[2:3, :] = lookup(final_col, color_col)


def routing_tables(dest):
    outs = [shaped((8, REQUESTS), jnp.int32)]
    return run_kernel(plan_kernel, [(dest, "h")], outs, "plan_states", flops=2 * 10**9)[0]


LAST = 24
PIECES = 15
MESSAGE = LAST + PIECES * SLOTS


def place_pieces(value):
    parts = []
    rest = value
    for _ in range(2):
        high = rest.astype(BF16)
        parts.append(high)
        rest = rest - high.astype(F32)
    parts.append(rest.astype(BF16))
    total = jnp.zeros((SLOTS, 128), F32)
    for piece in range(3):
        spot = hot(iota((8, 128), 1) == iota((8, 128), 0) + 8 * piece)
        total = total + contract(parts[piece], spot)
    return total


def join_pieces(block):
    spot = hot((iota((128, 8), 0) % 8 == iota((128, 8), 1)) & (iota((128, 8), 0) < 24))
    return contract(block.astype(BF16), spot)


def read_rows(pack_ref, first):
    return jnp.concatenate([pack_ref[:, first + piece, :] for piece in range(4)], axis=1)


def sender_match(dest_row, me):
    slot = iota((SLOTS, REQUESTS), 0) + me * SLOTS
    owner = hot((iota((REQUESTS, OWNERS), 0) >> 3) == iota((REQUESTS, OWNERS), 1))
    return contract(hot(jnp.broadcast_to(dest_row, slot.shape) == slot), owner).astype(BF16)


def pack_kernel(ins, outs, scratch, wait):
    dest_ref, x_ref, z_ref, residual_ref, b_ref, c_ref, dt_ref, ids_ref = ins
    (message_ref,), (wide_ref, last_ref) = outs, scratch
    me = lax.axis_index("req")
    columns = pl.ds(pl.multiple_of(lax.axis_index("head") * WIDTH, WIDTH), WIDTH)
    back = sender_match(dest_ref[0:1, :], me)

    def pieces(step):
        wide = [x_ref[step], z_ref[step], residual_ref[step, :, columns]]
        cut = [value[:, 128 * i : 128 * (i + 1)] for value in wide for i in range(4)]
        return cut + [b_ref[step], c_ref[step], place_pieces(dt_ref[step]).astype(BF16)]

    one = pieces(1)
    two = pieces(2)
    wide_ref[:, PIECES:LAST, :] = jnp.zeros((OWNERS, LAST - PIECES, 128), F32)
    for row in range(PIECES):
        wide_ref[:, row, :] = contract(back, one[row], ((0,), (0,)))
    ids = jnp.zeros((SLOTS, 128), F32)
    for step in range(STEPS):
        spot = hot(iota((8, 128), 1) == iota((8, 128), 0) + 8 * (step + 3))
        ids = ids + contract(ids_ref[step].astype(F32).astype(BF16), spot)
    wide_ref[:, LAST:32, :] = jnp.broadcast_to(two[0].astype(F32)[None], (OWNERS, SLOTS, 128))
    for row in range(1, PIECES):
        value = two[row].astype(F32)
        if row == PIECES - 1:
            value = value + ids
        last_ref[(row - 1) * SLOTS : row * SLOTS, :] = value
    message_ref[:, 0:32, :] = wide_ref[...].astype(BF16)
    last = last_ref[...].astype(BF16)
    message_ref[:, 32:MESSAGE, :] = jnp.broadcast_to(last[None], (OWNERS,) + last.shape)


def pack_inputs(*arrays):
    outs = [shaped((OWNERS, MESSAGE, 128), BF16)]
    scratch = [pltpu.VMEM((OWNERS, 32, 128), F32), pltpu.VMEM((MESSAGE - 32, 128), F32)]
    return run_kernel(pack_kernel, [(array, "h") for array in arrays], outs, "pack_inputs", scratch, limit=58)[0]


def head_spread():
    return hot(iota((HEADS, WIDTH), 1) // HSIZE == iota((HEADS, WIDTH), 0))


def widen(value, spread):
    parts = []
    rest = value
    for _ in range(3):
        high = rest.astype(BF16)
        parts.append(high)
        rest = rest - high.astype(F32)
    return contract(parts[0], spread) + contract(parts[1], spread) + contract(parts[2], spread)


def softplus(value):
    return jnp.maximum(value, 0.0) + jnp.log1p(jnp.exp(-jnp.abs(value)))


def mamba_kernel(ins, outs, scratch, wait):
    dest_ref, got_ref, state_ref, x_ref, z_ref, residual_ref, b_ref, c_ref, dt_ref = ins[:9]
    decay_ref, skip_ref, gain_ref, weight_ref = ins[9:]
    keep_ref, send_ref, residual_out_ref, outer_ref, kept_ref, b_rows_ref = outs
    wide_ref, rows_in_ref, c_rows_ref, read_ref, rows_ref = scratch
    me = lax.axis_index("req")
    column = lax.axis_index("head")
    for slot in range(SLOTS):
        middle = dest_ref[0, me * SLOTS + slot]
        final = dest_ref[1, middle]
        rows_in_ref[slot, 0:16, :] = got_ref[middle // SLOTS, 0:16, :].astype(F32)
        wide_ref[slot] = got_ref[final // SLOTS].astype(F32)
        rows_in_ref[slot, 16 : 16 + PIECES, :] = wide_ref[
            slot, pl.ds(LAST + final % SLOTS, PIECES, stride=SLOTS), :
        ]
    xs = [x_ref[0].astype(F32), read_rows(rows_in_ref, 0), read_rows(rows_in_ref, 16)]
    zs = [z_ref[0].astype(F32), read_rows(rows_in_ref, 4), read_rows(rows_in_ref, 20)]
    steps_b = [b_ref[0].astype(F32), rows_in_ref[:, 12, :], rows_in_ref[:, 28, :]]
    steps_c = [c_ref[0].astype(F32), rows_in_ref[:, 13, :], rows_in_ref[:, 29, :]]
    raws = [dt_ref[0], join_pieces(rows_in_ref[:, 14, :]), join_pieces(rows_in_ref[:, 30, :])]
    own_columns = pl.ds(pl.multiple_of(column * WIDTH, WIDTH), WIDTH)
    residual_out_ref[0:8, :] = residual_ref[0, :, own_columns].astype(F32)
    residual_out_ref[8:16, :] = read_rows(rows_in_ref, 8)
    residual_out_ref[16:24, :] = read_rows(rows_in_ref, 24)

    c_rows_ref[...] = jnp.zeros_like(c_rows_ref)
    for step in range(STEPS):
        c_rows_ref[:, step, :] = steps_c[step]
    across = ((1,), (1,))
    wait(2)
    for slot in range(SLOTS):
        high, low = split_pair(state_ref[slot])
        c_rows = c_rows_ref[slot].astype(BF16)
        read_ref[slot] = contract(c_rows, high, across) + contract(c_rows, low, across)
    spread = head_spread()
    skip = widen(jnp.broadcast_to(skip_ref[...], (SLOTS, HEADS)), spread)
    inputs, kept = [], []
    for step in range(STEPS):
        step_size = softplus(raws[step])
        kept.append(widen(jnp.exp(-decay_ref[...] * step_size), spread))
        inputs.append(widen(step_size, spread) * xs[step])
    for step in range(STEPS):
        total = read_ref[:, step, :] * kept[0]
        for earlier in range(step + 1):
            if earlier > 0:
                total = total * kept[earlier]
            match = jnp.sum(steps_b[earlier] * steps_c[step], axis=1, keepdims=True)
            total = total + inputs[earlier] * match
        gated = (total + skip * xs[step]) * silu(zs[step])
        scale = lax.rsqrt(jnp.mean(gated * gated, axis=1, keepdims=True) + NORM_EPS)
        rows_ref[step * SLOTS : (step + 1) * SLOTS, :] = gated * scale * gain_ref[...]
    rows = rows_ref[...].astype(BF16)
    wait(12)
    for turn in range(HEADS):
        block = 2 * ((column // 2 + turn) % 4) + (column + turn // 4) % 2
        columns = pl.ds(pl.multiple_of(block * WIDTH, WIDTH), WIDTH)
        terms = contract(rows, weight_ref[:, columns]).astype(BF16)
        if turn < 4:
            keep_ref[turn] = terms
        else:
            send_ref[turn - 4] = terms
    late = kept[2]
    factors = [inputs[0] * (kept[1] * late), inputs[1] * late, inputs[2]]
    outer_ref[...] = jnp.zeros_like(outer_ref)
    kept_ref[...] = jnp.zeros_like(kept_ref)
    b_rows_ref[...] = jnp.zeros_like(b_rows_ref)
    for step in range(STEPS):
        outer_ref[:, step, :] = factors[step]
        b_rows_ref[:, step, :] = steps_b[step]
    kept_ref[:, 0, :] = kept[0] * (kept[1] * late)


def mamba(dest, got, state, *arrays):
    part = shaped((4, ROWS, WIDTH), BF16)
    factor = shaped((SLOTS, 8, WIDTH), F32)
    outs = [part, part, shaped((ROWS, WIDTH), F32), factor, factor, shaped((SLOTS, 8, NSTATE), F32)]
    scratch = [
        pltpu.VMEM((SLOTS, MESSAGE, 128), F32),
        pltpu.VMEM((SLOTS, 32, 128), F32),
        pltpu.VMEM((SLOTS, 8, NSTATE), F32),
        pltpu.VMEM((SLOTS, 8, WIDTH), F32),
        pltpu.VMEM((ROWS, WIDTH), F32),
    ]
    args = [(dest, "s"), (got, "v"), (state, "l")] + [(array, "h") for array in arrays[:-1]] + [(arrays[-1], "l")]
    return run_kernel(mamba_kernel, args, outs, "mamba_steps", scratch, 2 * 24 * 512 * 4096, 8 * 2**20, limit=54)


def update_kernel(ins, outs, scratch, wait):
    table_ref, state_any, outer_ref, keep_ref, b_ref = ins
    (out_any,), (state_ref, made_ref, in_sems, out_sems) = outs, scratch
    first = lax.axis_index("req") * SLOTS
    sources = [table_ref[0, first + block] for block in range(SLOTS)]
    loads = [
        pltpu.make_async_copy(state_any.at[sources[block]], state_ref.at[block], in_sems.at[block])
        for block in range(SLOTS)
    ]
    for load in loads:
        load.start()
    stores = []
    ones = jnp.ones((8, NSTATE), BF16)
    along = ((0,), (0,))
    for block in range(SLOTS):
        b_rows = b_ref[sources[block]].astype(BF16)
        outer_high, outer_low = split_pair(outer_ref[sources[block]])
        keep_high, keep_low = split_pair(keep_ref[sources[block]])
        keep = contract(keep_high, ones, along) + contract(keep_low, ones, along)
        added = contract(outer_high, b_rows, along) + contract(outer_low, b_rows, along)
        loads[block].wait()
        made_ref[block] = (keep * state_ref[block] + added).astype(BF16)
        store = pltpu.make_async_copy(made_ref.at[block], out_any.at[block], out_sems.at[block])
        store.start()
        stores.append(store)
    for store in stores:
        store.wait()


def update_states(table, state, factors):
    scratch = [
        pltpu.VMEM(state.shape, F32),
        pltpu.VMEM(state.shape, BF16),
        pltpu.SemaphoreType.DMA((SLOTS,)),
        pltpu.SemaphoreType.DMA((SLOTS,)),
    ]
    args = [(table, "s"), (state, "m")] + [(factor, "h") for factor in factors]
    return run_kernel(
        update_kernel, args, [shaped(state.shape, BF16)], "update_states", scratch,
        2 * 32 * 512 * 1024, 3 * 2**20, [HBM_SPEC],
    )[0]


CORES = [(i, i ^ 1) for i in range(HEADS)]


def along_y(value, distance):
    moves = [(i, ((i // 2 + distance) % 4) * 2 + i % 2) for i in range(HEADS)]
    return lax.ppermute(value, "head", moves)


def add_kernel(tail, ins, outs, scratch, wait):
    keep_ref, got_ref = ins
    first_ref, *rest_refs = outs
    for turn in range(4):
        total = keep_ref[turn].astype(F32) + got_ref[turn].astype(F32)
        if turn == 0:
            first_ref[...] = total
            continue
        out_ref = rest_refs[turn - 1]
        if tail:
            out_ref[:, : 2 * FFE] = total[:, : 2 * FFE].astype(BF16)
            out_ref[:, 2 * FFE :] = pair_lanes(jnp.sum(total[:, 2 * FFE :], axis=1, keepdims=True))
        else:
            out_ref[...] = total.astype(BF16)


def pair_lanes(value):
    high, low = split_pair(value)
    shape = (value.shape[0], 128)
    lane = iota(shape, 1)
    high_wide = jnp.broadcast_to(high.astype(F32), shape)
    low_wide = jnp.broadcast_to(low.astype(F32), shape)
    return jnp.where(lane == 0, high_wide, jnp.where(lane == 1, low_wide, 0.0)).astype(BF16)


def add_cores(keep, got, tail):
    shape = keep.shape[1:]
    outs = [shaped(shape, F32)] + [shaped(shape, BF16)] * 3
    return run_kernel(
        functools.partial(add_kernel, tail), [(keep, "v"), (got, "v")], outs, "add_cores", moved=4 * keep.size
    )


def scatter_sum(keep, send, tail, beside=None):
    got = lax.ppermute(send, "head", CORES)
    first, *rest = add_cores(keep, got, tail)
    if beside is not None:
        first, beside, *rest = lax.optimization_barrier((first, beside, *rest))
        beside = exchange(beside)
    far = along_y(rest[1], 2)
    near = along_y(rest[0], 1)
    other = along_y(rest[2], 3)
    return (first, near, far, other), beside


def stream_kernel(ins, outs, scratch, wait):
    first_ref, a_ref, b_ref, c_ref, residual_ref = ins
    (out_ref,) = outs
    total = first_ref[...] + a_ref[...].astype(F32) + b_ref[...].astype(F32) + c_ref[...].astype(F32)
    stream = (residual_ref[...] + total).astype(BF16)
    out_ref[...] = jnp.broadcast_to(stream[None], out_ref.shape)


def stream_copies(parts, residual):
    args = [(part, "v") for part in parts] + [(residual, "v")]
    return run_kernel(stream_kernel, args, [shaped((OWNERS, ROWS, WIDTH), BF16)], "stream_copies")[0]


def routes_kernel(ins, outs, scratch, wait):
    dest_ref, got_ref, ids_ref, weights_ref = ins
    pick_ref, kept_ref, high_ref, low_ref = outs
    me = lax.axis_index("req")
    column = lax.axis_index("head")
    total_rows = OWNERS * ROWS
    square = (REQUESTS, REQUESTS)
    row_id = iota(square, 1)
    col_id = iota(square, 0)
    first = dest_ref[0:1, :]
    second = jnp.broadcast_to(dest_ref[1:2, :], (8, REQUESTS)).astype(F32).astype(BF16)
    hop_one = hot(jnp.broadcast_to(first, square) == col_id)
    both = contract(second, hop_one)[0:1, :].astype(jnp.int32)
    hops = [hot(row_id == col_id), hop_one, hot(jnp.broadcast_to(both, square) == col_id)]
    slots = [iota((1, REQUESTS), 1), first, both]
    spread = []
    for step in range(STEPS):
        shape = (REQUESTS, total_rows)
        g = iota(shape, 0)
        spread.append(hot(iota(shape, 1) == (g >> 3) * ROWS + step * SLOTS + (g & 7)))
    at_row = jnp.zeros((8, total_rows), F32)
    for step in range(STEPS):
        wide = jnp.broadcast_to(slots[step], (8, REQUESTS)).astype(F32).astype(BF16)
        at_row = at_row + contract(wide, spread[step])
    ids = got_ref[:, MESSAGE - 16 :, :].astype(F32)[:, SLOTS:, :].reshape(REQUESTS, 128)
    step_of = hot((iota((128, 128), 0) >> 3) == iota((128, 128), 1) + 3)
    earlier = hot(((row_id >> 3) == (col_id >> 3)) & (row_id < col_id))
    slot = iota((REQUESTS, 128), 0)
    lane = iota((REQUESTS, 128), 1)
    owner = slot >> 3
    part = owner >> 2
    turn = (((part & 1) + column) & 1) * 4 + (((part >> 1) - (column >> 1)) & 3)
    base = turn * (CHUNK // 2) + (owner & 3) * (STEPS * CAP) + lane * CAP
    for expert in range(2):
        match = (ids == (me * 2 + expert).astype(F32)) & (lane >= 24) & (lane < 48)
        named = contract(hot(match), step_of)
        rank = contract(earlier, named.astype(BF16))
        target = jnp.where(named > 0.5, base.astype(F32) + rank + 1.0, 0.0).astype(BF16)
        row = jnp.zeros((8, total_rows), F32)
        for step in range(STEPS):
            select = hot(iota((8, 128), 1) == step)
            by_slot = contract(select, target, ((1,), (1,)))
            by_home = contract(by_slot.astype(BF16), hops[step])
            row = row + contract(by_home.astype(BF16), spread[step])
        half = OWNERS * STEPS * CAP
        want = iota((half, total_rows), 0).astype(F32) + 1.0
        pick_ref[expert * half : (expert + 1) * half, :] = hot(jnp.broadcast_to(row[0:1, :], (half, total_rows)) == want)
    shape = (ROWS, total_rows)
    mine = (me * SLOTS + iota(shape, 0) % SLOTS).astype(F32)
    step_match = (iota(shape, 1) % ROWS) // SLOTS == iota(shape, 0) // SLOTS
    kept_ref[...] = hot((jnp.broadcast_to(at_row[0:1, :], shape) == mine) & step_match)
    expert_lane = iota((ROWS, 128), 1)
    chosen = jnp.zeros((ROWS, 128), F32)
    weight = jnp.zeros((ROWS, 128), F32)
    for choice in range(8):
        hit = expert_lane == ids_ref[:, choice : choice + 1]
        chosen = chosen + jnp.where(hit, 1.0, 0.0)
        weight = weight + jnp.where(hit, weights_ref[:, choice : choice + 1], 0.0)
    small = (ROWS, ROWS)
    before = hot((iota(small, 0) // SLOTS == iota(small, 1) // SLOTS) & (iota(small, 1) < iota(small, 0)))
    rank = contract(before, chosen.astype(BF16))
    span = OWNERS * CHUNK
    place = iota((128, span), 1) % CHUNK % 12
    expert_of = 2 * (iota((128, span), 1) // CHUNK) + place // 6
    to_place = hot(iota((128, span), 0) == expert_of)
    spot = iota((ROWS, span), 1) % CHUNK
    fits = (contract(rank.astype(BF16), to_place) == (spot % 2).astype(F32)) & (
        (spot % 6) // 2 == iota((ROWS, span), 0) // SLOTS
    )
    for value, out_ref in zip(split_pair(weight), (high_ref, low_ref)):
        value = jnp.where(fits, contract(value, to_place), 0.0)
        for piece in range(4):
            out_ref[piece] = jnp.where(spot // 12 == piece, value, 0.0).astype(BF16)


def routes(dest, got, ids, weights):
    total_rows = OWNERS * ROWS
    mixing = shaped((4, ROWS, OWNERS * CHUNK), BF16)
    outs = [
        shaped((2 * OWNERS * STEPS * CAP, total_rows), BF16),
        shaped((ROWS, total_rows), BF16),
        mixing,
        mixing,
    ]
    args = [(dest, "h"), (got, "v"), (ids, "h"), (weights, "h")]
    return run_kernel(routes_kernel, args, outs, "routes", flops=10**9)


def expand_kernel(ins, outs, scratch, wait):
    pick_ref, stream_ref, gain_ref, gate_ref, up_ref = ins
    keep_ref, send_ref = outs
    half = pick_ref.shape[0] // 2
    some = CHUNK // 2
    for expert in range(2):
        picked = contract(pick_ref[expert * half : (expert + 1) * half, :], stream_ref[...])
        tail = pair_lanes(jnp.sum(picked * picked, axis=1, keepdims=True))
        scaled = (picked * gain_ref[...]).astype(BF16)
        if expert == 0:
            wait(3)
            wait(4)
        values = [
            contract(scaled, gate_ref[expert]).astype(BF16),
            contract(scaled, up_ref[expert]).astype(BF16),
            tail,
        ]
        rows = slice(expert * some, (expert + 1) * some)
        for turn in range(HEADS):
            out_ref = keep_ref if turn < 4 else send_ref
            source = slice(turn * some, (turn + 1) * some)
            for value, start in zip(values, (0, FFE, 2 * FFE)):
                out_ref[turn % 4, rows, start : start + value.shape[1]] = value[source, :]


def expand(pick, stream, gain, gate_weight, up_weight):
    part = shaped((4, CHUNK, TERMS), BF16)
    args = [(pick, "h"), (stream, "v"), (gain, "h"), (gate_weight, "l"), (up_weight, "l")]
    return run_kernel(
        expand_kernel, args, [part, part], "expand_experts", flops=2 * 384 * 512 * (2048 + 768), moved=8 * 2**20
    )


def hidden_kernel(ins, outs, scratch, wait):
    first_ref, a_ref, b_ref, c_ref = ins
    (out_ref,) = outs
    total = first_ref[...] + a_ref[...].astype(F32) + b_ref[...].astype(F32) + c_ref[...].astype(F32)
    square = jnp.sum(total[:, 2 * FFE :], axis=1, keepdims=True)
    inverse = lax.rsqrt(square * (1.0 / (HEADS * WIDTH)) + NORM_EPS)
    out_ref[...] = (silu(total[:, :FFE] * inverse) * (total[:, FFE : 2 * FFE] * inverse)).astype(BF16)


def hidden_units(parts):
    args = [(part, "v") for part in parts]
    return run_kernel(hidden_kernel, args, [shaped((CHUNK, FFE), BF16)], "hidden_units")[0]


def shrink_kernel(ins, outs, scratch, wait):
    table_ref, pieces_ref, weight_ref, *hidden_refs = ins
    (out_ref,), (sems,) = outs, scratch
    first = lax.axis_index("req") // 4 * OWNERS
    column = lax.axis_index("head")
    moves = [
        pltpu.make_async_copy(
            pieces_ref.at[table_ref[1, first + block]],
            out_ref.at[block, pl.ds(CHUNK, 2 * HSIZE), :],
            sems.at[block],
        )
        for block in range(OWNERS)
    ]
    for move in moves:
        move.start()
    hidden = jnp.concatenate([ref[...] for ref in hidden_refs], axis=0)
    wait(2)
    served = [contract(hidden, weight_ref[expert]) for expert in range(2)]
    shape = (4 * 16, CHUNK)
    row, source = iota(shape, 0), iota(shape, 1)
    inside = row % 16
    spot = hot((inside < 12) & (source == (inside // 6) * (CHUNK // 2) + (row // 16) * 6 + inside % 6))
    half = iota((CHUNK, WIDTH), 0) < CHUNK // 2
    for turn in range(HEADS):
        rows = slice(turn * CHUNK, (turn + 1) * CHUNK)
        chunk = jnp.where(half, served[0][rows], served[1][rows]).astype(BF16)
        owner = (2 * ((column // 2 - turn + 8) % 4) + (column + turn // 4) % 2) * 4
        block = contract(spot, chunk)
        for piece in range(4):
            wide = block[piece * 16 : piece * 16 + 12, :]
            cut = [wide[:, 128 * i : 128 * (i + 1)] for i in range(4)]
            out_ref[owner + piece, 0:CHUNK, :] = jnp.concatenate(cut, axis=0).astype(BF16)
    for move in moves:
        move.wait()


def shrink(table, pieces, hidden, weight):
    args = [(table, "s"), (pieces, "m"), (weight, "l")] + [(block, "v") for block in hidden]
    outs = [shaped((OWNERS, CHUNK + 2 * HSIZE, 128), BF16)]
    return run_kernel(
        shrink_kernel, args, outs, "shrink_experts", [pltpu.SemaphoreType.DMA((OWNERS,))],
        2 * 2 * 384 * 1024 * 512, 4 * 2**20,
    )[0]


def finish_kernel(ins, outs, scratch, wait):
    table_ref, back_ref, high_ref, low_ref, kept_ref, stream_ref = ins
    mixed_ref, states_any = outs
    made_ref, sems = scratch
    first = lax.axis_index("req") * SLOTS
    stores = []
    for slot in range(SLOTS):
        color = table_ref[2, first + slot]
        for piece in range(4):
            rows = slice(piece * 2 * HSIZE, (piece + 1) * 2 * HSIZE)
            made_ref[slot, rows, :] = back_ref[color * 4 + piece, CHUNK:, :].astype(F32)
        store = pltpu.make_async_copy(made_ref.at[slot], states_any.at[slot], sems.at[slot])
        store.start()
        stores.append(store)
    served = back_ref[:, 0:CHUNK, :].reshape(OWNERS * CHUNK, 128)
    for ref in (2, 3, 4, 5):
        wait(ref)
    stream = contract(kept_ref[...], stream_ref[...])
    for piece in range(4):
        columns = slice(piece * 128, (piece + 1) * 128)
        mixed = contract(high_ref[piece], served) + contract(low_ref[piece], served)
        mixed_ref[:, columns] = (stream[:, columns] + mixed).astype(BF16)
    for store in stores:
        store.wait()


def finish(table, back, high, low, kept, streams):
    args = [(table, "s"), (back, "v"), (high, "l"), (low, "l"), (kept, "l"), (streams, "l")]
    outs = [shaped((ROWS, WIDTH), BF16), shaped((SLOTS, HEADS * HSIZE, NSTATE), F32)]
    scratch = [pltpu.VMEM((SLOTS, HEADS * HSIZE, NSTATE), F32), pltpu.SemaphoreType.DMA((SLOTS,))]
    return run_kernel(
        finish_kernel, args, outs, "finish", scratch, 10**8, 4 * 2**20, [VMEM_SPEC, HBM_SPEC]
    )


def exchange(value):
    return lax.all_to_all(value, "req", split_axis=0, concat_axis=0, tiled=True)


def shards(
    states, ssm_x, gate_z, ssm_b, ssm_c, dt_raw, decay_rate, skip_gain, ssm_gain, out_weight,
    residual, ffn_gain, route_ids, route_weights, gate_weight, up_weight, down_weight, dest,
):
    fence = lax.optimization_barrier
    state_rows = states.reshape(SLOTS, HEADS * HSIZE, NSTATE)
    own = (ssm_x, gate_z, residual, ssm_b, ssm_c, dt_raw)

    message = pack_inputs(dest, *own, route_ids)
    message, later_dest = fence((message, dest))
    got = exchange(message)
    table = routing_tables(later_dest)
    got, table = fence((got, table))

    keep_part, send_part, home_residual, *factors = mamba(
        dest, got, state_rows, *own, decay_rate[None], skip_gain[None], ssm_gain[None], out_weight
    )
    parts, _ = scatter_sum(keep_part, send_part, False)
    copies, got, factors = fence((stream_copies(parts, home_residual), got, factors))
    streams = exchange(copies).reshape(OWNERS * ROWS, WIDTH)
    routed = routes(dest, got, route_ids.reshape(ROWS, 8), route_weights.reshape(ROWS, 8))
    pieces = update_states(table, state_rows, factors)
    streams, pieces, (pick, kept, high, low) = fence((streams, pieces, routed))

    keep_part, send_part = expand(pick, streams, ffn_gain[None], gate_weight, up_weight)
    parts, pieces = scatter_sum(keep_part, send_part, True, pieces.reshape(OWNERS, 2 * HSIZE, NSTATE))
    hidden = hidden_units(parts)
    far = along_y(hidden, 2)
    near = along_y(hidden, 1)
    other = along_y(hidden, 3)
    blocks = [hidden, near, far, other]
    blocks = blocks + [lax.ppermute(block, "head", CORES) for block in blocks]
    back = exchange(shrink(table, pieces, blocks, down_weight))
    mixed, final_states = finish(table, back, high, low, kept, streams)
    return mixed.reshape(STEPS, SLOTS, WIDTH), final_states.reshape(states.shape)


def solution(mesh):
    placed = (
        P("req", "head", None, None),
        P(None, "req", "head"),
        P(None, "req", "head"),
        P(None, "req", "head"),
        P(None, "req", "head"),
        P(None, "req", "head"),
        P("head"),
        P("head"),
        P("head"),
        P("head", None),
        P(None, "req", None),
        P("head"),
        P(None, "req", None),
        P(None, "req", None),
        P("req", "head", None),
        P("req", "head", None),
        P("req", None, "head"),
        P(),
    )
    return jax.shard_map(
        shards,
        mesh=mesh,
        in_specs=placed,
        out_specs=(P(None, "req", "head"), P("req", "head", None, None)),
        check_vma=False,
    )
```

time: 718 us -> 187 us (0.26)
  waiting for transfers between devices: 548 us -> 65.8 us
  blocking collectives: 0 us -> 43.7 us
  other arithmetic: 34.6 us -> 0 us
  matrix products: 30.9 us -> 0 us
  Pallas kernels: 0 us -> 30.5 us
  local copies, waits for them, and re-layouts: 34.5 us -> 9.85 us
  starting transfers between devices: 54.2 us -> 35.4 us
  between operations: 14.6 us -> 1.12 us
    all_to_all x8 -> x3, waiting for transfers between devices: 416 us -> 42.6 us  [exchange(): return lax.all_to_all(value, 'req', split_axis=0, concat_axis=0, tiled=True)]
    psum x2 -> x0, waiting for transfers between devices: 132 us -> none  [the longest x1 68.4 us: shards(): summed = lax.psum(partial_value, 'head')]
    all_to_all x0 -> x1, blocking collectives: none -> 43.7 us  [exchange(): return lax.all_to_all(value, 'req', split_axis=0, concat_axis=0, tiled=True)]
    all_to_all x8 -> x3, starting transfers between devices: 53.9 us -> 21.5 us  [exchange(): return lax.all_to_all(value, 'req', split_axis=0, concat_axis=0, tiled=True)]
    dot_general x18 -> x0, matrix products: 30.9 us -> none  [the longest x3 11.7 us: shards(): jnp.einsum('shpn,shn->shp', updated, expand_groups(ssm_c[step_index]), pr...]
    pallas_call x0 -> x12, Pallas kernels: none -> 30.5 us  [run_kernel(): pl.pallas_call(kernel, out_shape=tuple(outs), in_specs=[VMEM_SPEC if mode...]
    gather x7 -> x0, local copies, waits for them, and re-layouts: 24.7 us -> none  [the longest x2 11.8 us: shards(): jnp.take(ssm_state, jnp.sum(jnp.where(matched, lax.iota(jnp.int32, slot_c...]
    ppermute x0 -> x15, waiting for transfers between devices: none -> 23.2 us  [the longest x9 18.1 us: along_y(): return lax.ppermute(value, 'head', moves)]
  transfers between devices with their start and end apart: 10 -> 18, of which waited for: 10 -> 15; matrix products, arithmetic and copies ran while one was open for 3% -> 0% of each run, Pallas kernels for 0% -> 7%
where the time goes in v2:
time: 187 us; the launch traced here: 186 us
  waiting for transfers between devices  65.8 us (35%)
  blocking collectives  43.7 us (23%)
  starting transfers between devices  35.4 us (19%)
  Pallas kernels  30.5 us (16%)
  local copies, waits for them, and re-layouts  9.85 us (5%)
    all_to_all x1, blocking collectives, exchange(): return lax.all_to_all(value, 'req', split_axis=0, concat_axis=0, tiled=True)  43.7 us
    all_to_all x3, waiting for transfers between devices, exchange(): return lax.all_to_all(value, 'req', split_axis=0, concat_axis=0, tiled=True)  42.6 us
    pallas_call x12, Pallas kernels, run_kernel(): pl.pallas_call(kernel, out_shape=tuple(outs), in_specs=[VMEM_SPEC if mode...  30.5 us
    all_to_all x3, starting transfers between devices, exchange(): return lax.all_to_all(value, 'req', split_axis=0, concat_axis=0, tiled=True)  21.5 us
    ppermute x9, waiting for transfers between devices, along_y(): return lax.ppermute(value, 'head', moves)  18.1 us
    ppermute x9, starting transfers between devices, along_y(): return lax.ppermute(value, 'head', moves)  13.8 us
    unnamed x42, local copies, waits for them, and re-layouts  9.85 us
    ppermute x2, waiting for transfers between devices, scatter_sum(): got = lax.ppermute(send, 'head', CORES)  3.84 us
  transfers between devices with their start and end apart: 18, of which 15 were waited for; matrix products, arithmetic and copies ran while one was open for 0% of the time, Pallas kernels for 7%

profile of v2, /device:TPU:32, one launch (start us, length us, event | category | flops | bytes accessed | tf_op | source)
XLA Modules:
  0.0 186.4 jit_solution(7112912426620323940)
XLA Ops:
  0.6 0.0 copy-start.17
  0.6 2.6 %pack_inputs.1 = bf16[32,144,128]{2,1,0:T(8,128)(2,1)} custom-call(s32[2,256]{1,0:T(2,128)} %refs_0_.6, bf16[3,8,512]{2,1,0:T(8,128)(2,1)} %refs_3_.4, bf16[3,8,512]{2,1,0:T(8,128)(2,1)} %refs_4_.4, bf16[3,8,4096]{2,1,0:T(8,128)(2,1)} %refs_5_.3, bf16[3,8,128]{2,1,0:T(8,128)(2,1)} %refs_6_.3, bf16[3,8,128]{2,1,0:T(8,128)(2,1)} %refs_7_.3, ...), custom_call_target="tpu_custom_call" | custom-call | bytes 1048576 | tf_op jit(solution)/shard_map/pack_inputs/pallas_call | solution.py:63
  3.3 11.2 %all-to-all-start = ((bf16[32,144,128]{2,1,0:T(8,128)(2,1)}), bf16[32,144,128]{2,1,0:T(8,128)(2,1)S(1)}, u32[]{:S(2)}, u32[]{:S(2)}) async-start(bf16[32,144,128]{2,1,0:T(8,128)(2,1)} %pack_inputs.1), calls=%async_computation | async-start | bytes 2359296 | tf_op jit(solution)/shard_map/all_to_all | solution.py:646
  14.5 5.6 %plan_states.1.refs_0_ = s32[8,256]{1,0:T(8,128)S(1)} custom-call(s32[2,256]{1,0:T(2,128)S(1)} %copy-done.17), custom_call_target="tpu_custom_call" | custom-call | flops 2000000000 | bytes 1048576 | tf_op jit(solution)/shard_map/plan_states/pallas_call | solution.py:63
  20.1 25.6 %all-to-all-done.refs_1_ = bf16[32,144,128]{2,1,0:T(8,128)(2,1)S(1)} async-done(((bf16[32,144,128]{2,1,0:T(8,128)(2,1)}), bf16[32,144,128]{2,1,0:T(8,128)(2,1)S(1)}, u32[]{:S(2)}, u32[]{:S(2)}) %all-to-all-start) | async-done | bytes 1179680 | tf_op jit(solution)/shard_map/all_to_all | solution.py:646
  45.7 1.0 copy-done.1
  46.7 5.9 %mamba_steps.1 = (bf16[4,24,512]{2,1,0:T(8,128)(2,1)}, bf16[4,24,512]{2,1,0:T(8,128)(2,1)}, f32[24,512]{1,0:T(8,128)}, f32[8,8,512]{2,1,0:T(8,128)}, f32[8,8,512]{2,1,0:T(8,128)}, /*index=5*/f32[8,8,128]{2,1,0:T(8,128)}) custom-call(s32[2,256]{1,0:T(2,128)} %refs_0_.6, bf16[32,144,128]{2,1,0:T(8,128)(2,1)} %copy-done.1, f32[8,512,128]{2,1,0:T(8,128)} %bitcast.11, ...), custom_call_target="tpu_custom_call" | custom-call | flops 100663296 | bytes 8388608 | tf_op jit(solution)/shard_map/mamba_steps/pallas_call | solution.py:63
  52.6 0.0 copy-start
  52.6 0.1 collective-permute-start
  52.7 1.5 collective-permute-done.refs_1_
  54.2 0.9 copy-done.13
  55.2 1.7 collective-permute-start.1
  56.8 2.9 %collective-permute-start.2 = (bf16[24,512]{1,0:T(8,128)(2,1)S(1)}, bf16[24,512]{1,0:T(8,128)(2,1)S(1)}, u32[]{:S(2)}, u32[]{:S(2)}) collective-permute-start(bf16[24,512]{1,0:T(8,128)(2,1)S(1)} %get-tuple-element.52), channel_id=1, source_target_pairs={{0,4},{1,5},{2,6},{3,7},{4,0},{5,1},{6,2},{7,3},{8,12},{9,13},{10,... | collective-permute-start | bytes 73736 | tf_op jit(solution)/shard_map/ppermute | solution.py:369
  59.7 1.3 collective-permute-start.3
  61.1 0.0 collective-permute-done.1.refs_1_
  61.1 1.1 collective-permute-done.2.refs_2_
  62.1 1.4 collective-permute-done.3.refs_3_
  63.5 0.8 copy-done.14
  64.3 0.1 stream_copies.1
  64.4 0.9 copy-done.3
  65.3 5.3 %all-to-all-start.1 = ((bf16[32,24,512]{2,1,0:T(8,128)(2,1)}), bf16[32,24,512]{2,1,0:T(8,128)(2,1)S(1)}, u32[]{:S(2)}, u32[]{:S(2)}) async-start(bf16[32,24,512]{2,1,0:T(8,128)(2,1)} %copy-done.3), calls=%async_computation.1 | async-start | bytes 1572864 | tf_op jit(solution)/shard_map/all_to_all | solution.py:646
  70.7 0.0 copy-start.2
  70.7 0.0 copy-start.16
  70.7 0.0 copy-start.18
  70.7 0.0 copy-start.20
  70.7 4.4 %update_states.1 = bf16[8,512,128]{2,1,0:T(8,128)(2,1)} custom-call(s32[8,256]{1,0:T(8,128)S(1)} %plan_states.1.refs_0_, f32[8,512,128]{2,1,0:T(8,128)S(1)} %bitcast.12, f32[8,8,512]{2,1,0:T(8,128)S(1)} %copy-done.11, f32[8,8,512]{2,1,0:T(8,128)S(1)} %copy-done.12, f32[8,8,128]{2,1,0:T(8,128)S(1)} %copy-done.15), custom_call_target="tpu_custom_call" | custom-call | flops 33554432 | bytes 3145728 | tf_op jit(solution)/shard_map/update_states/pallas_call | solution.py:63
  75.2 0.0 copy-start.19
  75.2 2.8 %routes.1 = (bf16[384,768]{1,0:T(8,128)(2,1)S(1)}, bf16[24,768]{1,0:T(8,128)(2,1)S(1)}, bf16[4,24,1536]{2,1,0:T(8,128)(2,1)S(1)}, bf16[4,24,1536]{2,1,0:T(8,128)(2,1)S(1)}) custom-call(s32[2,256]{1,0:T(2,128)S(1)} %copy-done.18, bf16[32,144,128]{2,1,0:T(8,128)(2,1)S(1)} %copy-done.2, s32[24,8]{1,0:T(8,128)S(1)} %bitcast.15, f32[24,8]{1,0:T(8,128)S(1)} %bitcast.17), custom_call_target="tpu_custom_call" | custom-call | flops 1000000000 | bytes 1048576 | tf_op jit(solution)/shard_map/routes/pallas_call | solution.py:63
  78.0 0.0 copy-start.7
  78.0 0.7 copy-done.7
  78.7 0.7 copy-done.9
  79.5 13.2 %all-to-all-done.1 = bf16[32,24,512]{2,1,0:T(8,128)(2,1)S(1)} async-done(((bf16[32,24,512]{2,1,0:T(8,128)(2,1)}), bf16[32,24,512]{2,1,0:T(8,128)(2,1)S(1)}, u32[]{:S(2)}, u32[]{:S(2)}) %all-to-all-start.1) | async-done | bytes 786464 | tf_op jit(solution)/shard_map/all_to_all | solution.py:646
  92.7 1.6 copy-done.4
  94.3 1.6 copy-done.5
  95.9 2.1 %expand_experts.1 = (bf16[4,48,2176]{2,1,0:T(8,128)(2,1)S(1)}, bf16[4,48,2176]{2,1,0:T(8,128)(2,1)S(1)}) custom-call(bf16[384,768]{1,0:T(8,128)(2,1)S(1)} %get-tuple-element.67.refs_0_, bf16[768,512]{1,0:T(8,128)(2,1)S(1)} %bitcast.13, f32[1,512]{1,0:T(1,128)S(1)} %bitcast.16, bf16[2,512,1024]{2,1,0:T(8,128)(2,1)S(1)} %copy-done.4, ...), custom_call_target="tpu_custom_call" | custom-call | flops 1107296256 | bytes 8388608 | tf_op jit(solution)/shard_map/expand_experts/pallas_call | solution.py:63
  98.0 0.1 collective-permute-start.4
  98.1 2.3 %collective-permute-done.4.refs_1_ = bf16[4,48,2176]{2,1,0:T(8,128)(2,1)S(1)} collective-permute-done((bf16[4,48,2176]{2,1,0:T(8,128)(2,1)S(1)}, bf16[4,48,2176]{2,1,0:T(8,128)(2,1)S(1)}, u32[]{:S(2)}, u32[]{:S(2)}) %collective-permute-start.4) | collective-permute-done | bytes 835616 | tf_op jit(solution)/shard_map/ppermute | solution.py:406
  100.4 0.3 add_cores.3
  100.7 4.9 %all-to-all-start.2 = ((bf16[32,128,128]{2,1,0:T(8,128)(2,1)}), bf16[32,128,128]{2,1,0:T(8,128)(2,1)S(1)}, u32[]{:S(2)}, u32[]{:S(2)}) async-start(bf16[32,128,128]{2,1,0:T(8,128)(2,1)} %bitcast.8), calls=%async_computation.2 | async-start | bytes 2097152 | tf_op jit(solution)/shard_map/all_to_all | solution.py:646
  105.7 0.3 collective-permute-start.5
  105.9 3.6 %collective-permute-start.6 = (bf16[48,2176]{1,0:T(8,128)(2,1)S(1)}, bf16[48,2176]{1,0:T(8,128)(2,1)S(1)}, u32[]{:S(2)}, u32[]{:S(2)}) collective-permute-start(bf16[48,2176]{1,0:T(8,128)(2,1)S(1)} %get-tuple-element.79), channel_id=1, source_target_pairs={{0,4},{1,5},{2,6},{3,7},{4,0},{5,1},{6,2},{7,3},{8,12},{9,13},{10,... | collective-permute-start | bytes 626696 | tf_op jit(solution)/shard_map/ppermute | solution.py:369
  109.5 0.4 collective-permute-start.7
  109.9 4.7 %collective-permute-done.5.refs_1_ = bf16[48,2176]{1,0:T(8,128)(2,1)S(1)} collective-permute-done((bf16[48,2176]{1,0:T(8,128)(2,1)S(1)}, bf16[48,2176]{1,0:T(8,128)(2,1)S(1)}, u32[]{:S(2)}, u32[]{:S(2)}) %collective-permute-start.5) | collective-permute-done | bytes 208928 | tf_op jit(solution)/shard_map/ppermute | solution.py:369
  114.5 4.0 %collective-permute-done.6.refs_2_ = bf16[48,2176]{1,0:T(8,128)(2,1)S(1)} collective-permute-done((bf16[48,2176]{1,0:T(8,128)(2,1)S(1)}, bf16[48,2176]{1,0:T(8,128)(2,1)S(1)}, u32[]{:S(2)}, u32[]{:S(2)}) %collective-permute-start.6) | collective-permute-done | bytes 208928 | tf_op jit(solution)/shard_map/ppermute | solution.py:369
  118.6 0.1 collective-permute-done.7.refs_3_
  118.7 0.2 hidden_units.1.refs_3_
  118.9 2.7 %collective-permute-start.10 = (bf16[48,1024]{1,0:T(8,128)(2,1)S(1)}, bf16[48,1024]{1,0:T(8,128)(2,1)S(1)}, u32[]{:S(2)}, u32[]{:S(2)}) collective-permute-start(bf16[48,1024]{1,0:T(8,128)(2,1)S(1)} %hidden_units.1.refs_3_), channel_id=1, source_target_pairs={{0,6},{1,7},{2,0},{3,1},{4,2},{5,3},{6,4},{7,5},{8,14},{9,15},{10,... | collective-permute-start | bytes 294920 | tf_op jit(solution)/shard_map/ppermute | solution.py:369
  121.6 0.3 collective-permute-start.9
  121.9 0.7 collective-permute-start.8
  122.5 0.0 collective-permute-start.11
  122.5 3.4 %collective-permute-done.10.refs_6_ = bf16[48,1024]{1,0:T(8,128)(2,1)S(1)} collective-permute-done((bf16[48,1024]{1,0:T(8,128)(2,1)S(1)}, bf16[48,1024]{1,0:T(8,128)(2,1)S(1)}, u32[]{:S(2)}, u32[]{:S(2)}) %collective-permute-start.10) | collective-permute-done | bytes 98336 | tf_op jit(solution)/shard_map/ppermute | solution.py:369
  126.0 0.0 collective-permute-start.14
  126.0 2.7 %collective-permute-done.9.refs_5_ = bf16[48,1024]{1,0:T(8,128)(2,1)S(1)} collective-permute-done((bf16[48,1024]{1,0:T(8,128)(2,1)S(1)}, bf16[48,1024]{1,0:T(8,128)(2,1)S(1)}, u32[]{:S(2)}, u32[]{:S(2)}) %collective-permute-start.9) | collective-permute-done | bytes 98336 | tf_op jit(solution)/shard_map/ppermute | solution.py:369
  128.6 0.0 collective-permute-start.13
  128.6 0.7 collective-permute-done.8.refs_4_
  129.4 0.0 collective-permute-done.14.refs_10_
  129.4 0.6 collective-permute-done.13.refs_9_
  129.9 0.7 collective-permute-done.12.refs_8_
  130.7 3.8 %all-to-all-done.2.refs_1_ = bf16[32,128,128]{2,1,0:T(8,128)(2,1)S(1)} async-done(((bf16[32,128,128]{2,1,0:T(8,128)(2,1)}), bf16[32,128,128]{2,1,0:T(8,128)(2,1)S(1)}, u32[]{:S(2)}, u32[]{:S(2)}) %all-to-all-start.2) | async-done | bytes 1048608 | tf_op jit(solution)/shard_map/all_to_all | solution.py:646
  134.4 1.6 copy-done.6
  136.0 3.8 %shrink_experts.1 = bf16[32,176,128]{2,1,0:T(8,128)(2,1)S(1)} custom-call(s32[8,256]{1,0:T(8,128)S(1)} %plan_states.1.refs_0_, bf16[32,128,128]{2,1,0:T(8,128)(2,1)S(1)} %all-to-all-done.2.refs_1_, bf16[2,1024,512]{2,1,0:T(8,128)(2,1)S(1)} %copy-done.6, bf16[48,1024]{1,0:T(8,128)(2,1)S(1)} %hidden_units.1.refs_3_, ...), custom_call_target="tpu_custom_call" | custom-call | flops 805306368 | bytes 4194304 | tf_op jit(solution)/shard_map/shrink_experts/pallas_call | solution.py:63
  139.8 0.0 copy-start.8
  139.8 43.7 %all_to_all.20.refs_1_ = bf16[32,176,128]{2,1,0:T(8,128)(2,1)S(1)} all-to-all(bf16[32,176,128]{2,1,0:T(8,128)(2,1)S(1)} %shrink_experts.1), channel_id=1, replica_groups=mesh['req'=32,'head'=8] {'req'}, dimensions={0} | all-to-all | bytes 2883584 | tf_op jit(solution)/shard_map/all_to_all | solution.py:646
  183.5 2.7 %finish.1 = (bf16[24,512]{1,0:T(8,128)(2,1)}, f32[8,512,128]{2,1,0:T(8,128)}) custom-call(s32[8,256]{1,0:T(8,128)S(1)} %plan_states.1.refs_0_, bf16[32,176,128]{2,1,0:T(8,128)(2,1)S(1)} %all_to_all.20.refs_1_, bf16[4,24,1536]{2,1,0:T(8,128)(2,1)S(1)} %copy-done.8, bf16[4,24,1536]{2,1,0:T(8,128)(2,1)S(1)} %copy-done.10, ...), custom_call_target="tpu_custom_call" | custom-call | flops 100000000 | bytes 4194304 | tf_op jit(solution)/shard_map/finish/pallas_call | solution.py:63
  (27 shorter events, 0.1 us)
Async XLA Ops:
  0.6 13.8 %copy-start.17 = (s32[2,256]{1,0:T(2,128)S(1)}, s32[2,256]{1,0:T(2,128)}, u32[]{:S(2)}) copy-start(s32[2,256]{1,0:T(2,128)} %refs_0_.6) | copy-start | bytes 6148
  3.3 42.4 %all-to-all-start = ((bf16[32,144,128]{2,1,0:T(8,128)(2,1)}), bf16[32,144,128]{2,1,0:T(8,128)(2,1)S(1)}, u32[]{:S(2)}, u32[]{:S(2)}) async-start(bf16[32,144,128]{2,1,0:T(8,128)(2,1)} %pack_inputs.1), calls=%async_computation | async-start | bytes 2359296 | tf_op jit(solution)/shard_map/all_to_all | solution.py:646
  45.7 1.0 copy-start.1
  52.6 18.0 %copy-start = (f32[8,8,64,128]{3,2,1,0:T(8,128)S(1)}, f32[8,8,64,128]{3,2,1,0:T(8,128)}, u32[]{:S(2)}) copy-start(f32[8,8,64,128]{3,2,1,0:T(8,128)} %param.18) | copy-start | bytes 6291460
  52.6 18.0 %copy-start.11 = (f32[8,8,512]{2,1,0:T(8,128)S(1)}, f32[8,8,512]{2,1,0:T(8,128)}, u32[]{:S(2)}) copy-start(f32[8,8,512]{2,1,0:T(8,128)} %get-tuple-element.59.refs_2_) | copy-start | bytes 393220
  52.6 18.0 %copy-start.12 = (f32[8,8,512]{2,1,0:T(8,128)S(1)}, f32[8,8,512]{2,1,0:T(8,128)}, u32[]{:S(2)}) copy-start(f32[8,8,512]{2,1,0:T(8,128)} %get-tuple-element.60.refs_3_) | copy-start | bytes 393220
  52.6 1.6 collective-permute-start
  54.2 0.9 copy-start.13
  55.2 5.9 %collective-permute-start.1 = (bf16[24,512]{1,0:T(8,128)(2,1)S(1)}, bf16[24,512]{1,0:T(8,128)(2,1)S(1)}, u32[]{:S(2)}, u32[]{:S(2)}) collective-permute-start(bf16[24,512]{1,0:T(8,128)(2,1)S(1)} %get-tuple-element.51), channel_id=1, source_target_pairs={{0,2},{1,3},{2,4},{3,5},{4,6},{5,7},{6,0},{7,1},{8,10},{9,11},{10,... | collective-permute-start | bytes 73736 | tf_op jit(solution)/shard_map/ppermute | solution.py:369
  56.8 5.3 %collective-permute-start.2 = (bf16[24,512]{1,0:T(8,128)(2,1)S(1)}, bf16[24,512]{1,0:T(8,128)(2,1)S(1)}, u32[]{:S(2)}, u32[]{:S(2)}) collective-permute-start(bf16[24,512]{1,0:T(8,128)(2,1)S(1)} %get-tuple-element.52), channel_id=1, source_target_pairs={{0,4},{1,5},{2,6},{3,7},{4,0},{5,1},{6,2},{7,3},{8,12},{9,13},{10,... | collective-permute-start | bytes 73736 | tf_op jit(solution)/shard_map/ppermute | solution.py:369
  59.7 3.8 %collective-permute-start.3 = (bf16[24,512]{1,0:T(8,128)(2,1)S(1)}, bf16[24,512]{1,0:T(8,128)(2,1)S(1)}, u32[]{:S(2)}, u32[]{:S(2)}) collective-permute-start(bf16[24,512]{1,0:T(8,128)(2,1)S(1)} %get-tuple-element.53), channel_id=1, source_target_pairs={{0,6},{1,7},{2,0},{3,1},{4,2},{5,3},{6,4},{7,5},{8,14},{9,15},{10,... | collective-permute-start | bytes 73736 | tf_op jit(solution)/shard_map/ppermute | solution.py:369
  63.5 0.8 copy-start.14
  64.3 6.3 %copy-start.15 = (f32[8,8,128]{2,1,0:T(8,128)S(1)}, f32[8,8,128]{2,1,0:T(8,128)}, u32[]{:S(2)}) copy-start(f32[8,8,128]{2,1,0:T(8,128)} %get-tuple-element.61.refs_4_) | copy-start | bytes 98308
  64.4 0.9 copy-start.3
  65.3 27.4 %all-to-all-start.1 = ((bf16[32,24,512]{2,1,0:T(8,128)(2,1)}), bf16[32,24,512]{2,1,0:T(8,128)(2,1)S(1)}, u32[]{:S(2)}, u32[]{:S(2)}) async-start(bf16[32,24,512]{2,1,0:T(8,128)(2,1)} %copy-done.3), calls=%async_computation.1 | async-start | bytes 1572864 | tf_op jit(solution)/shard_map/all_to_all | solution.py:646
  70.7 4.5 %copy-start.2 = (bf16[32,144,128]{2,1,0:T(8,128)(2,1)S(1)}, bf16[32,144,128]{2,1,0:T(8,128)(2,1)}, u32[]{:S(2)}) copy-start(bf16[32,144,128]{2,1,0:T(8,128)(2,1)} %copy-done.1) | copy-start | bytes 3538948
  70.7 4.5 %copy-start.16 = (s32[3,8,8]{2,1,0:T(8,128)S(1)}, s32[3,8,8]{2,1,0:T(8,128)}, u32[]{:S(2)}) copy-start(s32[3,8,8]{2,1,0:T(8,128)} %refs_7_.2) | copy-start | bytes 2308
  70.7 4.5 %copy-start.18 = (s32[2,256]{1,0:T(2,128)S(1)}, s32[2,256]{1,0:T(2,128)}, u32[]{:S(2)}) copy-start(s32[2,256]{1,0:T(2,128)} %refs_0_.6) | copy-start | bytes 6148
  70.7 4.5 %copy-start.20 = (f32[3,8,8]{2,1,0:T(8,128)S(1)}, f32[3,8,8]{2,1,0:T(8,128)}, u32[]{:S(2)}) copy-start(f32[3,8,8]{2,1,0:T(8,128)} %param.31) | copy-start | bytes 2308
  75.2 17.5 %copy-start.19 = (f32[512]{0:T(512)S(1)}, f32[512]{0:T(512)}, u32[]{:S(2)}) copy-start(f32[512]{0:T(512)} %param.29) | copy-start | bytes 6148
  78.0 0.7 copy-start.7
  78.7 0.7 copy-start.9
  92.7 1.6 copy-start.4
  94.3 1.6 copy-start.5
  98.0 2.4 %collective-permute-start.4 = (bf16[4,48,2176]{2,1,0:T(8,128)(2,1)S(1)}, bf16[4,48,2176]{2,1,0:T(8,128)(2,1)S(1)}, u32[]{:S(2)}, u32[]{:S(2)}) collective-permute-start(bf16[4,48,2176]{2,1,0:T(8,128)(2,1)S(1)} %get-tuple-element.70), channel_id=1, source_target_pairs={{0,1},{1,0},{2,3},{3,2},{4,5},{5,4},{6,7},{7,6},{8,9},{9,8},{10,11... | collective-permute-start | bytes 2506760 | tf_op jit(solution)/shard_map/ppermute | solution.py:406
  100.7 33.7 %all-to-all-start.2 = ((bf16[32,128,128]{2,1,0:T(8,128)(2,1)}), bf16[32,128,128]{2,1,0:T(8,128)(2,1)S(1)}, u32[]{:S(2)}, u32[]{:S(2)}) async-start(bf16[32,128,128]{2,1,0:T(8,128)(2,1)} %bitcast.8), calls=%async_computation.2 | async-start | bytes 2097152 | tf_op jit(solution)/shard_map/all_to_all | solution.py:646
  105.7 8.9 %collective-permute-start.5 = (bf16[48,2176]{1,0:T(8,128)(2,1)S(1)}, bf16[48,2176]{1,0:T(8,128)(2,1)S(1)}, u32[]{:S(2)}, u32[]{:S(2)}) collective-permute-start(bf16[48,2176]{1,0:T(8,128)(2,1)S(1)} %get-tuple-element.78), channel_id=1, source_target_pairs={{0,2},{1,3},{2,4},{3,5},{4,6},{5,7},{6,0},{7,1},{8,10},{9,11},{10,... | collective-permute-start | bytes 626696 | tf_op jit(solution)/shard_map/ppermute | solution.py:369
  105.9 12.7 %collective-permute-start.6 = (bf16[48,2176]{1,0:T(8,128)(2,1)S(1)}, bf16[48,2176]{1,0:T(8,128)(2,1)S(1)}, u32[]{:S(2)}, u32[]{:S(2)}) collective-permute-start(bf16[48,2176]{1,0:T(8,128)(2,1)S(1)} %get-tuple-element.79), channel_id=1, source_target_pairs={{0,4},{1,5},{2,6},{3,7},{4,0},{5,1},{6,2},{7,3},{8,12},{9,13},{10,... | collective-permute-start | bytes 626696 | tf_op jit(solution)/shard_map/ppermute | solution.py:369
  109.5 9.2 %collective-permute-start.7 = (bf16[48,2176]{1,0:T(8,128)(2,1)S(1)}, bf16[48,2176]{1,0:T(8,128)(2,1)S(1)}, u32[]{:S(2)}, u32[]{:S(2)}) collective-permute-start(bf16[48,2176]{1,0:T(8,128)(2,1)S(1)} %get-tuple-element.80), channel_id=1, source_target_pairs={{0,6},{1,7},{2,0},{3,1},{4,2},{5,3},{6,4},{7,5},{8,14},{9,15},{10,... | collective-permute-start | bytes 626696 | tf_op jit(solution)/shard_map/ppermute | solution.py:369
  118.9 7.1 %collective-permute-start.10 = (bf16[48,1024]{1,0:T(8,128)(2,1)S(1)}, bf16[48,1024]{1,0:T(8,128)(2,1)S(1)}, u32[]{:S(2)}, u32[]{:S(2)}) collective-permute-start(bf16[48,1024]{1,0:T(8,128)(2,1)S(1)} %hidden_units.1.refs_3_), channel_id=1, source_target_pairs={{0,6},{1,7},{2,0},{3,1},{4,2},{5,3},{6,4},{7,5},{8,14},{9,15},{10,... | collective-permute-start | bytes 294920 | tf_op jit(solution)/shard_map/ppermute | solution.py:369
  121.6 7.1 %collective-permute-start.9 = (bf16[48,1024]{1,0:T(8,128)(2,1)S(1)}, bf16[48,1024]{1,0:T(8,128)(2,1)S(1)}, u32[]{:S(2)}, u32[]{:S(2)}) collective-permute-start(bf16[48,1024]{1,0:T(8,128)(2,1)S(1)} %hidden_units.1.refs_3_), channel_id=1, source_target_pairs={{0,4},{1,5},{2,6},{3,7},{4,0},{5,1},{6,2},{7,3},{8,12},{9,13},{10,... | collective-permute-start | bytes 294920 | tf_op jit(solution)/shard_map/ppermute | solution.py:369
  121.9 7.5 %collective-permute-start.8 = (bf16[48,1024]{1,0:T(8,128)(2,1)S(1)}, bf16[48,1024]{1,0:T(8,128)(2,1)S(1)}, u32[]{:S(2)}, u32[]{:S(2)}) collective-permute-start(bf16[48,1024]{1,0:T(8,128)(2,1)S(1)} %hidden_units.1.refs_3_), channel_id=1, source_target_pairs={{0,2},{1,3},{2,4},{3,5},{4,6},{5,7},{6,0},{7,1},{8,10},{9,11},{10,... | collective-permute-start | bytes 294920 | tf_op jit(solution)/shard_map/ppermute | solution.py:369
  122.5 6.8 %collective-permute-start.11 = (bf16[48,1024]{1,0:T(8,128)(2,1)S(1)}, bf16[48,1024]{1,0:T(8,128)(2,1)S(1)}, u32[]{:S(2)}, u32[]{:S(2)}) collective-permute-start(bf16[48,1024]{1,0:T(8,128)(2,1)S(1)} %hidden_units.1.refs_3_), channel_id=1, source_target_pairs={{0,1},{1,0},{2,3},{3,2},{4,5},{5,4},{6,7},{7,6},{8,9},{9,8},{10,11... | collective-permute-start | bytes 294920 | tf_op jit(solution)/shard_map/ppermute | solution.py:680
  126.0 3.4 %collective-permute-start.14 = (bf16[48,1024]{1,0:T(8,128)(2,1)S(1)}, bf16[48,1024]{1,0:T(8,128)(2,1)S(1)}, u32[]{:S(2)}, u32[]{:S(2)}) collective-permute-start(bf16[48,1024]{1,0:T(8,128)(2,1)S(1)} %collective-permute-done.10.refs_6_), channel_id=1, source_target_pairs={{0,1},{1,0},{2,3},{3,2},{4,5},{5,4},{6,7},{7,6},{8,9},{9,8},{10,11... | collective-permute-start | bytes 294920 | tf_op jit(solution)/shard_map/ppermute | solution.py:680
  128.6 1.3 collective-permute-start.13
  129.4 1.3 collective-permute-start.12
  134.4 1.6 copy-start.6
  139.8 43.7 %copy-start.8 = (bf16[4,24,1536]{2,1,0:T(8,128)(2,1)S(1)}, bf16[4,24,1536]{2,1,0:T(8,128)(2,1)}, u32[]{:S(2)}) copy-start(bf16[4,24,1536]{2,1,0:T(8,128)(2,1)} %copy-done.7) | copy-start | bytes 884740
  139.8 43.7 %copy-start.10 = (bf16[4,24,1536]{2,1,0:T(8,128)(2,1)S(1)}, bf16[4,24,1536]{2,1,0:T(8,128)(2,1)}, u32[]{:S(2)}) copy-start(bf16[4,24,1536]{2,1,0:T(8,128)(2,1)} %copy-done.9) | copy-start | bytes 884740

commit v3 on v2

--- a/solution.py
+++ b/solution.py
@@ -143,8 +143,7 @@
 LAST = 24
 PIECES = 15
 MESSAGE = LAST + PIECES * SLOTS
-
-
+SPARE = 3
 def place_pieces(value):
     parts = []
     rest = value
@@ -175,20 +174,117 @@
     return contract(hot(jnp.broadcast_to(dest_row, slot.shape) == slot), owner).astype(BF16)
 
 
-def pack_kernel(ins, outs, scratch, wait):
-    dest_ref, x_ref, z_ref, residual_ref, b_ref, c_ref, dt_ref, ids_ref = ins
+def step_pieces(ins, step):
+    x_ref, z_ref, residual_ref, b_ref, c_ref, dt_ref = ins
+    columns = pl.ds(pl.multiple_of(lax.axis_index("head") * WIDTH, WIDTH), WIDTH)
+    wide = [x_ref[step], z_ref[step], residual_ref[step, :, columns]]
+    cut = [value[:, 128 * i : 128 * (i + 1)] for value in wide for i in range(4)]
+    return cut + [b_ref[step], c_ref[step], place_pieces(dt_ref[step]).astype(BF16)]
+
+
+def pack_few_kernel(ins, outs, scratch, wait):
+    dest_ref, ids_ref = ins[0], ins[7]
+    (message_ref, most_ref), (wide_ref,) = outs, scratch
+    me = lax.axis_index("req")
+    back = sender_match(dest_ref[0:1, :], me)
+    square = (REQUESTS, REQUESTS)
+    hop = hot(jnp.broadcast_to(dest_ref[0:1, :], square) == iota(square, 0))
+    second = jnp.broadcast_to(dest_ref[1:2, :], (8, REQUESTS)).astype(F32).astype(BF16)
+    both = contract(second, hop)[0:1, :].astype(jnp.int32)
+    home = sender_match(both, me).astype(F32)
+    same = contract(home.astype(BF16), home.astype(BF16), ((1,), (1,)))
+    before = iota((SLOTS, SLOTS), 1) < iota((SLOTS, SLOTS), 0)
+    rank = jnp.sum(jnp.where(before, same, 0.0), axis=1, keepdims=True)
+    target = hot((jnp.broadcast_to(both, (OWNERS, REQUESTS)) >> 3) == iota((OWNERS, REQUESTS), 0))
+    source = hot((iota((REQUESTS, OWNERS), 0) >> 3) == iota((REQUESTS, OWNERS), 1))
+    most_ref[0, 0] = jnp.max(contract(target, source)).astype(jnp.int32)
+    over = ((0,), (0,))
+    one = jnp.concatenate(step_pieces(ins[1:7], 1), axis=1)
+    two = jnp.concatenate(step_pieces(ins[1:7], 2), axis=1)
+    rows = [contract(back, one, over)]
+    for place in range(SPARE):
+        rows.append(contract(jnp.where(rank == place, home, 0.0).astype(BF16), two, over))
+    for block, value in enumerate(rows):
+        for row in range(PIECES):
+            wide_ref[:, block * 16 + row, :] = value[:, row * 128 : (row + 1) * 128]
+    for half in range(2):
+        total = jnp.zeros((8, 128), F32)
+        for step in range(STEPS):
+            for slot in range(4):
+                spot = hot(iota((8, 128), 1) == iota((8, 128), 0) + 24 * slot + 8 * step)
+                here = ids_ref[step].astype(F32)[half * 4 + slot : half * 4 + slot + 1, :]
+                total = total + contract(jnp.broadcast_to(here, (8, 8)).astype(BF16), spot)
+        wide_ref[:, half * 16 + 15, :] = jnp.broadcast_to(total[0:1, :], (OWNERS, 128))
+    for block in range(2, SPARE + 1):
+        wide_ref[:, block * 16 + 15, :] = jnp.zeros((OWNERS, 128), F32)
+    message_ref[...] = wide_ref[...].astype(BF16)
+
+
+def pack_few(*arrays):
+    shape = (OWNERS, 16 * (SPARE + 1), 128)
+    outs = [shaped(shape, BF16), shaped((1, 1), jnp.int32)]
+    scratch = [pltpu.VMEM(shape, F32)]
+    args = [(array, "h") for array in arrays]
+    specs = [VMEM_SPEC, pl.BlockSpec(memory_space=pltpu.SMEM)]
+    return run_kernel(pack_few_kernel, args, outs, "pack_few", scratch, out_specs=specs, limit=58)
+
+
+def own_slots(dest_ref):
+    first = lax.axis_index("req") * SLOTS
+    middle = [dest_ref[0, first + slot] for slot in range(SLOTS)]
+    return middle, [dest_ref[1, slot] for slot in middle]
+
+
+def take_few_kernel(ins, outs, scratch, wait):
+    dest_ref, got_ref = ins
+    (rows_ref, ids_ref), (wide_ref,) = outs, scratch
+    middle, final = own_slots(dest_ref)
+    for slot in range(SLOTS):
+        rows_ref[slot, 0:16, :] = got_ref[middle[slot] // SLOTS, 0:16, :]
+        owner = final[slot] // SLOTS
+        rank = jnp.int32(0)
+        for other in range(SLOTS):
+            if other != slot:
+                ahead = (final[other] // SLOTS == owner) & (final[other] < final[slot])
+                rank = rank + ahead.astype(jnp.int32)
+        start = pl.multiple_of(16 + 16 * jnp.minimum(rank, SPARE - 1), 16)
+        rows_ref[slot, 16:32, :] = got_ref[owner, pl.ds(start, 16), :]
+    wide = got_ref[:, 0:32, :].astype(F32)
+    for slot in range(SLOTS):
+        row = wide[:, 16 * (slot // 4) + 15, :].astype(BF16)
+        lane = iota((128, 128), 1)
+        spot = hot((iota((128, 128), 0) == lane - 24 + 24 * (slot % 4)) & (lane >= 24) & (lane < 48))
+        wide_ref[:, slot, :] = contract(row, spot)
+    ids_ref[...] = wide_ref[...].reshape(REQUESTS, 128).astype(BF16)
+
+
+def take_all_kernel(ins, outs, scratch, wait):
+    dest_ref, got_ref = ins
+    (rows_ref, ids_ref), (wide_ref, picked_ref) = outs, scratch
+    middle, final = own_slots(dest_ref)
+    picked_ref[...] = jnp.zeros_like(picked_ref)
+    for slot in range(SLOTS):
+        rows_ref[slot, 0:16, :] = got_ref[middle[slot] // SLOTS, 0:16, :]
+        wide_ref[slot] = got_ref[final[slot] // SLOTS].astype(F32)
+        picked_ref[slot, 0:PIECES, :] = wide_ref[
+            slot, pl.ds(LAST + final[slot] % SLOTS, PIECES, stride=SLOTS), :
+        ]
+    rows_ref[:, 16:32, :] = picked_ref[...].astype(BF16)
+    ids = got_ref[:, MESSAGE - 16 :, :].astype(F32)[:, SLOTS:, :]
+    ids_ref[...] = ids.reshape(REQUESTS, 128).astype(BF16)
+
+
+def take(body, dest, got, scratch):
+    outs = [shaped((SLOTS, 32, 128), BF16), shaped((REQUESTS, 128), BF16)]
+    return tuple(run_kernel(body, [(dest, "s"), (got, "v")], outs, "take_rows", scratch))
+
+
+def pack_all_kernel(ins, outs, scratch, wait):
+    dest_ref, ids_ref = ins[0], ins[7]
     (message_ref,), (wide_ref, last_ref) = outs, scratch
-    me = lax.axis_index("req")
-    columns = pl.ds(pl.multiple_of(lax.axis_index("head") * WIDTH, WIDTH), WIDTH)
-    back = sender_match(dest_ref[0:1, :], me)
-
-    def pieces(step):
-        wide = [x_ref[step], z_ref[step], residual_ref[step, :, columns]]
-        cut = [value[:, 128 * i : 128 * (i + 1)] for value in wide for i in range(4)]
-        return cut + [b_ref[step], c_ref[step], place_pieces(dt_ref[step]).astype(BF16)]
-
-    one = pieces(1)
-    two = pieces(2)
+    back = sender_match(dest_ref[0:1, :], lax.axis_index("req"))
+    one = step_pieces(ins[1:7], 1)
+    two = step_pieces(ins[1:7], 2)
     wide_ref[:, PIECES:LAST, :] = jnp.zeros((OWNERS, LAST - PIECES, 128), F32)
     for row in range(PIECES):
         wide_ref[:, row, :] = contract(back, one[row], ((0,), (0,)))
@@ -207,10 +303,10 @@
     message_ref[:, 32:MESSAGE, :] = jnp.broadcast_to(last[None], (OWNERS,) + last.shape)
 
 
-def pack_inputs(*arrays):
+def pack_all(*arrays):
     outs = [shaped((OWNERS, MESSAGE, 128), BF16)]
     scratch = [pltpu.VMEM((OWNERS, 32, 128), F32), pltpu.VMEM((MESSAGE - 32, 128), F32)]
-    return run_kernel(pack_kernel, [(array, "h") for array in arrays], outs, "pack_inputs", scratch, limit=58)[0]
+    return run_kernel(pack_all_kernel, [(array, "h") for array in arrays], outs, "pack_all", scratch, limit=58)[0]
 
 
 def head_spread():
@@ -232,20 +328,12 @@
 
 
 def mamba_kernel(ins, outs, scratch, wait):
-    dest_ref, got_ref, state_ref, x_ref, z_ref, residual_ref, b_ref, c_ref, dt_ref = ins[:9]
-    decay_ref, skip_ref, gain_ref, weight_ref = ins[9:]
+    got_ref, state_ref, x_ref, z_ref, residual_ref, b_ref, c_ref, dt_ref = ins[:8]
+    decay_ref, skip_ref, gain_ref, weight_ref = ins[8:]
     keep_ref, send_ref, residual_out_ref, outer_ref, kept_ref, b_rows_ref = outs
-    wide_ref, rows_in_ref, c_rows_ref, read_ref, rows_ref = scratch
-    me = lax.axis_index("req")
+    rows_in_ref, c_rows_ref, read_ref, rows_ref = scratch
     column = lax.axis_index("head")
-    for slot in range(SLOTS):
-        middle = dest_ref[0, me * SLOTS + slot]
-        final = dest_ref[1, middle]
-        rows_in_ref[slot, 0:16, :] = got_ref[middle // SLOTS, 0:16, :].astype(F32)
-        wide_ref[slot] = got_ref[final // SLOTS].astype(F32)
-        rows_in_ref[slot, 16 : 16 + PIECES, :] = wide_ref[
-            slot, pl.ds(LAST + final % SLOTS, PIECES, stride=SLOTS), :
-        ]
+    rows_in_ref[...] = got_ref[...].astype(F32)
     xs = [x_ref[0].astype(F32), read_rows(rows_in_ref, 0), read_rows(rows_in_ref, 16)]
     zs = [z_ref[0].astype(F32), read_rows(rows_in_ref, 4), read_rows(rows_in_ref, 20)]
     steps_b = [b_ref[0].astype(F32), rows_in_ref[:, 12, :], rows_in_ref[:, 28, :]]
@@ -260,7 +348,7 @@
     for step in range(STEPS):
         c_rows_ref[:, step, :] = steps_c[step]
     across = ((1,), (1,))
-    wait(2)
+    wait(1)
     for slot in range(SLOTS):
         high, low = split_pair(state_ref[slot])
         c_rows = c_rows_ref[slot].astype(BF16)
@@ -283,7 +371,7 @@
         scale = lax.rsqrt(jnp.mean(gated * gated, axis=1, keepdims=True) + NORM_EPS)
         rows_ref[step * SLOTS : (step + 1) * SLOTS, :] = gated * scale * gain_ref[...]
     rows = rows_ref[...].astype(BF16)
-    wait(12)
+    wait(11)
     for turn in range(HEADS):
         block = 2 * ((column // 2 + turn) % 4) + (column + turn // 4) % 2
         columns = pl.ds(pl.multiple_of(block * WIDTH, WIDTH), WIDTH)
@@ -303,18 +391,17 @@
     kept_ref[:, 0, :] = kept[0] * (kept[1] * late)
 
 
-def mamba(dest, got, state, *arrays):
+def mamba(got, state, *arrays):
     part = shaped((4, ROWS, WIDTH), BF16)
     factor = shaped((SLOTS, 8, WIDTH), F32)
     outs = [part, part, shaped((ROWS, WIDTH), F32), factor, factor, shaped((SLOTS, 8, NSTATE), F32)]
     scratch = [
-        pltpu.VMEM((SLOTS, MESSAGE, 128), F32),
         pltpu.VMEM((SLOTS, 32, 128), F32),
         pltpu.VMEM((SLOTS, 8, NSTATE), F32),
         pltpu.VMEM((SLOTS, 8, WIDTH), F32),
         pltpu.VMEM((ROWS, WIDTH), F32),
     ]
-    args = [(dest, "s"), (got, "v"), (state, "l")] + [(array, "h") for array in arrays[:-1]] + [(arrays[-1], "l")]
+    args = [(got, "v"), (state, "l")] + [(array, "h") for array in arrays[:-1]] + [(arrays[-1], "l")]
     return run_kernel(mamba_kernel, args, outs, "mamba_steps", scratch, 2 * 24 * 512 * 4096, 8 * 2**20, limit=54)
 
 
@@ -428,7 +515,7 @@
 
 
 def routes_kernel(ins, outs, scratch, wait):
-    dest_ref, got_ref, ids_ref, weights_ref = ins
+    dest_ref, all_ids_ref, ids_ref, weights_ref = ins
     pick_ref, kept_ref, high_ref, low_ref = outs
     me = lax.axis_index("req")
     column = lax.axis_index("head")
@@ -451,7 +538,7 @@
     for step in range(STEPS):
         wide = jnp.broadcast_to(slots[step], (8, REQUESTS)).astype(F32).astype(BF16)
         at_row = at_row + contract(wide, spread[step])
-    ids = got_ref[:, MESSAGE - 16 :, :].astype(F32)[:, SLOTS:, :].reshape(REQUESTS, 128)
+    ids = all_ids_ref[...].astype(F32)
     step_of = hot((iota((128, 128), 0) >> 3) == iota((128, 128), 1) + 3)
     earlier = hot(((row_id >> 3) == (col_id >> 3)) & (row_id < col_id))
     slot = iota((REQUESTS, 128), 0)
@@ -502,7 +589,7 @@
             out_ref[piece] = jnp.where(spot // 12 == piece, value, 0.0).astype(BF16)
 
 
-def routes(dest, got, ids, weights):
+def routes(dest, all_ids, ids, weights):
     total_rows = OWNERS * ROWS
     mixing = shaped((4, ROWS, OWNERS * CHUNK), BF16)
     outs = [
@@ -511,7 +598,7 @@
         mixing,
         mixing,
     ]
-    args = [(dest, "h"), (got, "v"), (ids, "h"), (weights, "h")]
+    args = [(dest, "h"), (all_ids, "v"), (ids, "h"), (weights, "h")]
     return run_kernel(routes_kernel, args, outs, "routes", flops=10**9)
 
 
@@ -654,19 +741,26 @@
     state_rows = states.reshape(SLOTS, HEADS * HSIZE, NSTATE)
     own = (ssm_x, gate_z, residual, ssm_b, ssm_c, dt_raw)
 
-    message = pack_inputs(dest, *own, route_ids)
-    message, later_dest = fence((message, dest))
-    got = exchange(message)
-    table = routing_tables(later_dest)
-    got, table = fence((got, table))
+    message, most = pack_few(dest, *own, route_ids)
+
+    def few(message):
+        scratch = [pltpu.VMEM((OWNERS, SLOTS, 128), F32)]
+        return take(take_few_kernel, dest, exchange(message), scratch)
+
+    def every(_):
+        scratch = [pltpu.VMEM((SLOTS, MESSAGE, 128), F32), pltpu.VMEM((SLOTS, 16, 128), F32)]
+        return take(take_all_kernel, dest, exchange(pack_all(dest, *own, route_ids)), scratch)
+
+    rows, all_ids = lax.cond(most[0, 0] <= SPARE, few, every, message)
 
     keep_part, send_part, home_residual, *factors = mamba(
-        dest, got, state_rows, *own, decay_rate[None], skip_gain[None], ssm_gain[None], out_weight
+        rows, state_rows, *own, decay_rate[None], skip_gain[None], ssm_gain[None], out_weight
     )
     parts, _ = scatter_sum(keep_part, send_part, False)
-    copies, got, factors = fence((stream_copies(parts, home_residual), got, factors))
+    copies, later_dest, all_ids, factors = fence((stream_copies(parts, home_residual), dest, all_ids, factors))
     streams = exchange(copies).reshape(OWNERS * ROWS, WIDTH)
-    routed = routes(dest, got, route_ids.reshape(ROWS, 8), route_weights.reshape(ROWS, 8))
+    table = routing_tables(later_dest)
+    routed = routes(later_dest, all_ids, route_ids.reshape(ROWS, 8), route_weights.reshape(ROWS, 8))
     pieces = update_states(table, state_rows, factors)
     streams, pieces, (pick, kept, high, low) = fence((streams, pieces, routed))
 

time: 187 us -> 171 us (0.914)
  waiting for transfers between devices: 65.8 us -> 34.6 us
  blocking collectives: 43.7 us -> 72.3 us
  starting transfers between devices: 35.4 us -> 23.8 us
  local copies, waits for them, and re-layouts: 9.85 us -> 6.35 us
    all_to_all x3 -> x2, waiting for transfers between devices: 42.6 us -> 11.4 us  [exchange(): return lax.all_to_all(value, 'req', split_axis=0, concat_axis=0, tiled=True)]
    all_to_all x1 -> x2, blocking collectives: 43.7 us -> 72.3 us  [exchange(): return lax.all_to_all(value, 'req', split_axis=0, concat_axis=0, tiled=True)]
    all_to_all x3 -> x2, starting transfers between devices: 21.5 us -> 9.81 us  [exchange(): return lax.all_to_all(value, 'req', split_axis=0, concat_axis=0, tiled=True)]
    unnamed x42 -> x36, local copies, waits for them, and re-layouts: 9.85 us -> 6.35 us
    pallas_call x12 -> x13, Pallas kernels: 30.5 us -> 31.4 us  [run_kernel(): pl.pallas_call(kernel, out_shape=tuple(outs), in_specs=[VMEM_SPEC if mode...]
  transfers between devices with their start and end apart: 18 -> 17, of which waited for: 15 -> 14; matrix products, arithmetic and copies ran while one was open for 0% -> 0% of each run, Pallas kernels for 7% -> 8%
where the time goes in v3:
time: 171 us; the launch traced here: 170 us
  blocking collectives  72.3 us (42%)
  waiting for transfers between devices  34.6 us (20%)
  Pallas kernels  31.4 us (18%)
  starting transfers between devices  23.8 us (14%)
  local copies, waits for them, and re-layouts  6.35 us (4%)
  between operations  1.76 us (1%)
    all_to_all x2, blocking collectives, exchange(): return lax.all_to_all(value, 'req', split_axis=0, concat_axis=0, tiled=True)  72.3 us
    pallas_call x13, Pallas kernels, run_kernel(): pl.pallas_call(kernel, out_shape=tuple(outs), in_specs=[VMEM_SPEC if mode...  31.4 us
    ppermute x9, waiting for transfers between devices, along_y(): return lax.ppermute(value, 'head', moves)  18.1 us
    ppermute x9, starting transfers between devices, along_y(): return lax.ppermute(value, 'head', moves)  13.8 us
    all_to_all x2, waiting for transfers between devices, exchange(): return lax.all_to_all(value, 'req', split_axis=0, concat_axis=0, tiled=True)  11.4 us
    all_to_all x2, starting transfers between devices, exchange(): return lax.all_to_all(value, 'req', split_axis=0, concat_axis=0, tiled=True)  9.81 us
    unnamed x36, local copies, waits for them, and re-layouts  6.35 us
    ppermute x2, waiting for transfers between devices, scatter_sum(): got = lax.ppermute(send, 'head', CORES)  3.84 us
  transfers between devices with their start and end apart: 17, of which 14 were waited for; matrix products, arithmetic and copies ran while one was open for 0% of the time, Pallas kernels for 8%

profile of v3, /device:TPU:32, one launch (start us, length us, event | category | flops | bytes accessed | tf_op | source)
XLA Modules:
  0.0 170.3 jit_solution(16855860514334825732)
XLA Ops:
  0.6 2.4 %pack_few.1 = (bf16[32,64,128]{2,1,0:T(8,128)(2,1)S(1)}, s32[1,1]{1,0:T(1,128)}) custom-call(s32[2,256]{1,0:T(2,128)} %refs_0_.3, bf16[3,8,512]{2,1,0:T(8,128)(2,1)} %refs_2_.4, bf16[3,8,512]{2,1,0:T(8,128)(2,1)} %refs_3_.4, bf16[3,8,4096]{2,1,0:T(8,128)(2,1)} %refs_4_.4, bf16[3,8,128]{2,1,0:T(8,128)(2,1)} %refs_5_.3, bf16[3,8,128]{2,1,0:T(8,128)(2,1)} %refs_6_.3, ...), custom_call_target="tpu_custom_call" | custom-call | bytes 1048576 | tf_op jit(solution)/shard_map/pack_few/pallas_call | solution.py:63
  3.6 30.2 %conditional.1 = ((bf16[8,32,128]{2,1,0:T(8,128)(2,1)S(1)}, bf16[256,128]{1,0:T(8,128)(2,1)})) conditional(s32[]{:T(128)} %bitcast, (s32[2,256]{1,0:T(2,128)}, bf16[3,8,512]{2,1,0:T(8,128)(2,1)}, bf16[3,8,512]{2,1,0:T(8,128)(2,1)}, bf16[3,8,4096]{2,1,0:T(8,128)(2,1)}, bf16[3,8,128]{2,1,0:T(8,128)(2,1)}, /*index=5*/bf16[3,8,128]{2,1,0:T(8,128)(2,1)}, ...), branch_computations={%region_0.0_spmd, %region_1.0_spmd} | conditional | bytes 4464676 | solution.py:754
  3.7 28.6 %all_to_all.24.refs_1_ = bf16[32,64,128]{2,1,0:T(8,128)(2,1)S(1)} all-to-all(bf16[32,64,128]{2,1,0:T(8,128)(2,1)S(1)} %get-tuple-element.29), channel_id=1, replica_groups=mesh['req'=32,'head'=8] {'req'}, dimensions={0} | all-to-all | bytes 1048576 | tf_op jit(solution)/shard_map/cond/branch_1_fun/all_to_all | solution.py:733
  32.3 1.6 take_rows.3
  33.8 4.6 %mamba_steps.1 = (bf16[4,24,512]{2,1,0:T(8,128)(2,1)}, bf16[4,24,512]{2,1,0:T(8,128)(2,1)}, f32[24,512]{1,0:T(8,128)}, f32[8,8,512]{2,1,0:T(8,128)}, f32[8,8,512]{2,1,0:T(8,128)}, /*index=5*/f32[8,8,128]{2,1,0:T(8,128)}) custom-call(bf16[8,32,128]{2,1,0:T(8,128)(2,1)S(1)} %get-tuple-element.77.refs_0_, f32[8,512,128]{2,1,0:T(8,128)} %bitcast.12, ...), custom_call_target="tpu_custom_call" | custom-call | flops 100663296 | bytes 8388608 | tf_op jit(solution)/shard_map/mamba_steps/pallas_call | solution.py:63
  38.5 0.0 copy-start.16
  38.5 0.1 collective-permute-start
  38.6 1.5 collective-permute-done.refs_1_
  40.1 0.9 copy-done.10
  41.0 1.7 collective-permute-start.1
  42.7 2.9 %collective-permute-start.2 = (bf16[24,512]{1,0:T(8,128)(2,1)S(1)}, bf16[24,512]{1,0:T(8,128)(2,1)S(1)}, u32[]{:S(2)}, u32[]{:S(2)}) collective-permute-start(bf16[24,512]{1,0:T(8,128)(2,1)S(1)} %get-tuple-element.82), channel_id=1, source_target_pairs={{0,4},{1,5},{2,6},{3,7},{4,0},{5,1},{6,2},{7,3},{8,12},{9,13},{10,... | collective-permute-start | bytes 73736 | tf_op jit(solution)/shard_map/ppermute | solution.py:456
  45.6 1.3 collective-permute-start.3
  46.9 0.0 collective-permute-done.1.refs_1_
  46.9 1.1 collective-permute-done.2.refs_2_
  48.0 1.4 collective-permute-done.3.refs_3_
  49.4 0.8 copy-done.11
  50.2 1.0 stream_copies.1
  51.1 4.9 %all-to-all-start.2 = ((bf16[32,24,512]{2,1,0:T(8,128)(2,1)}), bf16[32,24,512]{2,1,0:T(8,128)(2,1)S(1)}, u32[]{:S(2)}, u32[]{:S(2)}) async-start(bf16[32,24,512]{2,1,0:T(8,128)(2,1)} %stream_copies.1), calls=%async_computation.2 | async-start | bytes 1572864 | tf_op jit(solution)/shard_map/all_to_all | solution.py:733
  56.0 0.0 copy-start
  56.0 0.0 copy-start.8
  56.1 5.6 %plan_states.1.refs_0_ = s32[8,256]{1,0:T(8,128)S(1)} custom-call(s32[2,256]{1,0:T(2,128)S(1)} %copy-done.16), custom_call_target="tpu_custom_call" | custom-call | flops 2000000000 | bytes 1048576 | tf_op jit(solution)/shard_map/plan_states/pallas_call | solution.py:63
  61.7 0.0 copy-start.14
  61.7 0.0 copy-start.15
  61.7 4.4 %update_states.1 = bf16[8,512,128]{2,1,0:T(8,128)(2,1)} custom-call(s32[8,256]{1,0:T(8,128)S(1)} %plan_states.1.refs_0_, f32[8,512,128]{2,1,0:T(8,128)S(1)} %bitcast.13, f32[8,8,512]{2,1,0:T(8,128)S(1)} %copy-done.8, f32[8,8,512]{2,1,0:T(8,128)S(1)} %copy-done.9, f32[8,8,128]{2,1,0:T(8,128)S(1)} %copy-done.12), custom_call_target="tpu_custom_call" | custom-call | flops 33554432 | bytes 3145728 | tf_op jit(solution)/shard_map/update_states/pallas_call | solution.py:63
  66.2 0.0 copy-start.1
  66.2 0.0 copy-start.13
  66.2 2.8 %routes.1 = (bf16[384,768]{1,0:T(8,128)(2,1)S(1)}, bf16[24,768]{1,0:T(8,128)(2,1)S(1)}, bf16[4,24,1536]{2,1,0:T(8,128)(2,1)S(1)}, bf16[4,24,1536]{2,1,0:T(8,128)(2,1)S(1)}) custom-call(s32[2,256]{1,0:T(2,128)S(1)} %copy-done.16, bf16[256,128]{1,0:T(8,128)(2,1)S(1)} %copy-done.18, s32[24,8]{1,0:T(8,128)S(1)} %bitcast.18, f32[24,8]{1,0:T(8,128)S(1)} %bitcast.17), custom_call_target="tpu_custom_call" | custom-call | flops 1000000000 | bytes 1048576 | tf_op jit(solution)/shard_map/routes/pallas_call | solution.py:63
  69.1 0.0 copy-start.4
  69.1 0.7 copy-done.4
  69.8 0.7 copy-done.6
  70.5 7.6 %all-to-all-done.2 = bf16[32,24,512]{2,1,0:T(8,128)(2,1)S(1)} async-done(((bf16[32,24,512]{2,1,0:T(8,128)(2,1)}), bf16[32,24,512]{2,1,0:T(8,128)(2,1)S(1)}, u32[]{:S(2)}, u32[]{:S(2)}) %all-to-all-start.2) | async-done | bytes 786464 | tf_op jit(solution)/shard_map/all_to_all | solution.py:733
  78.1 0.0 copy-done.1
  78.1 1.6 copy-done.2
  79.7 2.1 %expand_experts.1 = (bf16[4,48,2176]{2,1,0:T(8,128)(2,1)S(1)}, bf16[4,48,2176]{2,1,0:T(8,128)(2,1)S(1)}) custom-call(bf16[384,768]{1,0:T(8,128)(2,1)S(1)} %get-tuple-element.99.refs_0_, bf16[768,512]{1,0:T(8,128)(2,1)S(1)} %bitcast.14, f32[1,512]{1,0:T(1,128)S(1)} %bitcast.16, bf16[2,512,1024]{2,1,0:T(8,128)(2,1)S(1)} %copy-done.1, ...), custom_call_target="tpu_custom_call" | custom-call | flops 1107296256 | bytes 8388608 | tf_op jit(solution)/shard_map/expand_experts/pallas_call | solution.py:63
  81.8 0.1 collective-permute-start.4
  81.9 2.3 %collective-permute-done.4.refs_1_ = bf16[4,48,2176]{2,1,0:T(8,128)(2,1)S(1)} collective-permute-done((bf16[4,48,2176]{2,1,0:T(8,128)(2,1)S(1)}, bf16[4,48,2176]{2,1,0:T(8,128)(2,1)S(1)}, u32[]{:S(2)}, u32[]{:S(2)}) %collective-permute-start.4) | collective-permute-done | bytes 835616 | tf_op jit(solution)/shard_map/ppermute | solution.py:493
  84.2 0.3 add_cores.3
  84.5 4.9 %all-to-all-start.3 = ((bf16[32,128,128]{2,1,0:T(8,128)(2,1)}), bf16[32,128,128]{2,1,0:T(8,128)(2,1)S(1)}, u32[]{:S(2)}, u32[]{:S(2)}) async-start(bf16[32,128,128]{2,1,0:T(8,128)(2,1)} %bitcast.9), calls=%async_computation.3 | async-start | bytes 2097152 | tf_op jit(solution)/shard_map/all_to_all | solution.py:733
  89.5 0.3 collective-permute-start.5
  89.7 3.6 %collective-permute-start.6 = (bf16[48,2176]{1,0:T(8,128)(2,1)S(1)}, bf16[48,2176]{1,0:T(8,128)(2,1)S(1)}, u32[]{:S(2)}, u32[]{:S(2)}) collective-permute-start(bf16[48,2176]{1,0:T(8,128)(2,1)S(1)} %get-tuple-element.111), channel_id=1, source_target_pairs={{0,4},{1,5},{2,6},{3,7},{4,0},{5,1},{6,2},{7,3},{8,12},{9,13},{10,... | collective-permute-start | bytes 626696 | tf_op jit(solution)/shard_map/ppermute | solution.py:456
  93.3 0.4 collective-permute-start.7
  93.7 4.7 %collective-permute-done.5.refs_1_ = bf16[48,2176]{1,0:T(8,128)(2,1)S(1)} collective-permute-done((bf16[48,2176]{1,0:T(8,128)(2,1)S(1)}, bf16[48,2176]{1,0:T(8,128)(2,1)S(1)}, u32[]{:S(2)}, u32[]{:S(2)}) %collective-permute-start.5) | collective-permute-done | bytes 208928 | tf_op jit(solution)/shard_map/ppermute | solution.py:456
  98.3 4.0 %collective-permute-done.6.refs_2_ = bf16[48,2176]{1,0:T(8,128)(2,1)S(1)} collective-permute-done((bf16[48,2176]{1,0:T(8,128)(2,1)S(1)}, bf16[48,2176]{1,0:T(8,128)(2,1)S(1)}, u32[]{:S(2)}, u32[]{:S(2)}) %collective-permute-start.6) | collective-permute-done | bytes 208928 | tf_op jit(solution)/shard_map/ppermute | solution.py:456
  102.4 0.1 collective-permute-done.7.refs_3_
  102.5 0.2 hidden_units.1.refs_3_
  102.7 2.7 %collective-permute-start.10 = (bf16[48,1024]{1,0:T(8,128)(2,1)S(1)}, bf16[48,1024]{1,0:T(8,128)(2,1)S(1)}, u32[]{:S(2)}, u32[]{:S(2)}) collective-permute-start(bf16[48,1024]{1,0:T(8,128)(2,1)S(1)} %hidden_units.1.refs_3_), channel_id=1, source_target_pairs={{0,6},{1,7},{2,0},{3,1},{4,2},{5,3},{6,4},{7,5},{8,14},{9,15},{10,... | collective-permute-start | bytes 294920 | tf_op jit(solution)/shard_map/ppermute | solution.py:456
  105.4 0.3 collective-permute-start.9
  105.7 0.7 collective-permute-start.8
  106.4 0.0 collective-permute-start.11
  106.4 3.4 %collective-permute-done.10.refs_6_ = bf16[48,1024]{1,0:T(8,128)(2,1)S(1)} collective-permute-done((bf16[48,1024]{1,0:T(8,128)(2,1)S(1)}, bf16[48,1024]{1,0:T(8,128)(2,1)S(1)}, u32[]{:S(2)}, u32[]{:S(2)}) %collective-permute-start.10) | collective-permute-done | bytes 98336 | tf_op jit(solution)/shard_map/ppermute | solution.py:456
  109.8 0.0 collective-permute-start.14
  109.8 2.7 %collective-permute-done.9.refs_5_ = bf16[48,1024]{1,0:T(8,128)(2,1)S(1)} collective-permute-done((bf16[48,1024]{1,0:T(8,128)(2,1)S(1)}, bf16[48,1024]{1,0:T(8,128)(2,1)S(1)}, u32[]{:S(2)}, u32[]{:S(2)}) %collective-permute-start.9) | collective-permute-done | bytes 98336 | tf_op jit(solution)/shard_map/ppermute | solution.py:456
  112.5 0.0 collective-permute-start.13
  112.5 0.7 collective-permute-done.8.refs_4_
  113.2 0.0 collective-permute-start.12
  113.2 0.0 collective-permute-done.11.refs_7_
  113.2 0.0 collective-permute-done.14.refs_10_
  113.2 0.6 collective-permute-done.13.refs_9_
  113.8 0.7 collective-permute-done.12.refs_8_
  114.5 3.8 %all-to-all-done.3.refs_1_ = bf16[32,128,128]{2,1,0:T(8,128)(2,1)S(1)} async-done(((bf16[32,128,128]{2,1,0:T(8,128)(2,1)}), bf16[32,128,128]{2,1,0:T(8,128)(2,1)S(1)}, u32[]{:S(2)}, u32[]{:S(2)}) %all-to-all-start.3) | async-done | bytes 1048608 | tf_op jit(solution)/shard_map/all_to_all | solution.py:733
  118.2 1.6 copy-done.3
  119.8 3.8 %shrink_experts.1 = bf16[32,176,128]{2,1,0:T(8,128)(2,1)S(1)} custom-call(s32[8,256]{1,0:T(8,128)S(1)} %plan_states.1.refs_0_, bf16[32,128,128]{2,1,0:T(8,128)(2,1)S(1)} %all-to-all-done.3.refs_1_, bf16[2,1024,512]{2,1,0:T(8,128)(2,1)S(1)} %copy-done.3, bf16[48,1024]{1,0:T(8,128)(2,1)S(1)} %hidden_units.1.refs_3_, ...), custom_call_target="tpu_custom_call" | custom-call | flops 805306368 | bytes 4194304 | tf_op jit(solution)/shard_map/shrink_experts/pallas_call | solution.py:63
  123.6 43.7 %all_to_all.25.refs_1_ = bf16[32,176,128]{2,1,0:T(8,128)(2,1)S(1)} all-to-all(bf16[32,176,128]{2,1,0:T(8,128)(2,1)S(1)} %shrink_experts.1), channel_id=1, replica_groups=mesh['req'=32,'head'=8] {'req'}, dimensions={0} | all-to-all | bytes 2883584 | tf_op jit(solution)/shard_map/all_to_all | solution.py:733
  167.3 2.7 %finish.1 = (bf16[24,512]{1,0:T(8,128)(2,1)}, f32[8,512,128]{2,1,0:T(8,128)}) custom-call(s32[8,256]{1,0:T(8,128)S(1)} %plan_states.1.refs_0_, bf16[32,176,128]{2,1,0:T(8,128)(2,1)S(1)} %all_to_all.25.refs_1_, bf16[4,24,1536]{2,1,0:T(8,128)(2,1)S(1)} %copy-done.5, bf16[4,24,1536]{2,1,0:T(8,128)(2,1)S(1)} %copy-done.7, ...), custom_call_target="tpu_custom_call" | custom-call | flops 100000000 | bytes 4194304 | tf_op jit(solution)/shard_map/finish/pallas_call | solution.py:63
  (22 shorter events, 0.1 us)
Async XLA Ops:
  38.5 17.6 %copy-start.16 = (s32[2,256]{1,0:T(2,128)S(1)}, s32[2,256]{1,0:T(2,128)}, u32[]{:S(2)}) copy-start(s32[2,256]{1,0:T(2,128)} %refs_0_.3) | copy-start | bytes 6148
  38.5 1.6 collective-permute-start
  40.1 0.9 copy-start.10
  41.0 5.9 %collective-permute-start.1 = (bf16[24,512]{1,0:T(8,128)(2,1)S(1)}, bf16[24,512]{1,0:T(8,128)(2,1)S(1)}, u32[]{:S(2)}, u32[]{:S(2)}) collective-permute-start(bf16[24,512]{1,0:T(8,128)(2,1)S(1)} %get-tuple-element.81), channel_id=1, source_target_pairs={{0,2},{1,3},{2,4},{3,5},{4,6},{5,7},{6,0},{7,1},{8,10},{9,11},{10,... | collective-permute-start | bytes 73736 | tf_op jit(solution)/shard_map/ppermute | solution.py:456
  42.7 5.3 %collective-permute-start.2 = (bf16[24,512]{1,0:T(8,128)(2,1)S(1)}, bf16[24,512]{1,0:T(8,128)(2,1)S(1)}, u32[]{:S(2)}, u32[]{:S(2)}) collective-permute-start(bf16[24,512]{1,0:T(8,128)(2,1)S(1)} %get-tuple-element.82), channel_id=1, source_target_pairs={{0,4},{1,5},{2,6},{3,7},{4,0},{5,1},{6,2},{7,3},{8,12},{9,13},{10,... | collective-permute-start | bytes 73736 | tf_op jit(solution)/shard_map/ppermute | solution.py:456
  45.6 3.8 %collective-permute-start.3 = (bf16[24,512]{1,0:T(8,128)(2,1)S(1)}, bf16[24,512]{1,0:T(8,128)(2,1)S(1)}, u32[]{:S(2)}, u32[]{:S(2)}) collective-permute-start(bf16[24,512]{1,0:T(8,128)(2,1)S(1)} %get-tuple-element.83), channel_id=1, source_target_pairs={{0,6},{1,7},{2,0},{3,1},{4,2},{5,3},{6,4},{7,5},{8,14},{9,15},{10,... | collective-permute-start | bytes 73736 | tf_op jit(solution)/shard_map/ppermute | solution.py:456
  49.4 0.8 copy-start.11
  51.1 26.9 %all-to-all-start.2 = ((bf16[32,24,512]{2,1,0:T(8,128)(2,1)}), bf16[32,24,512]{2,1,0:T(8,128)(2,1)S(1)}, u32[]{:S(2)}, u32[]{:S(2)}) async-start(bf16[32,24,512]{2,1,0:T(8,128)(2,1)} %stream_copies.1), calls=%async_computation.2 | async-start | bytes 1572864 | tf_op jit(solution)/shard_map/all_to_all | solution.py:733
  56.0 5.6 %copy-start = (f32[8,8,64,128]{3,2,1,0:T(8,128)S(1)}, f32[8,8,64,128]{3,2,1,0:T(8,128)}, u32[]{:S(2)}) copy-start(f32[8,8,64,128]{3,2,1,0:T(8,128)} %param.20) | copy-start | bytes 6291460
  56.0 5.6 %copy-start.8 = (f32[8,8,512]{2,1,0:T(8,128)S(1)}, f32[8,8,512]{2,1,0:T(8,128)}, u32[]{:S(2)}) copy-start(f32[8,8,512]{2,1,0:T(8,128)} %get-tuple-element.91.refs_2_) | copy-start | bytes 393220
  56.1 5.6 %copy-start.9 = (f32[8,8,512]{2,1,0:T(8,128)S(1)}, f32[8,8,512]{2,1,0:T(8,128)}, u32[]{:S(2)}) copy-start(f32[8,8,512]{2,1,0:T(8,128)} %get-tuple-element.92.refs_3_) | copy-start | bytes 393220
  56.1 5.6 %copy-start.12 = (f32[8,8,128]{2,1,0:T(8,128)S(1)}, f32[8,8,128]{2,1,0:T(8,128)}, u32[]{:S(2)}) copy-start(f32[8,8,128]{2,1,0:T(8,128)} %get-tuple-element.93.refs_4_) | copy-start | bytes 98308
  61.7 4.5 %copy-start.14 = (f32[3,8,8]{2,1,0:T(8,128)S(1)}, f32[3,8,8]{2,1,0:T(8,128)}, u32[]{:S(2)}) copy-start(f32[3,8,8]{2,1,0:T(8,128)} %param.33) | copy-start | bytes 2308
  61.7 4.5 %copy-start.15 = (s32[3,8,8]{2,1,0:T(8,128)S(1)}, s32[3,8,8]{2,1,0:T(8,128)}, u32[]{:S(2)}) copy-start(s32[3,8,8]{2,1,0:T(8,128)} %refs_7_.2) | copy-start | bytes 2308
  61.7 4.5 %copy-start.18 = (bf16[256,128]{1,0:T(8,128)(2,1)S(1)}, bf16[256,128]{1,0:T(8,128)(2,1)}, u32[]{:S(2)}) copy-start(bf16[256,128]{1,0:T(8,128)(2,1)} %get-tuple-element.94.refs_1_) | copy-start | bytes 196612
  66.2 11.9 %copy-start.1 = (bf16[2,512,1024]{2,1,0:T(8,128)(2,1)S(1)}, bf16[2,512,1024]{2,1,0:T(8,128)(2,1)}, u32[]{:S(2)}) copy-start(bf16[2,512,1024]{2,1,0:T(8,128)(2,1)} %refs_3_.5) | copy-start | bytes 6291460
  66.2 11.9 %copy-start.13 = (f32[512]{0:T(512)S(1)}, f32[512]{0:T(512)}, u32[]{:S(2)}) copy-start(f32[512]{0:T(512)} %param.31) | copy-start | bytes 6148
  69.1 0.7 copy-start.4
  69.8 0.7 copy-start.6
  78.1 1.6 copy-start.2
  81.8 2.4 %collective-permute-start.4 = (bf16[4,48,2176]{2,1,0:T(8,128)(2,1)S(1)}, bf16[4,48,2176]{2,1,0:T(8,128)(2,1)S(1)}, u32[]{:S(2)}, u32[]{:S(2)}) collective-permute-start(bf16[4,48,2176]{2,1,0:T(8,128)(2,1)S(1)} %get-tuple-element.102), channel_id=1, source_target_pairs={{0,1},{1,0},{2,3},{3,2},{4,5},{5,4},{6,7},{7,6},{8,9},{9,8},{10,11... | collective-permute-start | bytes 2506760 | tf_op jit(solution)/shard_map/ppermute | solution.py:493
  84.5 33.7 %all-to-all-start.3 = ((bf16[32,128,128]{2,1,0:T(8,128)(2,1)}), bf16[32,128,128]{2,1,0:T(8,128)(2,1)S(1)}, u32[]{:S(2)}, u32[]{:S(2)}) async-start(bf16[32,128,128]{2,1,0:T(8,128)(2,1)} %bitcast.9), calls=%async_computation.3 | async-start | bytes 2097152 | tf_op jit(solution)/shard_map/all_to_all | solution.py:733
  89.5 8.9 %collective-permute-start.5 = (bf16[48,2176]{1,0:T(8,128)(2,1)S(1)}, bf16[48,2176]{1,0:T(8,128)(2,1)S(1)}, u32[]{:S(2)}, u32[]{:S(2)}) collective-permute-start(bf16[48,2176]{1,0:T(8,128)(2,1)S(1)} %get-tuple-element.110), channel_id=1, source_target_pairs={{0,2},{1,3},{2,4},{3,5},{4,6},{5,7},{6,0},{7,1},{8,10},{9,11},{10,... | collective-permute-start | bytes 626696 | tf_op jit(solution)/shard_map/ppermute | solution.py:456
  89.7 12.7 %collective-permute-start.6 = (bf16[48,2176]{1,0:T(8,128)(2,1)S(1)}, bf16[48,2176]{1,0:T(8,128)(2,1)S(1)}, u32[]{:S(2)}, u32[]{:S(2)}) collective-permute-start(bf16[48,2176]{1,0:T(8,128)(2,1)S(1)} %get-tuple-element.111), channel_id=1, source_target_pairs={{0,4},{1,5},{2,6},{3,7},{4,0},{5,1},{6,2},{7,3},{8,12},{9,13},{10,... | collective-permute-start | bytes 626696 | tf_op jit(solution)/shard_map/ppermute | solution.py:456
  93.3 9.2 %collective-permute-start.7 = (bf16[48,2176]{1,0:T(8,128)(2,1)S(1)}, bf16[48,2176]{1,0:T(8,128)(2,1)S(1)}, u32[]{:S(2)}, u32[]{:S(2)}) collective-permute-start(bf16[48,2176]{1,0:T(8,128)(2,1)S(1)} %get-tuple-element.112), channel_id=1, source_target_pairs={{0,6},{1,7},{2,0},{3,1},{4,2},{5,3},{6,4},{7,5},{8,14},{9,15},{10,... | collective-permute-start | bytes 626696 | tf_op jit(solution)/shard_map/ppermute | solution.py:456
  102.7 7.1 %collective-permute-start.10 = (bf16[48,1024]{1,0:T(8,128)(2,1)S(1)}, bf16[48,1024]{1,0:T(8,128)(2,1)S(1)}, u32[]{:S(2)}, u32[]{:S(2)}) collective-permute-start(bf16[48,1024]{1,0:T(8,128)(2,1)S(1)} %hidden_units.1.refs_3_), channel_id=1, source_target_pairs={{0,6},{1,7},{2,0},{3,1},{4,2},{5,3},{6,4},{7,5},{8,14},{9,15},{10,... | collective-permute-start | bytes 294920 | tf_op jit(solution)/shard_map/ppermute | solution.py:456
  105.4 7.1 %collective-permute-start.9 = (bf16[48,1024]{1,0:T(8,128)(2,1)S(1)}, bf16[48,1024]{1,0:T(8,128)(2,1)S(1)}, u32[]{:S(2)}, u32[]{:S(2)}) collective-permute-start(bf16[48,1024]{1,0:T(8,128)(2,1)S(1)} %hidden_units.1.refs_3_), channel_id=1, source_target_pairs={{0,4},{1,5},{2,6},{3,7},{4,0},{5,1},{6,2},{7,3},{8,12},{9,13},{10,... | collective-permute-start | bytes 294920 | tf_op jit(solution)/shard_map/ppermute | solution.py:456
  105.7 7.5 %collective-permute-start.8 = (bf16[48,1024]{1,0:T(8,128)(2,1)S(1)}, bf16[48,1024]{1,0:T(8,128)(2,1)S(1)}, u32[]{:S(2)}, u32[]{:S(2)}) collective-permute-start(bf16[48,1024]{1,0:T(8,128)(2,1)S(1)} %hidden_units.1.refs_3_), channel_id=1, source_target_pairs={{0,2},{1,3},{2,4},{3,5},{4,6},{5,7},{6,0},{7,1},{8,10},{9,11},{10,... | collective-permute-start | bytes 294920 | tf_op jit(solution)/shard_map/ppermute | solution.py:456
  106.4 6.8 %collective-permute-start.11 = (bf16[48,1024]{1,0:T(8,128)(2,1)S(1)}, bf16[48,1024]{1,0:T(8,128)(2,1)S(1)}, u32[]{:S(2)}, u32[]{:S(2)}) collective-permute-start(bf16[48,1024]{1,0:T(8,128)(2,1)S(1)} %hidden_units.1.refs_3_), channel_id=1, source_target_pairs={{0,1},{1,0},{2,3},{3,2},{4,5},{5,4},{6,7},{7,6},{8,9},{9,8},{10,11... | collective-permute-start | bytes 294920 | tf_op jit(solution)/shard_map/ppermute | solution.py:774
  109.8 3.4 %collective-permute-start.14 = (bf16[48,1024]{1,0:T(8,128)(2,1)S(1)}, bf16[48,1024]{1,0:T(8,128)(2,1)S(1)}, u32[]{:S(2)}, u32[]{:S(2)}) collective-permute-start(bf16[48,1024]{1,0:T(8,128)(2,1)S(1)} %collective-permute-done.10.refs_6_), channel_id=1, source_target_pairs={{0,1},{1,0},{2,3},{3,2},{4,5},{5,4},{6,7},{7,6},{8,9},{9,8},{10,11... | collective-permute-start | bytes 294920 | tf_op jit(solution)/shard_map/ppermute | solution.py:774
  112.5 1.3 collective-permute-start.13
  113.2 1.3 collective-permute-start.12
  118.2 1.6 copy-start.3
  123.6 43.7 %copy-start.5 = (bf16[4,24,1536]{2,1,0:T(8,128)(2,1)S(1)}, bf16[4,24,1536]{2,1,0:T(8,128)(2,1)}, u32[]{:S(2)}) copy-start(bf16[4,24,1536]{2,1,0:T(8,128)(2,1)} %copy-done.4) | copy-start | bytes 884740
  123.6 43.7 %copy-start.7 = (bf16[4,24,1536]{2,1,0:T(8,128)(2,1)S(1)}, bf16[4,24,1536]{2,1,0:T(8,128)(2,1)}, u32[]{:S(2)}) copy-start(bf16[4,24,1536]{2,1,0:T(8,128)(2,1)} %copy-done.6) | copy-start | bytes 884740

commit v4 on v3

--- a/solution.py
+++ b/solution.py
@@ -402,7 +402,7 @@
         pltpu.VMEM((ROWS, WIDTH), F32),
     ]
     args = [(got, "v"), (state, "l")] + [(array, "h") for array in arrays[:-1]] + [(arrays[-1], "l")]
-    return run_kernel(mamba_kernel, args, outs, "mamba_steps", scratch, 2 * 24 * 512 * 4096, 8 * 2**20, limit=54)
+    return run_kernel(mamba_kernel, args, outs, "mamba_steps", scratch, 2 * 24 * 512 * 4096, 8 * 2**20, limit=50)
 
 
 def update_kernel(ins, outs, scratch, wait):
@@ -451,6 +451,15 @@
 CORES = [(i, i ^ 1) for i in range(HEADS)]
 
 
+LINE = 8
+LINES = OWNERS // LINE
+
+
+def along_x(value, distance):
+    moves = [(i, ((i // LINE + distance) % LINES) * LINE + i % LINE) for i in range(OWNERS)]
+    return lax.ppermute(value, "req", moves)
+
+
 def along_y(value, distance):
     moves = [(i, ((i // 2 + distance) % 4) * 2 + i % 2) for i in range(HEADS)]
     return lax.ppermute(value, "head", moves)
@@ -511,7 +520,7 @@
 
 def stream_copies(parts, residual):
     args = [(part, "v") for part in parts] + [(residual, "v")]
-    return run_kernel(stream_kernel, args, [shaped((OWNERS, ROWS, WIDTH), BF16)], "stream_copies")[0]
+    return run_kernel(stream_kernel, args, [shaped((LINE, ROWS, WIDTH), BF16)], "stream_copies")[0]
 
 
 def routes_kernel(ins, outs, scratch, wait):
@@ -533,7 +542,8 @@
     for step in range(STEPS):
         shape = (REQUESTS, total_rows)
         g = iota(shape, 0)
-        spread.append(hot(iota(shape, 1) == (g >> 3) * ROWS + step * SLOTS + (g & 7)))
+        source = (((me >> 3) - (g >> 6)) & 3) * LINE + ((g >> 3) & 7)
+        spread.append(hot(iota(shape, 1) == source * ROWS + step * SLOTS + (g & 7)))
     at_row = jnp.zeros((8, total_rows), F32)
     for step in range(STEPS):
         wide = jnp.broadcast_to(slots[step], (8, REQUESTS)).astype(F32).astype(BF16)
@@ -584,14 +594,12 @@
         (spot % 6) // 2 == iota((ROWS, span), 0) // SLOTS
     )
     for value, out_ref in zip(split_pair(weight), (high_ref, low_ref)):
-        value = jnp.where(fits, contract(value, to_place), 0.0)
-        for piece in range(4):
-            out_ref[piece] = jnp.where(spot // 12 == piece, value, 0.0).astype(BF16)
+        out_ref[...] = jnp.where(fits, contract(value, to_place), 0.0).astype(BF16)
 
 
 def routes(dest, all_ids, ids, weights):
     total_rows = OWNERS * ROWS
-    mixing = shaped((4, ROWS, OWNERS * CHUNK), BF16)
+    mixing = shaped((ROWS, OWNERS * CHUNK), BF16)
     outs = [
         shaped((2 * OWNERS * STEPS * CAP, total_rows), BF16),
         shaped((ROWS, total_rows), BF16),
@@ -603,17 +611,25 @@
 
 
 def expand_kernel(ins, outs, scratch, wait):
-    pick_ref, stream_ref, gain_ref, gate_ref, up_ref = ins
-    keep_ref, send_ref = outs
+    pick_ref, kept_ref, *stream_refs, gain_ref, gate_ref, up_ref = ins
+    keep_ref, send_ref, own_ref = outs
+
+    def choose(rows):
+        total = 0.0
+        for line, ref in enumerate(stream_refs):
+            total = total + contract(rows[:, line * LINE * ROWS : (line + 1) * LINE * ROWS], ref[...])
+        return total
+
+    own_ref[...] = choose(kept_ref[...]).astype(BF16)
     half = pick_ref.shape[0] // 2
     some = CHUNK // 2
     for expert in range(2):
-        picked = contract(pick_ref[expert * half : (expert + 1) * half, :], stream_ref[...])
+        picked = choose(pick_ref[expert * half : (expert + 1) * half, :])
         tail = pair_lanes(jnp.sum(picked * picked, axis=1, keepdims=True))
         scaled = (picked * gain_ref[...]).astype(BF16)
         if expert == 0:
-            wait(3)
-            wait(4)
+            wait(7)
+            wait(8)
         values = [
             contract(scaled, gate_ref[expert]).astype(BF16),
             contract(scaled, up_ref[expert]).astype(BF16),
@@ -627,11 +643,12 @@
                 out_ref[turn % 4, rows, start : start + value.shape[1]] = value[source, :]
 
 
-def expand(pick, stream, gain, gate_weight, up_weight):
+def expand(pick, kept, streams, gain, gate_weight, up_weight):
     part = shaped((4, CHUNK, TERMS), BF16)
-    args = [(pick, "h"), (stream, "v"), (gain, "h"), (gate_weight, "l"), (up_weight, "l")]
+    args = [(pick, "h"), (kept, "h")] + [(stream, "v") for stream in streams]
+    args += [(gain, "h"), (gate_weight, "l"), (up_weight, "l")]
     return run_kernel(
-        expand_kernel, args, [part, part], "expand_experts", flops=2 * 384 * 512 * (2048 + 768), moved=8 * 2**20
+        expand_kernel, args, [part, part, shaped((ROWS, WIDTH), BF16)], "expand_experts", flops=2 * 384 * 512 * (2048 + 768), moved=8 * 2**20
     )
 
 
@@ -690,12 +707,12 @@
     outs = [shaped((OWNERS, CHUNK + 2 * HSIZE, 128), BF16)]
     return run_kernel(
         shrink_kernel, args, outs, "shrink_experts", [pltpu.SemaphoreType.DMA((OWNERS,))],
-        2 * 2 * 384 * 1024 * 512, 4 * 2**20,
+        2 * 2 * 384 * 1024 * 512, 4 * 2**20, limit=56,
     )[0]
 
 
 def finish_kernel(ins, outs, scratch, wait):
-    table_ref, back_ref, high_ref, low_ref, kept_ref, stream_ref = ins
+    table_ref, back_ref, high_ref, low_ref, stream_ref = ins
     mixed_ref, states_any = outs
     made_ref, sems = scratch
     first = lax.axis_index("req") * SLOTS
@@ -709,19 +726,22 @@
         store.start()
         stores.append(store)
     served = back_ref[:, 0:CHUNK, :].reshape(OWNERS * CHUNK, 128)
-    for ref in (2, 3, 4, 5):
+    for ref in (2, 3, 4):
         wait(ref)
-    stream = contract(kept_ref[...], stream_ref[...])
+    stream = stream_ref[...].astype(F32)
+    high, low = high_ref[...].astype(F32), low_ref[...].astype(F32)
     for piece in range(4):
         columns = slice(piece * 128, (piece + 1) * 128)
-        mixed = contract(high_ref[piece], served) + contract(low_ref[piece], served)
+        here = iota((ROWS, OWNERS * CHUNK), 1) % CHUNK // 12 == piece
+        mixed = contract(jnp.where(here, high, 0.0).astype(BF16), served)
+        mixed = mixed + contract(jnp.where(here, low, 0.0).astype(BF16), served)
         mixed_ref[:, columns] = (stream[:, columns] + mixed).astype(BF16)
     for store in stores:
         store.wait()
 
 
-def finish(table, back, high, low, kept, streams):
-    args = [(table, "s"), (back, "v"), (high, "l"), (low, "l"), (kept, "l"), (streams, "l")]
+def finish(table, back, high, low, stream):
+    args = [(table, "s"), (back, "v"), (high, "l"), (low, "l"), (stream, "l")]
     outs = [shaped((ROWS, WIDTH), BF16), shaped((SLOTS, HEADS * HSIZE, NSTATE), F32)]
     scratch = [pltpu.VMEM((SLOTS, HEADS * HSIZE, NSTATE), F32), pltpu.SemaphoreType.DMA((SLOTS,))]
     return run_kernel(
@@ -745,26 +765,31 @@
 
     def few(message):
         scratch = [pltpu.VMEM((OWNERS, SLOTS, 128), F32)]
-        return take(take_few_kernel, dest, exchange(message), scratch)
+        got, table = fence((exchange(message), routing_tables(dest)))
+        return take(take_few_kernel, dest, got, scratch) + (table,)
 
     def every(_):
         scratch = [pltpu.VMEM((SLOTS, MESSAGE, 128), F32), pltpu.VMEM((SLOTS, 16, 128), F32)]
-        return take(take_all_kernel, dest, exchange(pack_all(dest, *own, route_ids)), scratch)
-
-    rows, all_ids = lax.cond(most[0, 0] <= SPARE, few, every, message)
+        got, table = fence((exchange(pack_all(dest, *own, route_ids)), routing_tables(dest)))
+        return take(take_all_kernel, dest, got, scratch) + (table,)
+
+    rows, all_ids, table = lax.cond(most[0, 0] <= SPARE, few, every, message)
 
     keep_part, send_part, home_residual, *factors = mamba(
         rows, state_rows, *own, decay_rate[None], skip_gain[None], ssm_gain[None], out_weight
     )
     parts, _ = scatter_sum(keep_part, send_part, False)
     copies, later_dest, all_ids, factors = fence((stream_copies(parts, home_residual), dest, all_ids, factors))
-    streams = exchange(copies).reshape(OWNERS * ROWS, WIDTH)
-    table = routing_tables(later_dest)
+    lines = [[line * LINE + place for place in range(LINE)] for line in range(LINES)]
+    line = lax.all_to_all(
+        copies, "req", split_axis=0, concat_axis=0, axis_index_groups=lines, tiled=True
+    ).reshape(LINE * ROWS, WIDTH)
+    streams = [line, along_x(line, 1), along_x(line, 2), along_x(line, 3)]
     routed = routes(later_dest, all_ids, route_ids.reshape(ROWS, 8), route_weights.reshape(ROWS, 8))
     pieces = update_states(table, state_rows, factors)
     streams, pieces, (pick, kept, high, low) = fence((streams, pieces, routed))
 
-    keep_part, send_part = expand(pick, streams, ffn_gain[None], gate_weight, up_weight)
+    keep_part, send_part, own_stream = expand(pick, kept, streams, ffn_gain[None], gate_weight, up_weight)
     parts, pieces = scatter_sum(keep_part, send_part, True, pieces.reshape(OWNERS, 2 * HSIZE, NSTATE))
     hidden = hidden_units(parts)
     far = along_y(hidden, 2)
@@ -773,7 +798,7 @@
     blocks = [hidden, near, far, other]
     blocks = blocks + [lax.ppermute(block, "head", CORES) for block in blocks]
     back = exchange(shrink(table, pieces, blocks, down_weight))
-    mixed, final_states = finish(table, back, high, low, kept, streams)
+    mixed, final_states = finish(table, back, high, low, own_stream)
     return mixed.reshape(STEPS, SLOTS, WIDTH), final_states.reshape(states.shape)
 
 

time: 171 us -> 165 us (0.965)
  blocking collectives: 72.3 us -> 56.5 us
  starting transfers between devices: 23.8 us -> 33.8 us
  local copies, waits for them, and re-layouts: 6.35 us -> 1.09 us
  waiting for transfers between devices: 34.6 us -> 38.8 us
    all_to_all x2 -> x1, blocking collectives: 72.3 us -> 44.4 us  [exchange(): return lax.all_to_all(value, 'req', split_axis=0, concat_axis=0, tiled=True)]
    all_to_all x0 -> x1, blocking collectives: none -> 12.1 us  [shards(): lax.all_to_all(copies, 'req', split_axis=0, concat_axis=0, axis_index_gro...]
    all_to_all x2, starting transfers between devices: 9.81 us -> 17.1 us  [exchange(): return lax.all_to_all(value, 'req', split_axis=0, concat_axis=0, tiled=True)]
    unnamed x36 -> x38, local copies, waits for them, and re-layouts: 6.35 us -> 1.08 us
    all_to_all x2, waiting for transfers between devices: 11.4 us -> 15 us  [exchange(): return lax.all_to_all(value, 'req', split_axis=0, concat_axis=0, tiled=True)]
    ppermute x0 -> x3, starting transfers between devices: none -> 2.8 us  [along_x(): return lax.ppermute(value, 'req', moves)]
  transfers between devices with their start and end apart: 17 -> 20, of which waited for: 14 -> 14; matrix products, arithmetic and copies ran while one was open for 0% -> 0% of each run, Pallas kernels for 8% -> 8%
where the time goes in v4:
time: 165 us; the launch traced here: 164 us
  blocking collectives  56.5 us (34%)
  waiting for transfers between devices  38.8 us (24%)
  starting transfers between devices  33.8 us (20%)
  Pallas kernels  32.1 us (19%)
  between operations  1.79 us (1%)
    all_to_all x1, blocking collectives, exchange(): return lax.all_to_all(value, 'req', split_axis=0, concat_axis=0, tiled=True)  44.4 us
    pallas_call x13, Pallas kernels, run_kernel(): pl.pallas_call(kernel, out_shape=tuple(outs), in_specs=[VMEM_SPEC if mode...  32.1 us
    ppermute x9, waiting for transfers between devices, along_y(): return lax.ppermute(value, 'head', moves)  18.4 us
    all_to_all x2, starting transfers between devices, exchange(): return lax.all_to_all(value, 'req', split_axis=0, concat_axis=0, tiled=True)  17.1 us
    all_to_all x2, waiting for transfers between devices, exchange(): return lax.all_to_all(value, 'req', split_axis=0, concat_axis=0, tiled=True)  15 us
    ppermute x9, starting transfers between devices, along_y(): return lax.ppermute(value, 'head', moves)  13.5 us
    all_to_all x1, blocking collectives, shards(): lax.all_to_all(copies, 'req', split_axis=0, concat_axis=0, axis_index_gro...  12.1 us
    ppermute x2, waiting for transfers between devices, scatter_sum(): got = lax.ppermute(send, 'head', CORES)  3.63 us
  transfers between devices with their start and end apart: 20, of which 14 were waited for; matrix products, arithmetic and copies ran while one was open for 0% of the time, Pallas kernels for 8%

profile of v4, /device:TPU:32, one launch (start us, length us, event | category | flops | bytes accessed | tf_op | source)
XLA Modules:
  0.0 164.2 jit_solution(10968767379849137172)
XLA Ops:
  0.6 3.2 %pack_few.1 = (bf16[32,64,128]{2,1,0:T(8,128)(2,1)}, s32[1,1]{1,0:T(1,128)}) custom-call(s32[2,256]{1,0:T(2,128)} %refs_0_.2, bf16[3,8,512]{2,1,0:T(8,128)(2,1)} %refs_2_.4, bf16[3,8,512]{2,1,0:T(8,128)(2,1)} %refs_3_.3, bf16[3,8,4096]{2,1,0:T(8,128)(2,1)} %refs_4_.3, bf16[3,8,128]{2,1,0:T(8,128)(2,1)} %refs_5_.3, bf16[3,8,128]{2,1,0:T(8,128)(2,1)} %refs_6_.3, ...), custom_call_target="tpu_custom_call" | custom-call | bytes 1048576 | tf_op jit(solution)/shard_map/pack_few/pallas_call | solution.py:63
  4.5 0.0 copy-start
  4.5 0.0 copy-start.4
  4.5 0.0 copy-start.6
  4.5 0.0 copy-start.7
  4.5 29.8 %conditional.1 = (bf16[8,32,128]{2,1,0:T(8,128)(2,1)S(1)}, bf16[256,128]{1,0:T(8,128)(2,1)S(1)}, s32[8,256]{1,0:T(8,128)S(1)}) conditional(s32[]{:T(128)} %bitcast, (s32[2,256]{1,0:T(2,128)}, bf16[3,8,512]{2,1,0:T(8,128)(2,1)}, bf16[3,8,512]{2,1,0:T(8,128)(2,1)}, bf16[3,8,4096]{2,1,0:T(8,128)(2,1)}, bf16[3,8,128]{2,1,0:T(8,128)(2,1)}, ...), branch_computations={%region_0.0_spmd, %region_1.0_spmd} | conditional | flops 2000000000 | bytes 6692948 | solution.py:776
  4.5 11.3 %all-to-all-start.1 = ((bf16[32,64,128]{2,1,0:T(8,128)(2,1)}), bf16[32,64,128]{2,1,0:T(8,128)(2,1)S(1)}, u32[]{:S(2)}, u32[]{:S(2)}) async-start(bf16[32,64,128]{2,1,0:T(8,128)(2,1)} %get-tuple-element.33), calls=%async_computation.1 | async-start | bytes 1048576 | tf_op jit(solution)/shard_map/cond/branch_1_fun/all_to_all | solution.py:753
  15.9 0.0 copy-start.20
  15.9 6.3 %plan_states.3 = s32[8,256]{1,0:T(8,128)S(1)} custom-call(s32[2,256]{1,0:T(2,128)} %get-tuple-element.32.refs_0_), custom_call_target="tpu_custom_call" | custom-call | flops 2000000000 | bytes 1048576 | tf_op jit(solution)/shard_map/cond/branch_1_fun/plan_states/pallas_call | solution.py:63
  22.2 11.3 %all-to-all-done.1.refs_1_ = bf16[32,64,128]{2,1,0:T(8,128)(2,1)S(1)} async-done(((bf16[32,64,128]{2,1,0:T(8,128)(2,1)}), bf16[32,64,128]{2,1,0:T(8,128)(2,1)S(1)}, u32[]{:S(2)}, u32[]{:S(2)}) %all-to-all-start.1) | async-done | bytes 524320 | tf_op jit(solution)/shard_map/cond/branch_1_fun/all_to_all | solution.py:753
  33.5 0.8 take_rows.3
  34.4 3.5 %mamba_steps.1 = (bf16[4,24,512]{2,1,0:T(8,128)(2,1)S(1)}, bf16[4,24,512]{2,1,0:T(8,128)(2,1)S(1)}, f32[24,512]{1,0:T(8,128)S(1)}, f32[8,8,512]{2,1,0:T(8,128)S(...) custom-call(bf16[8,32,128]{2,1,0:T(8,128)(2,1)S(1)} %get-tuple-element.91.refs_0_, f32[8,512,128]{2,1,0:T(8,128)S(1)} %bitcast.12, ...), custom_call_target="tpu_custom_call" | custom-call | flops 100663296 | bytes 8388608 | tf_op jit(solution)/shard_map/mamba_steps/pallas_call | solution.py:63
  37.9 0.3 collective-permute-start
  38.1 1.3 collective-permute-done.refs_1_
  39.5 1.7 %collective-permute-start.1 = (bf16[24,512]{1,0:T(8,128)(2,1)S(1)}, bf16[24,512]{1,0:T(8,128)(2,1)S(1)}, u32[]{:S(2)}, u32[]{:S(2)}) collective-permute-start(bf16[24,512]{1,0:T(8,128)(2,1)S(1)} %get-tuple-element.95), channel_id=1, source_target_pairs={{0,2},{1,3},{2,4},{3,5},{4,6},{5,7},{6,0},{7,1},{8,10},{9,11},{10,... | collective-permute-start | bytes 73736 | tf_op jit(solution)/shard_map/ppermute | solution.py:465
  41.1 2.9 %collective-permute-start.2 = (bf16[24,512]{1,0:T(8,128)(2,1)S(1)}, bf16[24,512]{1,0:T(8,128)(2,1)S(1)}, u32[]{:S(2)}, u32[]{:S(2)}) collective-permute-start(bf16[24,512]{1,0:T(8,128)(2,1)S(1)} %get-tuple-element.96), channel_id=1, source_target_pairs={{0,4},{1,5},{2,6},{3,7},{4,0},{5,1},{6,2},{7,3},{8,12},{9,13},{10,... | collective-permute-start | bytes 73736 | tf_op jit(solution)/shard_map/ppermute | solution.py:465
  44.0 1.3 collective-permute-start.3
  45.4 0.0 collective-permute-done.1.refs_1_
  45.4 1.1 collective-permute-done.2.refs_2_
  46.4 1.4 collective-permute-done.3.refs_3_
  47.9 12.1 %all_to_all.23 = bf16[8,24,512]{2,1,0:T(8,128)(2,1)S(1)} all-to-all(bf16[8,24,512]{2,1,0:T(8,128)(2,1)S(1)} %stream_copies.1), channel_id=1, replica_groups={{0,8,16,24,32,40,48,56},{64,72,80,88,96,104,112,120},{128,136,144,152,1..., dimensions={0} | all-to-all | bytes 393216 | tf_op jit(solution)/shard_map/all_to_all | solution.py:784
  60.0 1.1 collective-permute-start.6
  61.1 1.5 collective-permute-start.5
  62.7 0.1 collective-permute-start.4
  62.8 4.4 %update_states.1 = bf16[8,512,128]{2,1,0:T(8,128)(2,1)} custom-call(s32[8,256]{1,0:T(8,128)S(1)} %get-tuple-element.90.refs_0_, f32[8,512,128]{2,1,0:T(8,128)S(1)} %bitcast.13, f32[8,8,512]{2,1,0:T(8,128)S(1)} %get-tuple-element.104.refs_2_, f32[8,8,512]{2,1,0:T(8,128)S(1)} %get-tuple-element.105.refs_3_, f32[8,8,128]{2,1,0:T(8,128)S(1)} %get-tuple-element.106.refs_4_), custom_call_target="tpu_custom_call" | custom-call | flops 33554432 | bytes 3145728 | tf_op jit(solution)/shard_map/update_states/pallas_call | solution.py:63
  67.3 0.0 copy-start.1
  67.3 0.0 copy-start.5
  67.3 2.8 %routes.1 = (bf16[384,768]{1,0:T(8,128)(2,1)S(1)}, bf16[24,768]{1,0:T(8,128)(2,1)S(1)}, bf16[24,1536]{1,0:T(8,128)(2,1)S(1)}, bf16[24,1536]{1,0:T(8,128)(2,1)S(1)}) custom-call(s32[2,256]{1,0:T(2,128)S(1)} %copy-done.18, bf16[256,128]{1,0:T(8,128)(2,1)S(1)} %get-tuple-element.108.refs_1_, s32[24,8]{1,0:T(8,128)S(1)} %bitcast.23, f32[24,8]{1,0:T(8,128)S(1)} %bitcast.22), custom_call_target="tpu_custom_call" | custom-call | flops 1000000000 | bytes 1048576 | tf_op jit(solution)/shard_map/routes/pallas_call | solution.py:63
  70.1 0.0 collective-permute-done.6.refs_5_
  70.1 0.0 collective-permute-done.5.refs_4_
  70.1 0.5 collective-permute-done.4.refs_3_
  70.6 0.0 copy-done.1
  70.6 2.4 %expand_experts.1 = (bf16[4,48,2176]{2,1,0:T(8,128)(2,1)S(1)}, bf16[4,48,2176]{2,1,0:T(8,128)(2,1)S(1)}, bf16[24,512]{1,0:T(8,128)(2,1)S(1)}) custom-call(bf16[384,768]{1,0:T(8,128)(2,1)S(1)} %get-tuple-element.113.refs_0_, bf16[24,768]{1,0:T(8,128)(2,1)S(1)} %get-tuple-element.114.refs_1_, bf16[192,512]{1,0:T(8,128)(2,1)S(1)} %bitcast.17, ...), custom_call_target="tpu_custom_call" | custom-call | flops 1107296256 | bytes 8388608 | tf_op jit(solution)/shard_map/expand_experts/pallas_call | solution.py:63
  73.1 0.1 collective-permute-start.7
  73.2 2.3 %collective-permute-done.7.refs_1_ = bf16[4,48,2176]{2,1,0:T(8,128)(2,1)S(1)} collective-permute-done((bf16[4,48,2176]{2,1,0:T(8,128)(2,1)S(1)}, bf16[4,48,2176]{2,1,0:T(8,128)(2,1)S(1)}, u32[]{:S(2)}, u32[]{:S(2)}) %collective-permute-start.7) | collective-permute-done | bytes 835616 | tf_op jit(solution)/shard_map/ppermute | solution.py:502
  75.5 0.3 add_cores.3
  75.8 5.8 %all-to-all-start.3 = ((bf16[32,128,128]{2,1,0:T(8,128)(2,1)}), bf16[32,128,128]{2,1,0:T(8,128)(2,1)S(1)}, u32[]{:S(2)}, u32[]{:S(2)}) async-start(bf16[32,128,128]{2,1,0:T(8,128)(2,1)} %bitcast.9), calls=%async_computation.3 | async-start | bytes 2097152 | tf_op jit(solution)/shard_map/all_to_all | solution.py:753
  81.6 0.1 collective-permute-start.8
  81.8 4.0 %collective-permute-start.9 = (bf16[48,2176]{1,0:T(8,128)(2,1)S(1)}, bf16[48,2176]{1,0:T(8,128)(2,1)S(1)}, u32[]{:S(2)}, u32[]{:S(2)}) collective-permute-start(bf16[48,2176]{1,0:T(8,128)(2,1)S(1)} %get-tuple-element.129), channel_id=1, source_target_pairs={{0,4},{1,5},{2,6},{3,7},{4,0},{5,1},{6,2},{7,3},{8,12},{9,13},{10,... | collective-permute-start | bytes 626696 | tf_op jit(solution)/shard_map/ppermute | solution.py:465
  85.7 0.0 collective-permute-start.10
  85.7 4.5 %collective-permute-done.8.refs_1_ = bf16[48,2176]{1,0:T(8,128)(2,1)S(1)} collective-permute-done((bf16[48,2176]{1,0:T(8,128)(2,1)S(1)}, bf16[48,2176]{1,0:T(8,128)(2,1)S(1)}, u32[]{:S(2)}, u32[]{:S(2)}) %collective-permute-start.8) | collective-permute-done | bytes 208928 | tf_op jit(solution)/shard_map/ppermute | solution.py:465
  90.2 4.6 %collective-permute-done.9.refs_2_ = bf16[48,2176]{1,0:T(8,128)(2,1)S(1)} collective-permute-done((bf16[48,2176]{1,0:T(8,128)(2,1)S(1)}, bf16[48,2176]{1,0:T(8,128)(2,1)S(1)}, u32[]{:S(2)}, u32[]{:S(2)}) %collective-permute-start.9) | collective-permute-done | bytes 208928 | tf_op jit(solution)/shard_map/ppermute | solution.py:465
  94.8 0.0 collective-permute-done.10.refs_3_
  94.8 0.2 hidden_units.1.refs_3_
  95.0 2.5 %collective-permute-start.13 = (bf16[48,1024]{1,0:T(8,128)(2,1)S(1)}, bf16[48,1024]{1,0:T(8,128)(2,1)S(1)}, u32[]{:S(2)}, u32[]{:S(2)}) collective-permute-start(bf16[48,1024]{1,0:T(8,128)(2,1)S(1)} %hidden_units.1.refs_3_), channel_id=1, source_target_pairs={{0,6},{1,7},{2,0},{3,1},{4,2},{5,3},{6,4},{7,5},{8,14},{9,15},{10,... | collective-permute-start | bytes 294920 | tf_op jit(solution)/shard_map/ppermute | solution.py:465
  97.6 0.2 collective-permute-start.12
  97.7 0.8 collective-permute-start.11
  98.5 0.0 collective-permute-start.14
  98.5 3.4 %collective-permute-done.13.refs_6_ = bf16[48,1024]{1,0:T(8,128)(2,1)S(1)} collective-permute-done((bf16[48,1024]{1,0:T(8,128)(2,1)S(1)}, bf16[48,1024]{1,0:T(8,128)(2,1)S(1)}, u32[]{:S(2)}, u32[]{:S(2)}) %collective-permute-start.13) | collective-permute-done | bytes 98336 | tf_op jit(solution)/shard_map/ppermute | solution.py:465
  101.9 0.0 collective-permute-start.17
  101.9 2.7 %collective-permute-done.12.refs_5_ = bf16[48,1024]{1,0:T(8,128)(2,1)S(1)} collective-permute-done((bf16[48,1024]{1,0:T(8,128)(2,1)S(1)}, bf16[48,1024]{1,0:T(8,128)(2,1)S(1)}, u32[]{:S(2)}, u32[]{:S(2)}) %collective-permute-start.12) | collective-permute-done | bytes 98336 | tf_op jit(solution)/shard_map/ppermute | solution.py:465
  104.6 0.0 collective-permute-start.16
  104.6 0.7 collective-permute-done.11.refs_4_
  105.3 0.0 collective-permute-start.15
  105.3 0.0 collective-permute-done.14.refs_7_
  105.3 0.0 collective-permute-done.17.refs_10_
  105.4 0.0 copy-start.14
  105.4 0.6 collective-permute-done.16.refs_9_
  105.9 0.7 collective-permute-done.15.refs_8_
  106.6 3.8 %all-to-all-done.3.refs_1_ = bf16[32,128,128]{2,1,0:T(8,128)(2,1)S(1)} async-done(((bf16[32,128,128]{2,1,0:T(8,128)(2,1)}), bf16[32,128,128]{2,1,0:T(8,128)(2,1)S(1)}, u32[]{:S(2)}, u32[]{:S(2)}) %all-to-all-start.3) | async-done | bytes 1048608 | tf_op jit(solution)/shard_map/all_to_all | solution.py:753
  110.5 1.0 copy-done.9
  111.5 5.4 %shrink_experts.1 = bf16[32,176,128]{2,1,0:T(8,128)(2,1)} custom-call(s32[8,256]{1,0:T(8,128)S(1)} %get-tuple-element.90.refs_0_, bf16[32,128,128]{2,1,0:T(8,128)(2,1)} %copy-done.9, bf16[2,1024,512]{2,1,0:T(8,128)(2,1)} %refs_2_.5, bf16[48,1024]{1,0:T(8,128)(2,1)} %copy-done.3, bf16[48,1024]{1,0:T(8,128)(2,1)} %copy-done.12, bf16[48,1024]{1,0:T(8,128)(2,1)} %copy-done.11, ...), custom_call_target="tpu_custom_call" | custom-call | flops 805306368 | bytes 4194304 | tf_op jit(solution)/shard_map/shrink_experts/pallas_call | solution.py:63
  116.9 44.4 %all_to_all.24.refs_1_ = bf16[32,176,128]{2,1,0:T(8,128)(2,1)S(1)} all-to-all(bf16[32,176,128]{2,1,0:T(8,128)(2,1)} %shrink_experts.1), channel_id=1, replica_groups=mesh['req'=32,'head'=8] {'req'}, dimensions={0} | all-to-all | bytes 2883584 | tf_op jit(solution)/shard_map/all_to_all | solution.py:753
  161.3 2.7 %finish.1 = (bf16[24,512]{1,0:T(8,128)(2,1)}, f32[8,512,128]{2,1,0:T(8,128)}) custom-call(s32[8,256]{1,0:T(8,128)S(1)} %get-tuple-element.90.refs_0_, bf16[32,176,128]{2,1,0:T(8,128)(2,1)S(1)} %all_to_all.24.refs_1_, bf16[24,1536]{1,0:T(8,128)(2,1)S(1)} %get-tuple-element.131.refs_2_, bf16[24,1536]{1,0:T(8,128)(2,1)S(1)} %get-tuple-element.132.refs_3_, ...), custom_call_target="tpu_custom_call" | custom-call | flops 100000000 | bytes 4194304 | tf_op jit(solution)/shard_map/finish/pallas_call | solution.py:63
  (32 shorter events, 0.1 us)
Async XLA Ops:
  4.5 29.9 %copy-start = (f32[8,8,64,128]{3,2,1,0:T(8,128)S(1)}, f32[8,8,64,128]{3,2,1,0:T(8,128)}, u32[]{:S(2)}) copy-start(f32[8,8,64,128]{3,2,1,0:T(8,128)} %param.20) | copy-start | bytes 6291460
  4.5 29.9 %copy-start.4 = (f32[512]{0:T(512)S(1)}, f32[512]{0:T(512)}, u32[]{:S(2)}) copy-start(f32[512]{0:T(512)} %param.28) | copy-start | bytes 6148
  4.5 29.9 %copy-start.6 = (f32[8]{0:T(128)S(1)}, f32[8]{0:T(128)}, u32[]{:S(2)}) copy-start(f32[8]{0:T(128)} %param.26) | copy-start | bytes 100
  4.5 29.9 %copy-start.7 = (f32[8]{0:T(128)S(1)}, f32[8]{0:T(128)}, u32[]{:S(2)}) copy-start(f32[8]{0:T(128)} %param.27) | copy-start | bytes 100
  4.5 29.0 %all-to-all-start.1 = ((bf16[32,64,128]{2,1,0:T(8,128)(2,1)}), bf16[32,64,128]{2,1,0:T(8,128)(2,1)S(1)}, u32[]{:S(2)}, u32[]{:S(2)}) async-start(bf16[32,64,128]{2,1,0:T(8,128)(2,1)} %get-tuple-element.33), calls=%async_computation.1 | async-start | bytes 1048576 | tf_op jit(solution)/shard_map/cond/branch_1_fun/all_to_all | solution.py:753
  15.9 17.6 %copy-start.20 = (s32[2,256]{1,0:T(2,128)S(1)}, s32[2,256]{1,0:T(2,128)}, u32[]{:S(2)}) copy-start(s32[2,256]{1,0:T(2,128)} %get-tuple-element.32.refs_0_) | copy-start | bytes 6148 | tf_op jit(solution)/shard_map/cond
  37.9 1.6 collective-permute-start
  39.5 5.9 %collective-permute-start.1 = (bf16[24,512]{1,0:T(8,128)(2,1)S(1)}, bf16[24,512]{1,0:T(8,128)(2,1)S(1)}, u32[]{:S(2)}, u32[]{:S(2)}) collective-permute-start(bf16[24,512]{1,0:T(8,128)(2,1)S(1)} %get-tuple-element.95), channel_id=1, source_target_pairs={{0,2},{1,3},{2,4},{3,5},{4,6},{5,7},{6,0},{7,1},{8,10},{9,11},{10,... | collective-permute-start | bytes 73736 | tf_op jit(solution)/shard_map/ppermute | solution.py:465
  41.1 5.3 %collective-permute-start.2 = (bf16[24,512]{1,0:T(8,128)(2,1)S(1)}, bf16[24,512]{1,0:T(8,128)(2,1)S(1)}, u32[]{:S(2)}, u32[]{:S(2)}) collective-permute-start(bf16[24,512]{1,0:T(8,128)(2,1)S(1)} %get-tuple-element.96), channel_id=1, source_target_pairs={{0,4},{1,5},{2,6},{3,7},{4,0},{5,1},{6,2},{7,3},{8,12},{9,13},{10,... | collective-permute-start | bytes 73736 | tf_op jit(solution)/shard_map/ppermute | solution.py:465
  44.0 3.8 %collective-permute-start.3 = (bf16[24,512]{1,0:T(8,128)(2,1)S(1)}, bf16[24,512]{1,0:T(8,128)(2,1)S(1)}, u32[]{:S(2)}, u32[]{:S(2)}) collective-permute-start(bf16[24,512]{1,0:T(8,128)(2,1)S(1)} %get-tuple-element.97), channel_id=1, source_target_pairs={{0,6},{1,7},{2,0},{3,1},{4,2},{5,3},{6,4},{7,5},{8,14},{9,15},{10,... | collective-permute-start | bytes 73736 | tf_op jit(solution)/shard_map/ppermute | solution.py:465
  47.8 19.4 %copy-start.8 = (f32[3,8,8]{2,1,0:T(8,128)S(1)}, f32[3,8,8]{2,1,0:T(8,128)}, u32[]{:S(2)}) copy-start(f32[3,8,8]{2,1,0:T(8,128)} %param.33) | copy-start | bytes 2308
  47.8 19.5 %copy-start.17 = (s32[3,8,8]{2,1,0:T(8,128)S(1)}, s32[3,8,8]{2,1,0:T(8,128)}, u32[]{:S(2)}) copy-start(s32[3,8,8]{2,1,0:T(8,128)} %refs_7_.3) | copy-start | bytes 2308
  47.8 19.5 %copy-start.18 = (s32[2,256]{1,0:T(2,128)S(1)}, s32[2,256]{1,0:T(2,128)}, u32[]{:S(2)}) copy-start(s32[2,256]{1,0:T(2,128)} %refs_0_.2) | copy-start | bytes 6148
  60.0 10.1 %collective-permute-start.6 = (bf16[192,512]{1,0:T(8,128)(2,1)S(1)}, bf16[192,512]{1,0:T(8,128)(2,1)S(1)}, u32[]{:S(2)}, u32[]{:S(2)}) collective-permute-start(bf16[192,512]{1,0:T(8,128)(2,1)S(1)} %bitcast.14), channel_id=1, source_target_pairs={{0,192},{8,200},{16,208},{24,216},{32,224},{40,232},{48,240},{56,2... | collective-permute-start | bytes 589832 | tf_op jit(solution)/shard_map/ppermute | solution.py:460
  61.1 9.0 %collective-permute-start.5 = (bf16[192,512]{1,0:T(8,128)(2,1)S(1)}, bf16[192,512]{1,0:T(8,128)(2,1)S(1)}, u32[]{:S(2)}, u32[]{:S(2)}) collective-permute-start(bf16[192,512]{1,0:T(8,128)(2,1)S(1)} %bitcast.15), channel_id=1, source_target_pairs={{0,128},{8,136},{16,144},{24,152},{32,160},{40,168},{48,176},{56,1... | collective-permute-start | bytes 589832 | tf_op jit(solution)/shard_map/ppermute | solution.py:460
  62.7 7.9 %collective-permute-start.4 = (bf16[192,512]{1,0:T(8,128)(2,1)S(1)}, bf16[192,512]{1,0:T(8,128)(2,1)S(1)}, u32[]{:S(2)}, u32[]{:S(2)}) collective-permute-start(bf16[192,512]{1,0:T(8,128)(2,1)S(1)} %bitcast.16), channel_id=1, source_target_pairs={{0,64},{8,72},{16,80},{24,88},{32,96},{40,104},{48,112},{56,120},{... | collective-permute-start | bytes 589832 | tf_op jit(solution)/shard_map/ppermute | solution.py:460
  62.8 7.8 %copy-start.2 = (bf16[2,512,1024]{2,1,0:T(8,128)(2,1)S(1)}, bf16[2,512,1024]{2,1,0:T(8,128)(2,1)}, u32[]{:S(2)}) copy-start(bf16[2,512,1024]{2,1,0:T(8,128)(2,1)} %refs_8_.1) | copy-start | bytes 6291460
  67.3 3.4 %copy-start.1 = (bf16[2,512,1024]{2,1,0:T(8,128)(2,1)S(1)}, bf16[2,512,1024]{2,1,0:T(8,128)(2,1)}, u32[]{:S(2)}) copy-start(bf16[2,512,1024]{2,1,0:T(8,128)(2,1)} %refs_7_.5) | copy-start | bytes 6291460
  67.3 3.4 %copy-start.5 = (f32[512]{0:T(512)S(1)}, f32[512]{0:T(512)}, u32[]{:S(2)}) copy-start(f32[512]{0:T(512)} %param.31) | copy-start | bytes 6148
  73.1 2.4 %collective-permute-start.7 = (bf16[4,48,2176]{2,1,0:T(8,128)(2,1)S(1)}, bf16[4,48,2176]{2,1,0:T(8,128)(2,1)S(1)}, u32[]{:S(2)}, u32[]{:S(2)}) collective-permute-start(bf16[4,48,2176]{2,1,0:T(8,128)(2,1)S(1)} %get-tuple-element.120), channel_id=1, source_target_pairs={{0,1},{1,0},{2,3},{3,2},{4,5},{5,4},{6,7},{7,6},{8,9},{9,8},{10,11... | collective-permute-start | bytes 2506760 | tf_op jit(solution)/shard_map/ppermute | solution.py:502
  75.8 34.6 %all-to-all-start.3 = ((bf16[32,128,128]{2,1,0:T(8,128)(2,1)}), bf16[32,128,128]{2,1,0:T(8,128)(2,1)S(1)}, u32[]{:S(2)}, u32[]{:S(2)}) async-start(bf16[32,128,128]{2,1,0:T(8,128)(2,1)} %bitcast.9), calls=%async_computation.3 | async-start | bytes 2097152 | tf_op jit(solution)/shard_map/all_to_all | solution.py:753
  81.6 8.6 %collective-permute-start.8 = (bf16[48,2176]{1,0:T(8,128)(2,1)S(1)}, bf16[48,2176]{1,0:T(8,128)(2,1)S(1)}, u32[]{:S(2)}, u32[]{:S(2)}) collective-permute-start(bf16[48,2176]{1,0:T(8,128)(2,1)S(1)} %get-tuple-element.128), channel_id=1, source_target_pairs={{0,2},{1,3},{2,4},{3,5},{4,6},{5,7},{6,0},{7,1},{8,10},{9,11},{10,... | collective-permute-start | bytes 626696 | tf_op jit(solution)/shard_map/ppermute | solution.py:465
  81.8 13.1 %collective-permute-start.9 = (bf16[48,2176]{1,0:T(8,128)(2,1)S(1)}, bf16[48,2176]{1,0:T(8,128)(2,1)S(1)}, u32[]{:S(2)}, u32[]{:S(2)}) collective-permute-start(bf16[48,2176]{1,0:T(8,128)(2,1)S(1)} %get-tuple-element.129), channel_id=1, source_target_pairs={{0,4},{1,5},{2,6},{3,7},{4,0},{5,1},{6,2},{7,3},{8,12},{9,13},{10,... | collective-permute-start | bytes 626696 | tf_op jit(solution)/shard_map/ppermute | solution.py:465
  85.7 9.1 %collective-permute-start.10 = (bf16[48,2176]{1,0:T(8,128)(2,1)S(1)}, bf16[48,2176]{1,0:T(8,128)(2,1)S(1)}, u32[]{:S(2)}, u32[]{:S(2)}) collective-permute-start(bf16[48,2176]{1,0:T(8,128)(2,1)S(1)} %get-tuple-element.130), channel_id=1, source_target_pairs={{0,6},{1,7},{2,0},{3,1},{4,2},{5,3},{6,4},{7,5},{8,14},{9,15},{10,... | collective-permute-start | bytes 626696 | tf_op jit(solution)/shard_map/ppermute | solution.py:465
  95.0 15.4 %copy-start.3 = (bf16[48,1024]{1,0:T(8,128)(2,1)}, bf16[48,1024]{1,0:T(8,128)(2,1)S(1)}, u32[]{:S(2)}) copy-start(bf16[48,1024]{1,0:T(8,128)(2,1)S(1)} %hidden_units.1.refs_3_) | copy-start | bytes 294916
  95.0 6.9 %collective-permute-start.13 = (bf16[48,1024]{1,0:T(8,128)(2,1)S(1)}, bf16[48,1024]{1,0:T(8,128)(2,1)S(1)}, u32[]{:S(2)}, u32[]{:S(2)}) collective-permute-start(bf16[48,1024]{1,0:T(8,128)(2,1)S(1)} %hidden_units.1.refs_3_), channel_id=1, source_target_pairs={{0,6},{1,7},{2,0},{3,1},{4,2},{5,3},{6,4},{7,5},{8,14},{9,15},{10,... | collective-permute-start | bytes 294920 | tf_op jit(solution)/shard_map/ppermute | solution.py:465
  97.6 7.1 %collective-permute-start.12 = (bf16[48,1024]{1,0:T(8,128)(2,1)S(1)}, bf16[48,1024]{1,0:T(8,128)(2,1)S(1)}, u32[]{:S(2)}, u32[]{:S(2)}) collective-permute-start(bf16[48,1024]{1,0:T(8,128)(2,1)S(1)} %hidden_units.1.refs_3_), channel_id=1, source_target_pairs={{0,4},{1,5},{2,6},{3,7},{4,0},{5,1},{6,2},{7,3},{8,12},{9,13},{10,... | collective-permute-start | bytes 294920 | tf_op jit(solution)/shard_map/ppermute | solution.py:465
  97.7 7.6 %collective-permute-start.11 = (bf16[48,1024]{1,0:T(8,128)(2,1)S(1)}, bf16[48,1024]{1,0:T(8,128)(2,1)S(1)}, u32[]{:S(2)}, u32[]{:S(2)}) collective-permute-start(bf16[48,1024]{1,0:T(8,128)(2,1)S(1)} %hidden_units.1.refs_3_), channel_id=1, source_target_pairs={{0,2},{1,3},{2,4},{3,5},{4,6},{5,7},{6,0},{7,1},{8,10},{9,11},{10,... | collective-permute-start | bytes 294920 | tf_op jit(solution)/shard_map/ppermute | solution.py:465
  98.5 6.8 %collective-permute-start.14 = (bf16[48,1024]{1,0:T(8,128)(2,1)S(1)}, bf16[48,1024]{1,0:T(8,128)(2,1)S(1)}, u32[]{:S(2)}, u32[]{:S(2)}) collective-permute-start(bf16[48,1024]{1,0:T(8,128)(2,1)S(1)} %hidden_units.1.refs_3_), channel_id=1, source_target_pairs={{0,1},{1,0},{2,3},{3,2},{4,5},{5,4},{6,7},{7,6},{8,9},{9,8},{10,11... | collective-permute-start | bytes 294920 | tf_op jit(solution)/shard_map/ppermute | solution.py:799
  101.9 8.5 %copy-start.10 = (bf16[48,1024]{1,0:T(8,128)(2,1)}, bf16[48,1024]{1,0:T(8,128)(2,1)S(1)}, u32[]{:S(2)}) copy-start(bf16[48,1024]{1,0:T(8,128)(2,1)S(1)} %collective-permute-done.13.refs_6_) | copy-start | bytes 294916
  101.9 3.4 %collective-permute-start.17 = (bf16[48,1024]{1,0:T(8,128)(2,1)S(1)}, bf16[48,1024]{1,0:T(8,128)(2,1)S(1)}, u32[]{:S(2)}, u32[]{:S(2)}) collective-permute-start(bf16[48,1024]{1,0:T(8,128)(2,1)S(1)} %collective-permute-done.13.refs_6_), channel_id=1, source_target_pairs={{0,1},{1,0},{2,3},{3,2},{4,5},{5,4},{6,7},{7,6},{8,9},{9,8},{10,11... | collective-permute-start | bytes 294920 | tf_op jit(solution)/shard_map/ppermute | solution.py:799
  104.6 5.8 %copy-start.11 = (bf16[48,1024]{1,0:T(8,128)(2,1)}, bf16[48,1024]{1,0:T(8,128)(2,1)S(1)}, u32[]{:S(2)}) copy-start(bf16[48,1024]{1,0:T(8,128)(2,1)S(1)} %collective-permute-done.12.refs_5_) | copy-start | bytes 294916
  104.6 1.3 collective-permute-start.16
  105.3 5.1 %copy-start.12 = (bf16[48,1024]{1,0:T(8,128)(2,1)}, bf16[48,1024]{1,0:T(8,128)(2,1)S(1)}, u32[]{:S(2)}) copy-start(bf16[48,1024]{1,0:T(8,128)(2,1)S(1)} %collective-permute-done.11.refs_4_) | copy-start | bytes 294916
  105.3 1.3 collective-permute-start.15
  105.3 5.1 %copy-start.13 = (bf16[48,1024]{1,0:T(8,128)(2,1)}, bf16[48,1024]{1,0:T(8,128)(2,1)S(1)}, u32[]{:S(2)}) copy-start(bf16[48,1024]{1,0:T(8,128)(2,1)S(1)} %collective-permute-done.14.refs_7_) | copy-start | bytes 294916
  105.4 5.1 %copy-start.14 = (bf16[48,1024]{1,0:T(8,128)(2,1)}, bf16[48,1024]{1,0:T(8,128)(2,1)S(1)}, u32[]{:S(2)}) copy-start(bf16[48,1024]{1,0:T(8,128)(2,1)S(1)} %collective-permute-done.17.refs_10_) | copy-start | bytes 294916
  105.9 4.5 %copy-start.15 = (bf16[48,1024]{1,0:T(8,128)(2,1)}, bf16[48,1024]{1,0:T(8,128)(2,1)S(1)}, u32[]{:S(2)}) copy-start(bf16[48,1024]{1,0:T(8,128)(2,1)S(1)} %collective-permute-done.16.refs_9_) | copy-start | bytes 294916
  106.6 3.8 %copy-start.16 = (bf16[48,1024]{1,0:T(8,128)(2,1)}, bf16[48,1024]{1,0:T(8,128)(2,1)S(1)}, u32[]{:S(2)}) copy-start(bf16[48,1024]{1,0:T(8,128)(2,1)S(1)} %collective-permute-done.15.refs_8_) | copy-start | bytes 294916
  110.5 1.0 copy-start.9

commit v5 on v4

--- a/solution.py
+++ b/solution.py
@@ -784,13 +784,15 @@
     line = lax.all_to_all(
         copies, "req", split_axis=0, concat_axis=0, axis_index_groups=lines, tiled=True
     ).reshape(LINE * ROWS, WIDTH)
+    pieces = update_states(table, state_rows, factors)
+    routed = routes(later_dest, all_ids, route_ids.reshape(ROWS, 8), route_weights.reshape(ROWS, 8))
+    line, pieces, (pick, kept, high, low) = fence((line, pieces, routed))
     streams = [line, along_x(line, 1), along_x(line, 2), along_x(line, 3)]
-    routed = routes(later_dest, all_ids, route_ids.reshape(ROWS, 8), route_weights.reshape(ROWS, 8))
-    pieces = update_states(table, state_rows, factors)
-    streams, pieces, (pick, kept, high, low) = fence((streams, pieces, routed))
+    streams[1], pieces = fence((streams[1], pieces))
+    pieces = exchange(pieces.reshape(OWNERS, 2 * HSIZE, NSTATE))
 
     keep_part, send_part, own_stream = expand(pick, kept, streams, ffn_gain[None], gate_weight, up_weight)
-    parts, pieces = scatter_sum(keep_part, send_part, True, pieces.reshape(OWNERS, 2 * HSIZE, NSTATE))
+    parts, _ = scatter_sum(keep_part, send_part, True)
     hidden = hidden_units(parts)
     far = along_y(hidden, 2)
     near = along_y(hidden, 1)

time: 165 us -> 181 us (1.097)
  waiting for transfers between devices: 38.8 us -> 54.6 us
  blocking collectives: 56.5 us -> 48.6 us
  starting transfers between devices: 33.8 us -> 40.1 us
    ppermute x3, waiting for transfers between devices: 0.49 us -> 18.7 us  [along_x(): return lax.ppermute(value, 'req', moves)]
    all_to_all x1 -> x0, blocking collectives: 12.1 us -> none  [shards(): lax.all_to_all(copies, 'req', split_axis=0, concat_axis=0, axis_index_gro...]
    all_to_all x1, blocking collectives: 44.4 us -> 48.6 us  [exchange(): return lax.all_to_all(value, 'req', split_axis=0, concat_axis=0, tiled=True)]
    all_to_all x0 -> x1, starting transfers between devices: none -> 3.88 us  [shards(): lax.all_to_all(copies, 'req', split_axis=0, concat_axis=0, axis_index_gro...]
    all_to_all x2, waiting for transfers between devices: 15 us -> 11.3 us  [exchange(): return lax.all_to_all(value, 'req', split_axis=0, concat_axis=0, tiled=True)]
  transfers between devices with their start and end apart: 20 -> 21, of which waited for: 14 -> 16; matrix products, arithmetic and copies ran while one was open for 0% -> 0% of each run, Pallas kernels for 8% -> 9%
where the time goes in v5:
time: 181 us; the launch traced here: 180 us
  waiting for transfers between devices  54.6 us (30%)
  blocking collectives  48.6 us (27%)
  starting transfers between devices  40.1 us (22%)
  Pallas kernels  32.8 us (18%)
  local copies, waits for them, and re-layouts  2.24 us (1%)
    all_to_all x1, blocking collectives, exchange(): return lax.all_to_all(value, 'req', split_axis=0, concat_axis=0, tiled=True)  48.6 us
    pallas_call x13, Pallas kernels, run_kernel(): pl.pallas_call(kernel, out_shape=tuple(outs), in_specs=[VMEM_SPEC if mode...  32.8 us
    ppermute x3, waiting for transfers between devices, along_x(): return lax.ppermute(value, 'req', moves)  18.7 us
    ppermute x9, waiting for transfers between devices, along_y(): return lax.ppermute(value, 'head', moves)  18.7 us
    all_to_all x2, starting transfers between devices, exchange(): return lax.all_to_all(value, 'req', split_axis=0, concat_axis=0, tiled=True)  17.8 us
    ppermute x9, starting transfers between devices, along_y(): return lax.ppermute(value, 'head', moves)  13.8 us
    all_to_all x2, waiting for transfers between devices, exchange(): return lax.all_to_all(value, 'req', split_axis=0, concat_axis=0, tiled=True)  11.3 us
    ppermute x3, starting transfers between devices, along_x(): return lax.ppermute(value, 'req', moves)  4.21 us
  transfers between devices with their start and end apart: 21, of which 16 were waited for; matrix products, arithmetic and copies ran while one was open for 0% of the time, Pallas kernels for 9%

profile of v5, /device:TPU:32, one launch (start us, length us, event | category | flops | bytes accessed | tf_op | source)
XLA Modules:
  0.0 180.1 jit_solution(6548207363610645321)
XLA Ops:
  0.6 3.2 %pack_few.1 = (bf16[32,64,128]{2,1,0:T(8,128)(2,1)}, s32[1,1]{1,0:T(1,128)}) custom-call(s32[2,256]{1,0:T(2,128)} %refs_0_.2, bf16[3,8,512]{2,1,0:T(8,128)(2,1)} %refs_2_.4, bf16[3,8,512]{2,1,0:T(8,128)(2,1)} %refs_3_.3, bf16[3,8,4096]{2,1,0:T(8,128)(2,1)} %refs_4_.3, bf16[3,8,128]{2,1,0:T(8,128)(2,1)} %refs_5_.3, bf16[3,8,128]{2,1,0:T(8,128)(2,1)} %refs_6_.3, ...), custom_call_target="tpu_custom_call" | custom-call | bytes 1048576 | tf_op jit(solution)/shard_map/pack_few/pallas_call | solution.py:63
  4.4 0.0 copy-start
  4.5 0.0 copy-start.4
  4.5 0.0 copy-start.6
  4.5 0.0 copy-start.7
  4.5 29.8 %conditional.1 = (bf16[8,32,128]{2,1,0:T(8,128)(2,1)S(1)}, bf16[256,128]{1,0:T(8,128)(2,1)S(1)}, s32[8,256]{1,0:T(8,128)S(1)}) conditional(s32[]{:T(128)} %bitcast, (s32[2,256]{1,0:T(2,128)}, bf16[3,8,512]{2,1,0:T(8,128)(2,1)}, bf16[3,8,512]{2,1,0:T(8,128)(2,1)}, bf16[3,8,4096]{2,1,0:T(8,128)(2,1)}, bf16[3,8,128]{2,1,0:T(8,128)(2,1)}, ...), branch_computations={%region_0.0_spmd, %region_1.0_spmd} | conditional | flops 2000000000 | bytes 6692948 | solution.py:776
  4.5 11.3 %all-to-all-start.1 = ((bf16[32,64,128]{2,1,0:T(8,128)(2,1)}), bf16[32,64,128]{2,1,0:T(8,128)(2,1)S(1)}, u32[]{:S(2)}, u32[]{:S(2)}) async-start(bf16[32,64,128]{2,1,0:T(8,128)(2,1)} %get-tuple-element.33), calls=%async_computation.1 | async-start | bytes 1048576 | tf_op jit(solution)/shard_map/cond/branch_1_fun/all_to_all | solution.py:753
  15.9 0.0 copy-start.19
  15.9 6.3 %plan_states.3 = s32[8,256]{1,0:T(8,128)S(1)} custom-call(s32[2,256]{1,0:T(2,128)} %get-tuple-element.32.refs_0_), custom_call_target="tpu_custom_call" | custom-call | flops 2000000000 | bytes 1048576 | tf_op jit(solution)/shard_map/cond/branch_1_fun/plan_states/pallas_call | solution.py:63
  22.2 11.3 %all-to-all-done.1.refs_1_ = bf16[32,64,128]{2,1,0:T(8,128)(2,1)S(1)} async-done(((bf16[32,64,128]{2,1,0:T(8,128)(2,1)}), bf16[32,64,128]{2,1,0:T(8,128)(2,1)S(1)}, u32[]{:S(2)}, u32[]{:S(2)}) %all-to-all-start.1) | async-done | bytes 524320 | tf_op jit(solution)/shard_map/cond/branch_1_fun/all_to_all | solution.py:753
  33.5 0.8 take_rows.3
  34.3 3.5 %mamba_steps.1 = (bf16[4,24,512]{2,1,0:T(8,128)(2,1)S(1)}, bf16[4,24,512]{2,1,0:T(8,128)(2,1)S(1)}, f32[24,512]{1,0:T(8,128)S(1)}, f32[8,8,512]{2,1,0:T(8,128)S(...) custom-call(bf16[8,32,128]{2,1,0:T(8,128)(2,1)S(1)} %get-tuple-element.85.refs_0_, f32[8,512,128]{2,1,0:T(8,128)S(1)} %bitcast.12, ...), custom_call_target="tpu_custom_call" | custom-call | flops 100663296 | bytes 8388608 | tf_op jit(solution)/shard_map/mamba_steps/pallas_call | solution.py:63
  37.8 0.3 collective-permute-start
  38.1 1.3 collective-permute-done.refs_1_
  39.4 1.7 collective-permute-start.1
  41.1 2.9 %collective-permute-start.2 = (bf16[24,512]{1,0:T(8,128)(2,1)S(1)}, bf16[24,512]{1,0:T(8,128)(2,1)S(1)}, u32[]{:S(2)}, u32[]{:S(2)}) collective-permute-start(bf16[24,512]{1,0:T(8,128)(2,1)S(1)} %get-tuple-element.90), channel_id=1, source_target_pairs={{0,4},{1,5},{2,6},{3,7},{4,0},{5,1},{6,2},{7,3},{8,12},{9,13},{10,... | collective-permute-start | bytes 73736 | tf_op jit(solution)/shard_map/ppermute | solution.py:465
  44.0 1.3 collective-permute-start.3
  45.3 0.0 collective-permute-done.1.refs_1_
  45.3 1.1 collective-permute-done.2.refs_2_
  46.4 1.4 collective-permute-done.3.refs_3_
  47.8 0.7 stream_copies.1
  48.5 3.9 %all-to-all-start.2 = ((bf16[8,24,512]{2,1,0:T(8,128)(2,1)}), bf16[8,24,512]{2,1,0:T(8,128)(2,1)S(1)}, u32[]{:S(2)}, u32[]{:S(2)}) async-start(bf16[8,24,512]{2,1,0:T(8,128)(2,1)} %stream_copies.1), calls=%async_computation.2 | async-start | bytes 393216 | tf_op jit(solution)/shard_map/all_to_all | solution.py:784
  52.4 4.4 %update_states.1 = bf16[8,512,128]{2,1,0:T(8,128)(2,1)} custom-call(s32[8,256]{1,0:T(8,128)S(1)} %get-tuple-element.84.refs_0_, f32[8,512,128]{2,1,0:T(8,128)S(1)} %bitcast.13, f32[8,8,512]{2,1,0:T(8,128)S(1)} %get-tuple-element.98.refs_2_, f32[8,8,512]{2,1,0:T(8,128)S(1)} %get-tuple-element.99.refs_3_, f32[8,8,128]{2,1,0:T(8,128)S(1)} %get-tuple-element.100.refs_4_), custom_call_target="tpu_custom_call" | custom-call | flops 33554432 | bytes 3145728 | tf_op jit(solution)/shard_map/update_states/pallas_call | solution.py:63
  56.9 0.0 copy-start.1
  56.9 0.0 copy-start.5
  56.9 2.8 %routes.1 = (bf16[384,768]{1,0:T(8,128)(2,1)S(1)}, bf16[24,768]{1,0:T(8,128)(2,1)S(1)}, bf16[24,1536]{1,0:T(8,128)(2,1)S(1)}, bf16[24,1536]{1,0:T(8,128)(2,1)S(1)}) custom-call(s32[2,256]{1,0:T(2,128)S(1)} %copy-done.17, bf16[256,128]{1,0:T(8,128)(2,1)S(1)} %get-tuple-element.102.refs_1_, s32[24,8]{1,0:T(8,128)S(1)} %bitcast.23, f32[24,8]{1,0:T(8,128)S(1)} %bitcast.22), custom_call_target="tpu_custom_call" | custom-call | flops 1000000000 | bytes 1048576 | tf_op jit(solution)/shard_map/routes/pallas_call | solution.py:63
  59.7 1.0 all-to-all-done.2
  60.7 0.6 collective-permute-start.4
  61.3 6.3 %collective-permute-done.4.refs_3_ = bf16[192,512]{1,0:T(8,128)(2,1)S(1)} collective-permute-done((bf16[192,512]{1,0:T(8,128)(2,1)S(1)}, bf16[192,512]{1,0:T(8,128)(2,1)S(1)}, u32[]{:S(2)}, u32[]{:S(2)}) %collective-permute-start.4) | collective-permute-done | bytes 196640 | tf_op jit(solution)/shard_map/ppermute | solution.py:460
  67.6 6.5 %all-to-all-start.3 = ((bf16[32,128,128]{2,1,0:T(8,128)(2,1)}), bf16[32,128,128]{2,1,0:T(8,128)(2,1)}, u32[]{:S(2)}, u32[]{:S(2)}) async-start(bf16[32,128,128]{2,1,0:T(8,128)(2,1)} %bitcast.8), calls=%async_computation.3 | async-start | bytes 2097152 | tf_op jit(solution)/shard_map/all_to_all | solution.py:753
  74.1 2.8 %collective-permute-start.6 = (bf16[192,512]{1,0:T(8,128)(2,1)S(1)}, bf16[192,512]{1,0:T(8,128)(2,1)S(1)}, u32[]{:S(2)}, u32[]{:S(2)}) collective-permute-start(bf16[192,512]{1,0:T(8,128)(2,1)S(1)} %bitcast.15), channel_id=1, source_target_pairs={{0,192},{8,200},{16,208},{24,216},{32,224},{40,232},{48,240},{56,2... | collective-permute-start | bytes 589832 | tf_op jit(solution)/shard_map/ppermute | solution.py:460
  76.9 0.8 collective-permute-start.5
  77.7 12.5 %collective-permute-done.6.refs_5_ = bf16[192,512]{1,0:T(8,128)(2,1)S(1)} collective-permute-done((bf16[192,512]{1,0:T(8,128)(2,1)S(1)}, bf16[192,512]{1,0:T(8,128)(2,1)S(1)}, u32[]{:S(2)}, u32[]{:S(2)}) %collective-permute-start.6) | collective-permute-done | bytes 196640 | tf_op jit(solution)/shard_map/ppermute | solution.py:460
  90.2 0.0 collective-permute-done.5.refs_4_
  90.2 1.6 copy-done.2
  91.8 2.4 %expand_experts.1 = (bf16[4,48,2176]{2,1,0:T(8,128)(2,1)S(1)}, bf16[4,48,2176]{2,1,0:T(8,128)(2,1)S(1)}, bf16[24,512]{1,0:T(8,128)(2,1)S(1)}) custom-call(bf16[384,768]{1,0:T(8,128)(2,1)S(1)} %get-tuple-element.110.refs_0_, bf16[24,768]{1,0:T(8,128)(2,1)S(1)} %get-tuple-element.111.refs_1_, bf16[192,512]{1,0:T(8,128)(2,1)S(1)} %bitcast.17, ...), custom_call_target="tpu_custom_call" | custom-call | flops 1107296256 | bytes 8388608 | tf_op jit(solution)/shard_map/expand_experts/pallas_call | solution.py:63
  94.2 0.1 collective-permute-start.7
  94.3 2.3 %collective-permute-done.7.refs_1_ = bf16[4,48,2176]{2,1,0:T(8,128)(2,1)S(1)} collective-permute-done((bf16[4,48,2176]{2,1,0:T(8,128)(2,1)S(1)}, bf16[4,48,2176]{2,1,0:T(8,128)(2,1)S(1)}, u32[]{:S(2)}, u32[]{:S(2)}) %collective-permute-start.7) | collective-permute-done | bytes 835616 | tf_op jit(solution)/shard_map/ppermute | solution.py:502
  96.7 0.3 add_cores.3
  97.0 0.3 collective-permute-start.8
  97.2 3.2 %collective-permute-start.9 = (bf16[48,2176]{1,0:T(8,128)(2,1)S(1)}, bf16[48,2176]{1,0:T(8,128)(2,1)S(1)}, u32[]{:S(2)}, u32[]{:S(2)}) collective-permute-start(bf16[48,2176]{1,0:T(8,128)(2,1)S(1)} %get-tuple-element.117), channel_id=1, source_target_pairs={{0,4},{1,5},{2,6},{3,7},{4,0},{5,1},{6,2},{7,3},{8,12},{9,13},{10,... | collective-permute-start | bytes 626696 | tf_op jit(solution)/shard_map/ppermute | solution.py:465
  100.4 0.8 collective-permute-start.10
  101.2 4.9 %collective-permute-done.8.refs_1_ = bf16[48,2176]{1,0:T(8,128)(2,1)S(1)} collective-permute-done((bf16[48,2176]{1,0:T(8,128)(2,1)S(1)}, bf16[48,2176]{1,0:T(8,128)(2,1)S(1)}, u32[]{:S(2)}, u32[]{:S(2)}) %collective-permute-start.8) | collective-permute-done | bytes 208928 | tf_op jit(solution)/shard_map/ppermute | solution.py:465
  106.1 4.0 %collective-permute-done.9.refs_2_ = bf16[48,2176]{1,0:T(8,128)(2,1)S(1)} collective-permute-done((bf16[48,2176]{1,0:T(8,128)(2,1)S(1)}, bf16[48,2176]{1,0:T(8,128)(2,1)S(1)}, u32[]{:S(2)}, u32[]{:S(2)}) %collective-permute-start.9) | collective-permute-done | bytes 208928 | tf_op jit(solution)/shard_map/ppermute | solution.py:465
  110.1 0.5 collective-permute-done.10.refs_3_
  110.6 0.2 hidden_units.1.refs_3_
  110.8 2.7 %collective-permute-start.13 = (bf16[48,1024]{1,0:T(8,128)(2,1)S(1)}, bf16[48,1024]{1,0:T(8,128)(2,1)S(1)}, u32[]{:S(2)}, u32[]{:S(2)}) collective-permute-start(bf16[48,1024]{1,0:T(8,128)(2,1)S(1)} %hidden_units.1.refs_3_), channel_id=1, source_target_pairs={{0,6},{1,7},{2,0},{3,1},{4,2},{5,3},{6,4},{7,5},{8,14},{9,15},{10,... | collective-permute-start | bytes 294920 | tf_op jit(solution)/shard_map/ppermute | solution.py:465
  113.5 0.3 collective-permute-start.12
  113.8 0.7 collective-permute-start.11
  114.4 0.0 collective-permute-start.14
  114.4 3.4 %collective-permute-done.13.refs_6_ = bf16[48,1024]{1,0:T(8,128)(2,1)S(1)} collective-permute-done((bf16[48,1024]{1,0:T(8,128)(2,1)S(1)}, bf16[48,1024]{1,0:T(8,128)(2,1)S(1)}, u32[]{:S(2)}, u32[]{:S(2)}) %collective-permute-start.13) | collective-permute-done | bytes 98336 | tf_op jit(solution)/shard_map/ppermute | solution.py:465
  117.9 0.0 collective-permute-start.17
  117.9 2.7 %collective-permute-done.12.refs_5_ = bf16[48,1024]{1,0:T(8,128)(2,1)S(1)} collective-permute-done((bf16[48,1024]{1,0:T(8,128)(2,1)S(1)}, bf16[48,1024]{1,0:T(8,128)(2,1)S(1)}, u32[]{:S(2)}, u32[]{:S(2)}) %collective-permute-start.12) | collective-permute-done | bytes 98336 | tf_op jit(solution)/shard_map/ppermute | solution.py:465
  120.5 0.0 collective-permute-start.16
  120.5 0.7 collective-permute-done.11.refs_4_
  121.3 0.0 collective-permute-start.15
  121.3 0.0 collective-permute-done.17.refs_10_
  121.3 0.5 collective-permute-done.16.refs_9_
  121.8 0.7 collective-permute-done.15.refs_8_
  122.6 0.0 all-to-all-done.3.refs_1_
  122.6 0.6 copy-done.15
  123.2 5.4 %shrink_experts.1 = bf16[32,176,128]{2,1,0:T(8,128)(2,1)} custom-call(s32[8,256]{1,0:T(8,128)S(1)} %get-tuple-element.84.refs_0_, bf16[32,128,128]{2,1,0:T(8,128)(2,1)} %all-to-all-done.3.refs_1_, bf16[2,1024,512]{2,1,0:T(8,128)(2,1)} %refs_2_.5, bf16[48,1024]{1,0:T(8,128)(2,1)} %copy-done.3, bf16[48,1024]{1,0:T(8,128)(2,1)} %copy-done.11, ...), custom_call_target="tpu_custom_call" | custom-call | flops 805306368 | bytes 4194304 | tf_op jit(solution)/shard_map/shrink_experts/pallas_call | solution.py:63
  128.6 48.6 %all_to_all.23.refs_1_ = bf16[32,176,128]{2,1,0:T(8,128)(2,1)S(1)} all-to-all(bf16[32,176,128]{2,1,0:T(8,128)(2,1)} %shrink_experts.1), channel_id=1, replica_groups=mesh['req'=32,'head'=8] {'req'}, dimensions={0} | all-to-all | bytes 2883584 | tf_op jit(solution)/shard_map/all_to_all | solution.py:753
  177.2 2.7 %finish.1 = (bf16[24,512]{1,0:T(8,128)(2,1)}, f32[8,512,128]{2,1,0:T(8,128)}) custom-call(s32[8,256]{1,0:T(8,128)S(1)} %get-tuple-element.84.refs_0_, bf16[32,176,128]{2,1,0:T(8,128)(2,1)S(1)} %all_to_all.23.refs_1_, bf16[24,1536]{1,0:T(8,128)(2,1)S(1)} %get-tuple-element.119.refs_2_, bf16[24,1536]{1,0:T(8,128)(2,1)S(1)} %get-tuple-element.120.refs_3_, ...), custom_call_target="tpu_custom_call" | custom-call | flops 100000000 | bytes 4194304 | tf_op jit(solution)/shard_map/finish/pallas_call | solution.py:63
  (31 shorter events, 0.1 us)
Async XLA Ops:
  4.4 29.9 %copy-start = (f32[8,8,64,128]{3,2,1,0:T(8,128)S(1)}, f32[8,8,64,128]{3,2,1,0:T(8,128)}, u32[]{:S(2)}) copy-start(f32[8,8,64,128]{3,2,1,0:T(8,128)} %param.20) | copy-start | bytes 6291460
  4.5 29.9 %copy-start.4 = (f32[512]{0:T(512)S(1)}, f32[512]{0:T(512)}, u32[]{:S(2)}) copy-start(f32[512]{0:T(512)} %param.28) | copy-start | bytes 6148
  4.5 29.9 %copy-start.6 = (f32[8]{0:T(128)S(1)}, f32[8]{0:T(128)}, u32[]{:S(2)}) copy-start(f32[8]{0:T(128)} %param.26) | copy-start | bytes 100
  4.5 29.9 %copy-start.7 = (f32[8]{0:T(128)S(1)}, f32[8]{0:T(128)}, u32[]{:S(2)}) copy-start(f32[8]{0:T(128)} %param.27) | copy-start | bytes 100
  4.5 29.0 %all-to-all-start.1 = ((bf16[32,64,128]{2,1,0:T(8,128)(2,1)}), bf16[32,64,128]{2,1,0:T(8,128)(2,1)S(1)}, u32[]{:S(2)}, u32[]{:S(2)}) async-start(bf16[32,64,128]{2,1,0:T(8,128)(2,1)} %get-tuple-element.33), calls=%async_computation.1 | async-start | bytes 1048576 | tf_op jit(solution)/shard_map/cond/branch_1_fun/all_to_all | solution.py:753
  15.9 17.6 %copy-start.19 = (s32[2,256]{1,0:T(2,128)S(1)}, s32[2,256]{1,0:T(2,128)}, u32[]{:S(2)}) copy-start(s32[2,256]{1,0:T(2,128)} %get-tuple-element.32.refs_0_) | copy-start | bytes 6148 | tf_op jit(solution)/shard_map/cond
  37.8 1.6 collective-permute-start
  39.4 5.9 %collective-permute-start.1 = (bf16[24,512]{1,0:T(8,128)(2,1)S(1)}, bf16[24,512]{1,0:T(8,128)(2,1)S(1)}, u32[]{:S(2)}, u32[]{:S(2)}) collective-permute-start(bf16[24,512]{1,0:T(8,128)(2,1)S(1)} %get-tuple-element.89), channel_id=1, source_target_pairs={{0,2},{1,3},{2,4},{3,5},{4,6},{5,7},{6,0},{7,1},{8,10},{9,11},{10,... | collective-permute-start | bytes 73736 | tf_op jit(solution)/shard_map/ppermute | solution.py:465
  41.1 5.3 %collective-permute-start.2 = (bf16[24,512]{1,0:T(8,128)(2,1)S(1)}, bf16[24,512]{1,0:T(8,128)(2,1)S(1)}, u32[]{:S(2)}, u32[]{:S(2)}) collective-permute-start(bf16[24,512]{1,0:T(8,128)(2,1)S(1)} %get-tuple-element.90), channel_id=1, source_target_pairs={{0,4},{1,5},{2,6},{3,7},{4,0},{5,1},{6,2},{7,3},{8,12},{9,13},{10,... | collective-permute-start | bytes 73736 | tf_op jit(solution)/shard_map/ppermute | solution.py:465
  44.0 3.8 %collective-permute-start.3 = (bf16[24,512]{1,0:T(8,128)(2,1)S(1)}, bf16[24,512]{1,0:T(8,128)(2,1)S(1)}, u32[]{:S(2)}, u32[]{:S(2)}) collective-permute-start(bf16[24,512]{1,0:T(8,128)(2,1)S(1)} %get-tuple-element.91), channel_id=1, source_target_pairs={{0,6},{1,7},{2,0},{3,1},{4,2},{5,3},{6,4},{7,5},{8,14},{9,15},{10,... | collective-permute-start | bytes 73736 | tf_op jit(solution)/shard_map/ppermute | solution.py:465
  47.8 9.0 %copy-start.8 = (f32[3,8,8]{2,1,0:T(8,128)S(1)}, f32[3,8,8]{2,1,0:T(8,128)}, u32[]{:S(2)}) copy-start(f32[3,8,8]{2,1,0:T(8,128)} %param.33) | copy-start | bytes 2308
  47.8 9.0 %copy-start.16 = (s32[3,8,8]{2,1,0:T(8,128)S(1)}, s32[3,8,8]{2,1,0:T(8,128)}, u32[]{:S(2)}) copy-start(s32[3,8,8]{2,1,0:T(8,128)} %refs_7_.3) | copy-start | bytes 2308
  47.8 9.1 %copy-start.17 = (s32[2,256]{1,0:T(2,128)S(1)}, s32[2,256]{1,0:T(2,128)}, u32[]{:S(2)}) copy-start(s32[2,256]{1,0:T(2,128)} %refs_0_.2) | copy-start | bytes 6148
  48.5 12.2 %all-to-all-start.2 = ((bf16[8,24,512]{2,1,0:T(8,128)(2,1)}), bf16[8,24,512]{2,1,0:T(8,128)(2,1)S(1)}, u32[]{:S(2)}, u32[]{:S(2)}) async-start(bf16[8,24,512]{2,1,0:T(8,128)(2,1)} %stream_copies.1), calls=%async_computation.2 | async-start | bytes 393216 | tf_op jit(solution)/shard_map/all_to_all | solution.py:784
  56.9 33.3 %copy-start.1 = (bf16[2,512,1024]{2,1,0:T(8,128)(2,1)S(1)}, bf16[2,512,1024]{2,1,0:T(8,128)(2,1)}, u32[]{:S(2)}) copy-start(bf16[2,512,1024]{2,1,0:T(8,128)(2,1)} %refs_7_.5) | copy-start | bytes 6291460
  56.9 33.3 %copy-start.5 = (f32[512]{0:T(512)S(1)}, f32[512]{0:T(512)}, u32[]{:S(2)}) copy-start(f32[512]{0:T(512)} %param.31) | copy-start | bytes 6148
  60.7 6.9 %collective-permute-start.4 = (bf16[192,512]{1,0:T(8,128)(2,1)S(1)}, bf16[192,512]{1,0:T(8,128)(2,1)S(1)}, u32[]{:S(2)}, u32[]{:S(2)}) collective-permute-start(bf16[192,512]{1,0:T(8,128)(2,1)S(1)} %bitcast.14), channel_id=1, source_target_pairs={{0,64},{8,72},{16,80},{24,88},{32,96},{40,104},{48,112},{56,120},{... | collective-permute-start | bytes 589832 | tf_op jit(solution)/shard_map/ppermute | solution.py:460
  67.6 54.9 %all-to-all-start.3 = ((bf16[32,128,128]{2,1,0:T(8,128)(2,1)}), bf16[32,128,128]{2,1,0:T(8,128)(2,1)}, u32[]{:S(2)}, u32[]{:S(2)}) async-start(bf16[32,128,128]{2,1,0:T(8,128)(2,1)} %bitcast.8), calls=%async_computation.3 | async-start | bytes 2097152 | tf_op jit(solution)/shard_map/all_to_all | solution.py:753
  74.1 16.1 %collective-permute-start.6 = (bf16[192,512]{1,0:T(8,128)(2,1)S(1)}, bf16[192,512]{1,0:T(8,128)(2,1)S(1)}, u32[]{:S(2)}, u32[]{:S(2)}) collective-permute-start(bf16[192,512]{1,0:T(8,128)(2,1)S(1)} %bitcast.15), channel_id=1, source_target_pairs={{0,192},{8,200},{16,208},{24,216},{32,224},{40,232},{48,240},{56,2... | collective-permute-start | bytes 589832 | tf_op jit(solution)/shard_map/ppermute | solution.py:460
  76.9 13.3 %collective-permute-start.5 = (bf16[192,512]{1,0:T(8,128)(2,1)S(1)}, bf16[192,512]{1,0:T(8,128)(2,1)S(1)}, u32[]{:S(2)}, u32[]{:S(2)}) collective-permute-start(bf16[192,512]{1,0:T(8,128)(2,1)S(1)} %bitcast.16), channel_id=1, source_target_pairs={{0,128},{8,136},{16,144},{24,152},{32,160},{40,168},{48,176},{56,1... | collective-permute-start | bytes 589832 | tf_op jit(solution)/shard_map/ppermute | solution.py:460
  90.2 1.6 copy-start.2
  94.2 2.4 %collective-permute-start.7 = (bf16[4,48,2176]{2,1,0:T(8,128)(2,1)S(1)}, bf16[4,48,2176]{2,1,0:T(8,128)(2,1)S(1)}, u32[]{:S(2)}, u32[]{:S(2)}) collective-permute-start(bf16[4,48,2176]{2,1,0:T(8,128)(2,1)S(1)} %get-tuple-element.114), channel_id=1, source_target_pairs={{0,1},{1,0},{2,3},{3,2},{4,5},{5,4},{6,7},{7,6},{8,9},{9,8},{10,11... | collective-permute-start | bytes 2506760 | tf_op jit(solution)/shard_map/ppermute | solution.py:502
  97.0 9.1 %collective-permute-start.8 = (bf16[48,2176]{1,0:T(8,128)(2,1)S(1)}, bf16[48,2176]{1,0:T(8,128)(2,1)S(1)}, u32[]{:S(2)}, u32[]{:S(2)}) collective-permute-start(bf16[48,2176]{1,0:T(8,128)(2,1)S(1)} %get-tuple-element.116), channel_id=1, source_target_pairs={{0,2},{1,3},{2,4},{3,5},{4,6},{5,7},{6,0},{7,1},{8,10},{9,11},{10,... | collective-permute-start | bytes 626696 | tf_op jit(solution)/shard_map/ppermute | solution.py:465
  97.2 12.9 %collective-permute-start.9 = (bf16[48,2176]{1,0:T(8,128)(2,1)S(1)}, bf16[48,2176]{1,0:T(8,128)(2,1)S(1)}, u32[]{:S(2)}, u32[]{:S(2)}) collective-permute-start(bf16[48,2176]{1,0:T(8,128)(2,1)S(1)} %get-tuple-element.117), channel_id=1, source_target_pairs={{0,4},{1,5},{2,6},{3,7},{4,0},{5,1},{6,2},{7,3},{8,12},{9,13},{10,... | collective-permute-start | bytes 626696 | tf_op jit(solution)/shard_map/ppermute | solution.py:465
  100.4 10.1 %collective-permute-start.10 = (bf16[48,2176]{1,0:T(8,128)(2,1)S(1)}, bf16[48,2176]{1,0:T(8,128)(2,1)S(1)}, u32[]{:S(2)}, u32[]{:S(2)}) collective-permute-start(bf16[48,2176]{1,0:T(8,128)(2,1)S(1)} %get-tuple-element.118), channel_id=1, source_target_pairs={{0,6},{1,7},{2,0},{3,1},{4,2},{5,3},{6,4},{7,5},{8,14},{9,15},{10,... | collective-permute-start | bytes 626696 | tf_op jit(solution)/shard_map/ppermute | solution.py:465
  110.8 11.8 %copy-start.3 = (bf16[48,1024]{1,0:T(8,128)(2,1)}, bf16[48,1024]{1,0:T(8,128)(2,1)S(1)}, u32[]{:S(2)}) copy-start(bf16[48,1024]{1,0:T(8,128)(2,1)S(1)} %hidden_units.1.refs_3_) | copy-start | bytes 294916
  110.8 7.1 %collective-permute-start.13 = (bf16[48,1024]{1,0:T(8,128)(2,1)S(1)}, bf16[48,1024]{1,0:T(8,128)(2,1)S(1)}, u32[]{:S(2)}, u32[]{:S(2)}) collective-permute-start(bf16[48,1024]{1,0:T(8,128)(2,1)S(1)} %hidden_units.1.refs_3_), channel_id=1, source_target_pairs={{0,6},{1,7},{2,0},{3,1},{4,2},{5,3},{6,4},{7,5},{8,14},{9,15},{10,... | collective-permute-start | bytes 294920 | tf_op jit(solution)/shard_map/ppermute | solution.py:465
  113.5 7.1 %collective-permute-start.12 = (bf16[48,1024]{1,0:T(8,128)(2,1)S(1)}, bf16[48,1024]{1,0:T(8,128)(2,1)S(1)}, u32[]{:S(2)}, u32[]{:S(2)}) collective-permute-start(bf16[48,1024]{1,0:T(8,128)(2,1)S(1)} %hidden_units.1.refs_3_), channel_id=1, source_target_pairs={{0,4},{1,5},{2,6},{3,7},{4,0},{5,1},{6,2},{7,3},{8,12},{9,13},{10,... | collective-permute-start | bytes 294920 | tf_op jit(solution)/shard_map/ppermute | solution.py:465
  113.8 7.5 %collective-permute-start.11 = (bf16[48,1024]{1,0:T(8,128)(2,1)S(1)}, bf16[48,1024]{1,0:T(8,128)(2,1)S(1)}, u32[]{:S(2)}, u32[]{:S(2)}) collective-permute-start(bf16[48,1024]{1,0:T(8,128)(2,1)S(1)} %hidden_units.1.refs_3_), channel_id=1, source_target_pairs={{0,2},{1,3},{2,4},{3,5},{4,6},{5,7},{6,0},{7,1},{8,10},{9,11},{10,... | collective-permute-start | bytes 294920 | tf_op jit(solution)/shard_map/ppermute | solution.py:465
  114.4 6.8 %collective-permute-start.14 = (bf16[48,1024]{1,0:T(8,128)(2,1)S(1)}, bf16[48,1024]{1,0:T(8,128)(2,1)S(1)}, u32[]{:S(2)}, u32[]{:S(2)}) collective-permute-start(bf16[48,1024]{1,0:T(8,128)(2,1)S(1)} %hidden_units.1.refs_3_), channel_id=1, source_target_pairs={{0,1},{1,0},{2,3},{3,2},{4,5},{5,4},{6,7},{7,6},{8,9},{9,8},{10,11... | collective-permute-start | bytes 294920 | tf_op jit(solution)/shard_map/ppermute | solution.py:801
  117.8 4.7 %copy-start.9 = (bf16[48,1024]{1,0:T(8,128)(2,1)}, bf16[48,1024]{1,0:T(8,128)(2,1)S(1)}, u32[]{:S(2)}) copy-start(bf16[48,1024]{1,0:T(8,128)(2,1)S(1)} %collective-permute-done.13.refs_6_) | copy-start | bytes 294916
  117.9 3.4 %collective-permute-start.17 = (bf16[48,1024]{1,0:T(8,128)(2,1)S(1)}, bf16[48,1024]{1,0:T(8,128)(2,1)S(1)}, u32[]{:S(2)}, u32[]{:S(2)}) collective-permute-start(bf16[48,1024]{1,0:T(8,128)(2,1)S(1)} %collective-permute-done.13.refs_6_), channel_id=1, source_target_pairs={{0,1},{1,0},{2,3},{3,2},{4,5},{5,4},{6,7},{7,6},{8,9},{9,8},{10,11... | collective-permute-start | bytes 294920 | tf_op jit(solution)/shard_map/ppermute | solution.py:801
  120.5 2.0 %copy-start.10 = (bf16[48,1024]{1,0:T(8,128)(2,1)}, bf16[48,1024]{1,0:T(8,128)(2,1)S(1)}, u32[]{:S(2)}) copy-start(bf16[48,1024]{1,0:T(8,128)(2,1)S(1)} %collective-permute-done.12.refs_5_) | copy-start | bytes 294916
  120.5 1.3 collective-permute-start.16
  121.3 1.3 copy-start.11
  121.3 1.3 collective-permute-start.15
  121.3 1.3 copy-start.12
  121.3 1.3 copy-start.13
  121.8 0.8 copy-start.14
  122.6 0.6 copy-start.15
